TPU v7x, 32 devices: a whole 2x2x4 slice. The times are simulated.
32 devices in a mesh: wide: 8 (over z, y), narrow: 4 (over x, core).
Axes of the slice: x: 2, y: 2, z: 4, core: 2. Of those that a mesh axis runs over, the one named last changes fastest.
Arguments:
- tokens: bfloat16 [34816, 768], P(('wide', 'narrow')), may hold values from -6 to 6
- cotangent: bfloat16 [34816, 768], P(('wide', 'narrow')), may hold values from -6 to 6
- latents: bfloat16 [34816, 16], P(('wide', 'narrow')), may hold values from -6 to 6
- added_noise: float32 [4, 16, 8192], P(None, None, ('wide', 'narrow')), may hold values from -6 to 6
- timesteps: int32 [4, 8192], P(None, ('wide', 'narrow')), may hold values from 0 to 999
- bucket: int32 [32], replicated, may hold values from 256 to 1024, as said below
- masked: int32 [32, 1088], P(('wide', 'narrow')), may hold values from 0 to 1, as said below
- deal_start: int32 [32], replicated, may hold values from 0 to 7
- first_gain: float32 [768], replicated, may hold values from 0.5 to 1.5
- first_shift: float32 [768], replicated, may hold values from -0.3125 to 0.3125
- joint_weight: bfloat16 [768, 2304], replicated, may hold values from -0.21875 to 0.21875
- query_value_bias: float32 [1536], replicated, may hold values from -0.3125 to 0.3125
- output_weight: bfloat16 [768, 768], replicated, may hold values from -1.5 to 1.5
- output_bias: float32 [768], replicated, may hold values from -0.3125 to 0.3125
- second_gain: float32 [768], replicated, may hold values from 0.5 to 1.5
- second_shift: float32 [768], replicated, may hold values from -0.3125 to 0.3125
- expand_weight: bfloat16 [768, 3072], replicated, may hold values from -0.21875 to 0.21875
- expand_bias: float32 [3072], replicated, may hold values from -1.25 to 1.25
- reduce_weight: bfloat16 [3072, 768], replicated, may hold values from -0.109375 to 0.109375
- reduce_bias: float32 [768], replicated, may hold values from -0.3125 to 0.3125
- input_proj: bfloat16 [1024, 16], replicated, may hold values from -1.5 to 1.5
- cond_proj: bfloat16 [768, 1024], replicated, may hold values from -0.21875 to 0.21875
- time_first: bfloat16 [256, 1024], replicated, may hold values from -0.375 to 0.375
- time_second: bfloat16 [1024, 1024], replicated, may hold values from -0.1875 to 0.1875
- block_mod: bfloat16 [1024, 3072], replicated, may hold values from -0.1875 to 0.1875
- block_expand: bfloat16 [1024, 1024], replicated, may hold values from -0.1875 to 0.1875
- block_reduce: bfloat16 [1024, 1024], replicated, may hold values from -0.1875 to 0.1875
- final_mod: bfloat16 [1024, 2048], replicated, may hold values from -0.1875 to 0.1875
- final_proj: bfloat16 [1024, 16], replicated, may hold values from -0.375 to 0.375
Outputs:
- block_output: bfloat16 [34816, 768], P(('wide', 'narrow'))
- noise_guess: float32 [4, 16, 8192], P(None, None, ('wide', 'narrow'))
- branch_spread: float32 [32, 2], P(('wide', 'narrow'))
- tokens_gradient: float32 [34816, 768], P(('wide', 'narrow'))
- first_gain_gradient: float32 [768], P('wide')
- first_shift_gradient: float32 [768], P('wide')
- joint_weight_gradient: float32 [768, 2304], P('wide')
- query_value_bias_gradient: float32 [1536], P('wide')
- output_weight_gradient: float32 [768, 768], P('wide')
- output_bias_gradient: float32 [768], P('wide')
- second_gain_gradient: float32 [768], P('wide')
- second_shift_gradient: float32 [768], P('wide')
- expand_weight_gradient: float32 [768, 3072], P('wide')
- expand_bias_gradient: float32 [3072], P('wide')
- reduce_weight_gradient: float32 [3072, 768], P('wide')
- reduce_bias_gradient: float32 [768], P('wide')
- input_proj_gradient: float32 [1024, 16], P('wide')
- cond_proj_gradient: float32 [768, 1024], P('wide')
- time_first_gradient: float32 [256, 1024], P('wide')
- time_second_gradient: float32 [1024, 1024], P('wide')
- block_mod_gradient: float32 [1024, 3072], P('wide')
- block_expand_gradient: float32 [1024, 1024], P('wide')
- block_reduce_gradient: float32 [1024, 1024], P('wide')
- final_mod_gradient: float32 [1024, 2048], P('wide')
- final_proj_gradient: float32 [1024, 16], P('wide')
Inputs may be any that keep to these rules, and one draw needn't show every extreme that they name: `bucket`: each entry is 256 or 1024; among the images whose index has one remainder modulo 4, at least one has 1024. `masked`: row i has exactly bucket[i] * 256 // 1024 ones, all at positions 64 to 64 + bucket[i] - 1.
All inputs are finite; a program needn't handle non-finite values.
Results may differ from a plain program's by a relative error of at most 0.017.
Values may be sent and summed in bfloat16 or wider, within the bound.
No kernel may reach another device: no remote copies, remote signals or barrier semaphores. Data moves between devices by JAX's collectives and lax.ppermute only.
A program may use at most 320 MiB of HBM per device.

v0:
```python
from functools import partial
import math

import jax
import jax.numpy as jnp
from jax import lax
from jax.experimental import pallas as pl
from jax.experimental.pallas import tpu as pltpu
from jax.sharding import PartitionSpec as P

D = 768
HEADS = 12
HEAD_DIM = 64
TOKEN_DIM = 16
BUFFER = 64
IMAGE_MAX = 1024
MASK_MAX = 256
REPEATS = 4
SEQ = 1088


SHIFT_ANGLE = 0.008 / 1.008 * math.pi / 2.0
STEP_ANGLE = math.pi / (2.0 * 1.008 * 1000.0)
PAIRS = 6
VMEM = 60 * 1024 * 1024

OWN = pl.CostEstimate(flops=1 << 40, bytes_accessed=1 << 20, transcendentals=0)
OTHER = pl.CostEstimate(flops=0, bytes_accessed=1 << 20, transcendentals=0)


def nt(a,b): return lax.dot_general(a,b,(((1,),(1,)),((),())),preferred_element_type=jnp.float32)
def nn(a,b): return jnp.dot(a,b,preferred_element_type=jnp.float32)
def tn(a,b): return lax.dot_general(a,b,(((0,),(0,)),((),())),preferred_element_type=jnp.float32)
def normalize(values):
    centre = values - jnp.mean(values, axis=-1, keepdims=True)
    inverse = lax.rsqrt(jnp.mean(centre * centre, axis=-1, keepdims=True) + 1e-06)
    return (centre * inverse, inverse)


def normalize_back(grad_normed, normed, inverse):
    return inverse * (
        grad_normed
        - jnp.mean(grad_normed, axis=-1, keepdims=True)
        - normed * jnp.mean(grad_normed * normed, axis=-1, keepdims=True)
    )


def sigmoid(value):
    return 0.5 * jnp.tanh(0.5 * value) + 0.5


def silu_slope(value, sigma):
    return sigma * (1.0 + value * (1.0 - sigma))


def whole_block(shape):
    zeros = (0,) * len(shape)
    return pl.BlockSpec(shape, lambda *unused: zeros, pipeline_mode=pl.Buffered(1))


def time_kernel(sinus_ref, first_ref, second_ref, low_ref, slope_ref, timed_ref):
    first = nn(sinus_ref[...], first_ref[...])
    sigma = sigmoid(first)
    low = (first * sigma).astype(jnp.bfloat16)
    slope_ref[...] = silu_slope(first, sigma).astype(jnp.bfloat16)
    low_ref[...] = low.T
    timed_ref[...] = nn(low, second_ref[...])


def time_embedding(sinus, time_first, time_second):
    count, freq = sinus.shape
    width = time_first.shape[1]
    rows = count // REPEATS
    by_rows = pl.BlockSpec((rows, width), lambda i: (i, 0))
    return pl.pallas_call(
        time_kernel,
        grid=(REPEATS,),
        in_specs=[
            pl.BlockSpec((rows, freq), lambda i: (i, 0)),
            whole_block(time_first.shape),
            whole_block(time_second.shape),
        ],
        out_specs=[pl.BlockSpec((width, rows), lambda i: (0, i)), by_rows, by_rows],
        out_shape=[
            jax.ShapeDtypeStruct((width, count), jnp.bfloat16),
            jax.ShapeDtypeStruct((count, width), jnp.bfloat16),
            jax.ShapeDtypeStruct((count, width), jnp.float32),
        ],
        compiler_params=pltpu.CompilerParams(vmem_limit_bytes=VMEM),
        cost_estimate=OTHER,
        name="time_embedding",
    )(sinus, time_first, time_second)


def head_kernel(
    dealt_ref,
    timed_ref,
    keep_ref,
    drop_ref,
    noise_ref,
    live_ref,
    input_ref,
    cond_ref,
    mod_ref,
    expand_ref,
    reduce_ref,
    fin_ref,
    final_ref,
    guess_ref,
    left_ref,
    fin_grad_ref,
    branch_grad_ref,
    upper_grad_ref,
    mod_grad_ref,
    timed_grad_ref,
    embed_grad_ref,
    rows_grad_ref,
    input_grad_ref,
    final_grad_ref,
    embed_scratch,
    total_scratch,
):
    turn = pl.program_id(0)
    width = timed_ref.shape[1]

    @pl.when(turn == 0)
    def _():
        embed_scratch[...] = nn(dealt_ref[:, :D], cond_ref[...])
        total_scratch[...] = jnp.zeros_like(total_scratch)
        input_grad_ref[...] = jnp.zeros_like(input_grad_ref)
        final_grad_ref[...] = jnp.zeros_like(final_grad_ref)

    cond = embed_scratch[...] + timed_ref[...]
    acted = (cond * sigmoid(cond)).astype(jnp.bfloat16)
    left_ref[0] = acted.T
    start = dealt_ref[:, D:].astype(jnp.float32).T[:TOKEN_DIM]
    noise = noise_ref[0]
    noisy = (keep_ref[0] * start + drop_ref[0] * noise).astype(jnp.bfloat16)
    entry = tn(noisy, input_ref[...])
    inner_normed, inner_inverse = normalize(entry)
    shift_a = nn(acted, mod_ref[:, :width])
    scale_a = nn(acted, mod_ref[:, width : 2 * width])
    gate_a = nn(acted, mod_ref[:, 2 * width :])
    inner = (inner_normed * (1.0 + scale_a) + shift_a).astype(jnp.bfloat16)
    left_ref[2] = inner.T
    upper = nn(inner, expand_ref[...])
    upper_sigma = sigmoid(upper)
    lifted = (upper * upper_sigma).astype(jnp.bfloat16)
    left_ref[1] = lifted.T
    branch = nn(lifted, reduce_ref[...])
    shift_b = nn(acted, fin_ref[:, :width])
    scale_b = nn(acted, fin_ref[:, width:])
    last_normed, last_inverse = normalize(entry + gate_a * branch)
    last = (last_normed * (1.0 + scale_b) + shift_b).astype(jnp.bfloat16)
    live = live_ref[...]
    guess = nt(final_ref[...], last) * live
    guess_ref[0] = guess
    guess_grad = (2.0 / REPEATS * (guess - noise * live) * live).astype(jnp.bfloat16)
    final_grad_ref[...] += nn(guess_grad, last)
    last_grad = tn(guess_grad, final_ref[...])
    fin_grad = jnp.concatenate([last_grad, last_grad * last_normed], axis=1).astype(jnp.bfloat16)
    fin_grad_ref[...] = fin_grad
    after_grad = normalize_back(last_grad * (1.0 + scale_b), last_normed, last_inverse)
    branch_grad = (after_grad * gate_a).astype(jnp.bfloat16)
    branch_grad_ref[...] = branch_grad
    lifted_grad = nt(branch_grad, reduce_ref[...])
    upper_grad = (lifted_grad * silu_slope(upper, upper_sigma)).astype(jnp.bfloat16)
    upper_grad_ref[...] = upper_grad
    inner_grad = nt(upper_grad, expand_ref[...])
    entry_grad = (
        after_grad + normalize_back(inner_grad * (1.0 + scale_a), inner_normed, inner_inverse)
    ).astype(jnp.bfloat16)
    input_grad_ref[...] += nn(noisy, entry_grad)
    mod_grad = jnp.concatenate(
        [inner_grad, inner_grad * inner_normed, after_grad * branch], axis=1
    ).astype(jnp.bfloat16)
    mod_grad_ref[...] = mod_grad
    acted_grad = nt(mod_grad, mod_ref[...]) + nt(fin_grad, fin_ref[...])
    cond = embed_scratch[...] + timed_ref[...]
    cond_grad = acted_grad * silu_slope(cond, sigmoid(cond))
    timed_grad_ref[...] = cond_grad.astype(jnp.bfloat16)
    total_scratch[...] += cond_grad

    @pl.when(turn == REPEATS - 1)
    def _():
        embed_grad = total_scratch[...].astype(jnp.bfloat16)
        embed_grad_ref[...] = embed_grad
        rows_grad_ref[...] = nt(embed_grad, cond_ref[...]).astype(jnp.bfloat16)


def head_pass(dealt, timed, keep_sig, drop_sig, noise, live, weights):
    input_proj, cond_proj, block_mod, block_expand, block_reduce, final_mod, final_proj = weights
    slots = dealt.shape[0]
    width = cond_proj.shape[1]
    count = REPEATS * slots
    by_rows = lambda n: pl.BlockSpec((slots, n), lambda i: (i, 0))
    by_turn = lambda a: pl.BlockSpec((1,) + a, lambda i: (i, 0, 0))
    low = lambda *s: jax.ShapeDtypeStruct(s, jnp.bfloat16)
    full = lambda *s: jax.ShapeDtypeStruct(s, jnp.float32)
    operands = (
        dealt,
        timed,
        keep_sig,
        drop_sig,
        noise,
        live,
        input_proj,
        cond_proj,
        block_mod,
        block_expand,
        block_reduce,
        final_mod,
        final_proj,
    )
    return pl.pallas_call(
        head_kernel,
        grid=(REPEATS,),
        in_specs=[
            whole_block(dealt.shape),
            by_rows(width),
            by_turn((1, slots)),
            by_turn((1, slots)),
            by_turn((TOKEN_DIM, slots)),
        ]
        + [whole_block(a.shape) for a in operands[5:]],
        out_specs=[
            by_turn((TOKEN_DIM, slots)),
            pl.BlockSpec((3, width, slots), lambda i: (0, 0, i)),
            by_rows(2 * width),
            by_rows(width),
            by_rows(width),
            by_rows(3 * width),
            by_rows(width),
            whole_block((slots, width)),
            whole_block((slots, D)),
            whole_block((TOKEN_DIM, width)),
            whole_block((TOKEN_DIM, width)),
        ],
        out_shape=[
            full(REPEATS, TOKEN_DIM, slots),
            low(3, width, count),
            low(count, 2 * width),
            low(count, width),
            low(count, width),
            low(count, 3 * width),
            low(count, width),
            low(slots, width),
            low(slots, D),
            full(TOKEN_DIM, width),
            full(TOKEN_DIM, width),
        ],
        scratch_shapes=[pltpu.VMEM((slots, width), jnp.float32)] * 2,
        compiler_params=pltpu.CompilerParams(vmem_limit_bytes=VMEM),
        cost_estimate=OTHER,
        name="head_pass",
    )(*operands)


MARK = jax.ShapeDtypeStruct((8, 128), jnp.float32)


def head_grads_one_kernel(half_ref, left_ref, fin_ref, branch_ref, upper_ref, *refs):
    turn = pl.program_id(0)
    tile = head_one_tile(turn, half_ref)

    def put(grad):
        if len(refs) == 2:
            out_ref, mark_ref = refs
            out_ref[0] = grad.astype(jnp.bfloat16)
        else:
            got_ref, sent_ref, kept_ref, mark_ref = refs
            grad = (grad + got_ref[0].astype(jnp.float32)).astype(jnp.bfloat16)

            @pl.when(turn < 2)
            def _():
                sent_ref[0] = grad

            @pl.when(turn >= 2)
            def _():
                kept_ref[0] = grad

        mark_ref[...] = jnp.zeros_like(mark_ref)

    @pl.when(tile < 4)
    def _():
        put(nn(left_ref[0], fin_ref[...]))

    @pl.when((tile >= 4) & (tile < 6))
    def _():
        put(nn(left_ref[0], branch_ref[...]))

    @pl.when(tile >= 6)
    def _():
        put(nn(left_ref[0], upper_ref[...]))


def head_one_tile(turn, half):
    return half[0] * 4 + (turn ^ (2 - 2 * half[1]))


def head_grads_one(half, left, fin_grad, branch_grad, upper_grad, got=None):
    width, count = left.shape[1:]
    cols = width // 2

    def at(first, tiles):
        return lambda i, half: (0, jnp.clip(head_one_tile(i, half) - first, 0, tiles - 1))

    def which(i, half):
        tile = head_one_tile(i, half)
        return (jnp.where(tile < 4, 0, jnp.where(tile < 6, 1, 2)), 0, 0)

    tiles = lambda n: jax.ShapeDtypeStruct((n, width, cols), jnp.bfloat16)
    block = lambda where: pl.BlockSpec((1, width, cols), where)
    if got is None:
        more = ()
        outs = [(block(lambda i, half: (i ^ (2 - 2 * half[1]), 0, 0)), tiles(4))]
    else:
        more = (got,)
        outs = [
            (block(lambda i, half: (jnp.minimum(i, 1), 0, 0)), tiles(2)),
            (block(lambda i, half: (jnp.maximum(i - 2, 0), 0, 0)), tiles(2)),
        ]
    outs.append((whole_block((8, 128)), MARK))
    return pl.pallas_call(
        head_grads_one_kernel,
        grid_spec=pltpu.PrefetchScalarGridSpec(
            num_scalar_prefetch=1,
            grid=(4,),
            in_specs=[
                pl.BlockSpec((1, width, count), which),
                pl.BlockSpec((count, cols), at(0, 4)),
                pl.BlockSpec((count, cols), at(4, 2)),
                pl.BlockSpec((count, cols), at(6, 2)),
            ]
            + [block(lambda i, half: (i ^ (2 - 2 * half[1]), 0, 0))] * len(more),
            out_specs=[o[0] for o in outs],
        ),
        out_shape=[o[1] for o in outs],
        compiler_params=pltpu.CompilerParams(vmem_limit_bytes=VMEM),
        cost_estimate=OTHER if got is None else OWN,
        name="head_grads_one",
    )(half, left, fin_grad, branch_grad, upper_grad, *more)


def time_back_kernel(grad_ref, weight_ref, slope_ref, out_ref):
    grad = nt(grad_ref[...], weight_ref[...])
    out_ref[...] = (grad * slope_ref[...].astype(jnp.float32)).astype(jnp.bfloat16)


def time_back(timed_grad, weight, slope):
    count, width = timed_grad.shape
    by_rows = pl.BlockSpec((count // 4, width), lambda i: (i, 0))
    return pl.pallas_call(
        time_back_kernel,
        grid=(4,),
        in_specs=[by_rows, whole_block(weight.shape), by_rows],
        out_specs=by_rows,
        out_shape=jax.ShapeDtypeStruct((count, width), jnp.bfloat16),
        compiler_params=pltpu.CompilerParams(vmem_limit_bytes=VMEM),
        cost_estimate=OTHER,
        name="time_back",
    )(timed_grad, weight, slope)


def split_rows(grad, wide, y):
    grad = grad.reshape((wide // 2, 2, -1) + grad.shape[1:])
    own, other = jnp.where(y == 0, grad[:, 0], grad[:, 1]), jnp.where(y == 0, grad[:, 1], grad[:, 0])
    flat = lambda a: a.reshape((-1,) + a.shape[2:]).astype(jnp.bfloat16)
    return flat(other), flat(own)


def head_grads_two_kernel(
    wide, half_ref, acted_ref, low_ref, mod_ref, timed_ref, rows_ref, embed_ref, sinus_ref, first_ref, *refs
):
    turn = pl.program_id(0)
    tile = half_ref[0] * 10 + head_two_tile(turn, half_ref)

    def put(grad):
        refs[-1][...] = jnp.zeros_like(refs[-1])
        if len(refs) == 2:
            refs[0][0] = grad.astype(jnp.bfloat16)
            return
        got_ref, sent_one, kept_one, sent_two, kept_two, unused = refs
        grad = grad + got_ref[0].astype(jnp.float32)

        @pl.when(turn < 2)
        def _():
            sent_one[0] = grad.astype(jnp.bfloat16)

        @pl.when((turn >= 5) & (turn < 7))
        def _():
            kept_one[0] = grad.astype(jnp.bfloat16)

        @pl.when(turn % 5 >= 2)
        def _():
            sent_two[0], kept_two[0] = split_rows(grad, wide, half_ref[2])

    @pl.when(tile < 12)
    def _():
        put(nn(acted_ref[0], mod_ref[...]))

    @pl.when((tile >= 12) & (tile < 16))
    def _():
        put(nn(low_ref[...], timed_ref[...]))

    @pl.when(tile >= 16)
    def _():
        cond = tn(rows_ref[:, :D], embed_ref[...])
        time = tn(sinus_ref[...], first_ref[...])
        cols = cond.shape[1]
        both = jnp.concatenate(
            [cond.reshape(wide, -1, cols), time.reshape(wide, -1, cols)], axis=1
        )
        put(both.reshape(-1, cols))


def head_two_tile(turn, half):
    return (turn // 5 ^ (1 - half[1])) * 5 + turn % 5


def head_grads_two(half, left, low, mod_grad, timed_grad, dealt, embed_grad, sinus, first_grad, wide, got=None):
    width, count = left.shape[1:]
    slots = dealt.shape[0]
    cols = width // 4

    def at(first, tiles):
        return lambda i, half: (0, jnp.clip(half[0] * 10 + head_two_tile(i, half) - first, 0, tiles - 1))

    whole = pl.BlockSpec((1, width, cols), lambda i, half: (head_two_tile(i, half), 0, 0))
    like = lambda n, rows: jax.ShapeDtypeStruct((n, rows, cols), jnp.bfloat16)
    if got is None:
        more = ()
        outs = [(whole, like(10, width))]
    else:
        more = (got,)
        block = lambda rows, where: pl.BlockSpec((1, rows, cols), where)

        def second(i, half):
            return ((i // 5 ^ (1 - half[1])) * 3 + jnp.maximum(i % 5 - 2, 0), 0, 0)

        outs = [
            (block(width, lambda i, half: (jnp.minimum(i, 1), 0, 0)), like(2, width)),
            (block(width, lambda i, half: (jnp.clip(i - 5, 0, 1), 0, 0)), like(2, width)),
            (block(width // 2, second), like(6, width // 2)),
            (block(width // 2, second), like(6, width // 2)),
        ]
    outs.append((whole_block((8, 128)), MARK))
    return pl.pallas_call(
        partial(head_grads_two_kernel, wide),
        grid_spec=pltpu.PrefetchScalarGridSpec(
            num_scalar_prefetch=1,
            grid=(10,),
            in_specs=[
                whole_block((1, width, count)),
                whole_block((width, count)),
                pl.BlockSpec((count, cols), at(0, 12)),
                pl.BlockSpec((count, cols), at(12, 4)),
                whole_block(dealt.shape),
                pl.BlockSpec((slots, cols), at(16, 4)),
                whole_block(sinus.shape),
                pl.BlockSpec((count, cols), at(16, 4)),
            ]
            + [whole] * len(more),
            out_specs=[o[0] for o in outs],
        ),
        out_shape=[o[1] for o in outs],
        compiler_params=pltpu.CompilerParams(vmem_limit_bytes=VMEM),
        cost_estimate=OTHER if got is None else OWN,
        name="head_grads_two",
    )(half, left, low, mod_grad, timed_grad, dealt, embed_grad, sinus, first_grad, *more)


def attend_kernel(QB, at_ref, bucket_ref, q_ref, k_ref, v_ref, o_ref, lse_ref):
    length=BUFFER + bucket_ref[at_ref[0]]
    low=lax.broadcasted_iota(jnp.int32,(1,128),1)<64
    bias=jnp.where(lax.broadcasted_iota(jnp.int32,(1,SEQ),1)<length,0.0,-1e30).astype(jnp.float32)
    k=k_ref[...]; v=v_ref[...]
    one=jnp.ones((),v.dtype); zero=jnp.zeros((),v.dtype)
    vs=(jnp.where(low,v,one),jnp.where(low,one,v))
    for b in range(SEQ//QB):
        rows=pl.ds(b*QB,QB)
        q=q_ref[rows,:]
        outs=[];lses=[]
        for h in range(2):
            qh=jnp.where(low,q,zero) if h==0 else jnp.where(low,zero,q)
            s=nt(qh,k)+bias
            top=jnp.max(s,axis=1,keepdims=True)
            p=jnp.exp(s-top).astype(jnp.bfloat16)
            o=nn(p,vs[h])
            total=pltpu.roll(o,64,1)
            outs.append(o/total)
            lses.append(top+jnp.log(total))
        o_ref[rows,:]=jnp.where(low,outs[0],outs[1]).astype(jnp.bfloat16)
        lse_ref[rows,:]=jnp.where(low,lses[0],lses[1])

def attend(at,bucket,joint,QB=272):
    spec=lambda off: pl.BlockSpec((SEQ,128),lambda i,off=off:(0,i+off))
    return pl.pallas_call(partial(attend_kernel,QB),
        grid=(PAIRS,),
        in_specs=[smem(),smem(),spec(0),spec(6),spec(12)],
        out_specs=[spec(0),spec(0)],
        out_shape=[jax.ShapeDtypeStruct((SEQ,D),jnp.bfloat16),jax.ShapeDtypeStruct((SEQ,D),jnp.float32)],
        compiler_params=pltpu.CompilerParams(vmem_limit_bytes=VMEM),
        cost_estimate=OTHER,
        name='attend')(at,bucket,joint,joint,joint)

def attend_back_kernel(KB, at_ref, bucket_ref,q_ref,k_ref,v_ref,do_ref,o_ref,lse_ref,grads_ref,ds_ref):
    length=BUFFER + bucket_ref[at_ref[0]]
    low=lax.broadcasted_iota(jnp.int32,(1,128),1)<64
    q=q_ref[...]; do=do_ref[...]
    zero=jnp.zeros((),q.dtype)
    prod=do.astype(jnp.float32)*o_ref[...].astype(jnp.float32)
    prodT=prod.T
    lseT=lse_ref[...].T
    deltas=(jnp.sum(prodT[:64],axis=0,keepdims=True),jnp.sum(prodT[64:],axis=0,keepdims=True))
    lses=(lseT[0:1],lseT[64:65])
    for b in range(SEQ//KB):
        rows=pl.ds(b*KB,KB)
        k=k_ref[rows,:]; v=v_ref[rows,:]
        bias=jnp.where(lax.broadcasted_iota(jnp.int32,(KB,1),0)+b*KB<length,0.0,-1e30).astype(jnp.float32)
        dks=[];dvs=[]
        for h in range(2):
            pick=(lambda a: jnp.where(low,a,zero)) if h==0 else (lambda a: jnp.where(low,zero,a))
            s=nt(pick(k),q)+bias
            p=jnp.exp(s-lses[h])
            dp=nt(pick(v),do)
            ds=(p*(dp-deltas[h])).astype(jnp.bfloat16)
            dvs.append(nn(p.astype(jnp.bfloat16),do))
            dks.append(nn(ds,q))
            ds_ref[h,rows,:]=ds
        grads_ref[1,rows,:]=jnp.where(low,dks[0],dks[1]).astype(jnp.bfloat16)
        grads_ref[2,rows,:]=jnp.where(low,dvs[0],dvs[1]).astype(jnp.bfloat16)
    kT=k_ref[...].astype(jnp.float32).T.astype(jnp.bfloat16)
    dqT=jnp.concatenate([nn(kT[64*h:64*h+64],ds_ref[h]) for h in range(2)],axis=0)
    grads_ref[0]=(dqT.T*0.125).astype(jnp.bfloat16)

def attend_back(first,count,at,bucket,joint,do,o,lse,KB=544):
    spec=lambda off: pl.BlockSpec((SEQ,128),lambda i,off=off:(0,i+off))
    return pl.pallas_call(partial(attend_back_kernel,KB),
        grid=(count,),
        in_specs=[smem(),smem(),spec(first),spec(6+first),spec(12+first),spec(first),spec(first),spec(first)],
        out_specs=pl.BlockSpec((3,SEQ,128),lambda i:(0,0,i)),
        out_shape=jax.ShapeDtypeStruct((3,SEQ,count*128),jnp.bfloat16),
        scratch_shapes=[pltpu.VMEM((2,SEQ,SEQ),jnp.bfloat16)],
        compiler_params=pltpu.CompilerParams(vmem_limit_bytes=VMEM),
        cost_estimate=OWN,
        name="attend_back")(at,bucket,joint,joint,joint,do,o,lse)


def line(ref):
    return ref[...].reshape(1, ref.shape[0])


def smem():
    return pl.BlockSpec(memory_space=pltpu.SMEM)


def place_kernel(wide, at_ref, bucket_ref, start_ref, chosen_ref, spot_ref, live_ref):
    image, place_wide, place_narrow, narrow = at_ref[0], at_ref[1], at_ref[2], at_ref[3]
    seq = chosen_ref.shape[1]
    slots = live_ref.shape[1]
    shift = wide.bit_length() - 1
    deep = slots // wide
    deep_shift = deep.bit_length() - 1
    row = lax.broadcasted_iota(jnp.int32, (seq, seq), 0)
    column = lax.broadcasted_iota(jnp.int32, (seq, seq), 1)
    lower = (column <= row).astype(jnp.float32).astype(jnp.bfloat16)
    chosen = jnp.broadcast_to(chosen_ref[...], (8, seq)).astype(jnp.float32).astype(jnp.bfloat16)
    counted = nt(lower, chosen)
    first_row = lax.broadcasted_iota(jnp.int32, counted.shape, 0) == 0
    before = jnp.where(first_row, 0.0, pltpu.roll(counted, 1, 0))
    is_chosen = (counted - before)[:, :1] > 0.5
    order = counted[:, :1].astype(jnp.int32) - 1
    target = ((start_ref[image] + order) & (wide - 1)) * deep + (order >> shift)
    target = jnp.where(is_chosen, target, -1)
    slot = lax.broadcasted_iota(jnp.int32, (seq, slots), 1)
    spot_ref[...] = (slot == target).astype(jnp.float32).astype(jnp.bfloat16)
    lane = lax.broadcasted_iota(jnp.int32, (1, slots), 1)
    live = jnp.zeros((1, slots), jnp.float32)
    for source in range(wide):
        other = source * narrow + place_narrow
        count = bucket_ref[other] * MASK_MAX // IMAGE_MAX
        rank = (place_wide - start_ref[other]) & (wide - 1)
        arrived = jnp.maximum((count - rank + wide - 1) >> shift, 0)
        inside = ((lane >> deep_shift) == source) & ((lane & (deep - 1)) < arrived)
        live = jnp.where(inside, 1.0, live)
    live_ref[...] = live


def places(at, bucket, deal_start, masked, wide):
    seq = masked.shape[1]
    return pl.pallas_call(
        partial(place_kernel, wide),
        in_specs=[smem(), smem(), smem(), whole_block((1, seq))],
        out_specs=[whole_block((seq, MASK_MAX)), whole_block((1, MASK_MAX))],
        grid=(1,),
        out_shape=[
            jax.ShapeDtypeStruct((seq, MASK_MAX), jnp.bfloat16),
            jax.ShapeDtypeStruct((1, MASK_MAX), jnp.float32),
        ],
        compiler_params=pltpu.CompilerParams(vmem_limit_bytes=VMEM),
        cost_estimate=OTHER,
        name="places",
    )(at, bucket, deal_start, masked)


def joint_kernel(tokens_ref, gain_ref, shift_ref, weight_ref, bias_ref, first_ref, joint_ref):
    normed, unused = normalize(tokens_ref[...].astype(jnp.float32))
    first = (normed * line(gain_ref) + line(shift_ref)).astype(jnp.bfloat16)
    first_ref[...] = first
    for part in range(3):
        cols = slice(part * D, (part + 1) * D)
        out = nn(first, weight_ref[:, cols])
        if part != 1:
            out = out + line(bias_ref)[:, part // 2 * D : part // 2 * D + D]
        out = out.astype(jnp.bfloat16)
        if part == 0:
            out = out * jnp.bfloat16(HEAD_DIM ** (-0.5))
        joint_ref[:, cols] = out


ROWS = 272


def by_block(columns):
    return pl.BlockSpec((ROWS, columns), lambda i: (i, 0))


def joint_pass(tokens, gain, shift, weight, bias):
    seq = tokens.shape[0]
    return pl.pallas_call(
        joint_kernel,
        grid=(seq // ROWS,),
        in_specs=[by_block(D)] + [whole_block(a.shape) for a in (gain, shift, weight, bias)],
        out_specs=[by_block(D), by_block(3 * D)],
        out_shape=[
            jax.ShapeDtypeStruct((seq, D), jnp.bfloat16),
            jax.ShapeDtypeStruct((seq, 3 * D), jnp.bfloat16),
        ],
        compiler_params=pltpu.CompilerParams(vmem_limit_bytes=VMEM),
        cost_estimate=OTHER,
        name="joint_pass",
    )(tokens, gain, shift, weight, bias)


def gelu_parts(value):
    size = jnp.abs(value)
    bell = jnp.exp(-0.5 * value * value)
    step = 1.0 / (1.0 + (0.3275911 * math.sqrt(0.5)) * size)
    tail = 0.5 * 1.061405429 * step - 0.5 * 1.453152027
    tail = tail * step + 0.5 * 1.421413741
    tail = tail * step - 0.5 * 0.284496736
    tail = tail * step + 0.5 * 0.254829592
    tail = tail * step * bell
    return jnp.where(value < 0.0, tail, 1.0 - tail), bell * (1.0 / math.sqrt(2.0 * math.pi))


def keep_column(at_ref, bucket_ref, rows):
    position = lax.broadcasted_iota(jnp.int32, (rows, 1), 0) + pl.program_id(0) * rows
    return (position < BUFFER + bucket_ref[at_ref[0]]).astype(jnp.float32)


def feed_kernel(
    at_ref,
    bucket_ref,
    mixed_ref,
    tokens_ref,
    latent_ref,
    spot_ref,
    out_w_ref,
    out_b_ref,
    gain_ref,
    shift_ref,
    expand_ref,
    expand_b_ref,
    reduce_ref,
    reduce_b_ref,
    output_ref,
    middle_ref,
    second_ref,
    active_ref,
    slope_ref,
    dealt_ref,
    spread_ref,
    dealt_scratch,
    spread_scratch,
):
    step = pl.program_id(0)

    @pl.when(step == 0)
    def _():
        dealt_scratch[...] = jnp.zeros_like(dealt_scratch)
        spread_scratch[...] = jnp.zeros_like(spread_scratch)

    keep = keep_column(at_ref, bucket_ref, mixed_ref.shape[0])
    branch = nn(mixed_ref[...], out_w_ref[...]) + line(out_b_ref)
    middle = tokens_ref[...].astype(jnp.float32) + branch
    middle_ref[...] = middle
    normed, unused = normalize(middle)
    second = (normed * line(gain_ref) + line(shift_ref)).astype(jnp.bfloat16)
    second_ref[...] = second
    hidden_width = expand_ref.shape[1]
    expand_b = line(expand_b_ref)
    feed = line(reduce_b_ref)
    for part in range(hidden_width // D):
        cols = slice(part * D, (part + 1) * D)
        hidden = nn(second, expand_ref[:, cols]) + expand_b[:, cols]
        phi, density = gelu_parts(hidden)
        active = (hidden * phi).astype(jnp.bfloat16)
        active_ref[:, cols] = active
        slope_ref[:, cols] = (phi + hidden * density).astype(jnp.bfloat16)
        feed = feed + nn(active, reduce_ref[cols, :])
    output = ((middle + feed) * keep).astype(jnp.bfloat16)
    output_ref[...] = output
    spread_scratch[0:1, :] += jnp.sum(keep * branch * branch, axis=0, keepdims=True)
    spread_scratch[1:2, :] += jnp.sum(keep * feed * feed, axis=0, keepdims=True)
    spot = spot_ref[...]
    dealt_scratch[:, :D] += tn(spot, output)
    dealt_scratch[:, D : D + TOKEN_DIM] += tn(spot, latent_ref[...])

    @pl.when(step == pl.num_programs(0) - 1)
    def _():
        dealt_ref[...] = dealt_scratch[...].astype(jnp.bfloat16)
        count = (BUFFER + bucket_ref[at_ref[0]]).astype(jnp.float32) * D
        total = jnp.sum(spread_scratch[...], axis=1, keepdims=True)
        spread_ref[...] = jnp.sqrt(jnp.broadcast_to(total, spread_ref.shape) / count)


def feed_pass(at, bucket, mixed, tokens, latents, spot, weights):
    seq = tokens.shape[0]
    slots = spot.shape[1]
    hidden = weights[4].shape[1]
    low = lambda *s: jax.ShapeDtypeStruct(s, jnp.bfloat16)
    full = lambda *s: jax.ShapeDtypeStruct(s, jnp.float32)
    return pl.pallas_call(
        feed_kernel,
        grid=(seq // ROWS,),
        in_specs=[smem(), smem(), by_block(D), by_block(D), by_block(TOKEN_DIM), by_block(slots)]
        + [whole_block(a.shape) for a in weights],
        out_specs=[
            by_block(D),
            by_block(D),
            by_block(D),
            by_block(hidden),
            by_block(hidden),
            whole_block((slots, D + 128)),
            whole_block((8, 128)),
        ],
        out_shape=[
            low(seq, D),
            full(seq, D),
            low(seq, D),
            low(seq, hidden),
            low(seq, hidden),
            low(slots, D + 128),
            full(8, 128),
        ],
        scratch_shapes=[pltpu.VMEM((slots, D + 128), jnp.float32), pltpu.VMEM((8, D), jnp.float32)],
        compiler_params=pltpu.CompilerParams(vmem_limit_bytes=VMEM),
        cost_estimate=OTHER,
        name="feed_pass",
    )(at, bucket, mixed, tokens, latents, spot, *weights)


def feed_back_kernel(
    at_ref,
    bucket_ref,
    cot_ref,
    spot_ref,
    middle_ref,
    slope_ref,
    returned_ref,
    out_w_ref,
    gain_ref,
    expand_ref,
    reduce_ref,
    feed_grad_ref,
    hidden_grad_ref,
    middle_grad_ref,
    branch_grad_ref,
    mixed_grad_ref,
    sums_ref,
    wide_sum_ref,
):
    @pl.when(pl.program_id(0) == 0)
    def _():
        sums_ref[...] = jnp.zeros_like(sums_ref)
        wide_sum_ref[...] = jnp.zeros_like(wide_sum_ref)

    def add_sum(row, value):
        sums_ref[row : row + 1, :] += jnp.sum(value, axis=0, keepdims=True)

    keep = keep_column(at_ref, bucket_ref, cot_ref.shape[0])
    grad = (cot_ref[...].astype(jnp.float32) + nn(spot_ref[...], returned_ref[...])) * keep
    feed_grad = grad.astype(jnp.bfloat16)
    feed_grad_ref[...] = feed_grad
    add_sum(0, feed_grad.astype(jnp.float32))
    second_grad = jnp.zeros(grad.shape, jnp.float32)
    for part in range(expand_ref.shape[1] // D):
        cols = slice(part * D, (part + 1) * D)
        active_grad = nt(feed_grad, reduce_ref[cols, :])
        hidden_grad = (active_grad * slope_ref[:, cols].astype(jnp.float32)).astype(jnp.bfloat16)
        hidden_grad_ref[:, cols] = hidden_grad
        wide_sum_ref[:, cols] += jnp.sum(hidden_grad.astype(jnp.float32), axis=0, keepdims=True)
        second_grad = second_grad + nt(hidden_grad, expand_ref[:, cols])
    normed, inverse = normalize(middle_ref[...])
    add_sum(1, second_grad * normed)
    add_sum(2, second_grad)
    middle_grad = grad + normalize_back(second_grad * line(gain_ref), normed, inverse)
    middle_grad_ref[...] = middle_grad
    branch_grad = middle_grad.astype(jnp.bfloat16)
    branch_grad_ref[...] = branch_grad
    add_sum(3, branch_grad.astype(jnp.float32))
    mixed_grad_ref[...] = nt(branch_grad, out_w_ref[...]).astype(jnp.bfloat16)


def feed_back(at, bucket, cotangent, spot, middle, slope, returned, weights):
    seq = cotangent.shape[0]
    slots = spot.shape[1]
    hidden = slope.shape[1]
    low = lambda *s: jax.ShapeDtypeStruct(s, jnp.bfloat16)
    full = lambda *s: jax.ShapeDtypeStruct(s, jnp.float32)
    return pl.pallas_call(
        feed_back_kernel,
        grid=(seq // ROWS,),
        in_specs=[smem(), smem(), by_block(D), by_block(slots), by_block(D), by_block(hidden)]
        + [whole_block(a.shape) for a in (returned,) + weights],
        out_specs=[
            by_block(D),
            by_block(hidden),
            by_block(D),
            by_block(D),
            by_block(D),
            whole_block((8, D)),
            whole_block((1, hidden)),
        ],
        out_shape=[
            low(seq, D),
            low(seq, hidden),
            full(seq, D),
            low(seq, D),
            low(seq, D),
            full(8, D),
            full(1, hidden),
        ],
        compiler_params=pltpu.CompilerParams(vmem_limit_bytes=VMEM),
        cost_estimate=OTHER,
        name="feed_back",
    )(at, bucket, cotangent, spot, middle, slope, returned, *weights)


def feed_grads_kernel(wide, half_ref, second_ref, hidden_ref, active_ref, grad_ref, *refs):
    step = pl.program_id(0)
    refs[-1][...] = jnp.zeros_like(refs[-1])

    @pl.when(step < 2)
    def _():
        grad = tn(second_ref[...], hidden_ref[...])
        if len(refs) == 3:
            refs[0][0] = grad.astype(jnp.bfloat16)
        else:
            grad = (grad + refs[0][0].astype(jnp.float32)).astype(jnp.bfloat16)

            @pl.when(step == 0)
            def _():
                refs[2][...] = grad[None]

            @pl.when(step == 1)
            def _():
                refs[3][...] = grad[None]

    @pl.when(step >= 2)
    def _():
        whole = tn(active_ref[...], grad_ref[...])
        pieces = 4
        rows = D // wide
        places = whole.shape[0] // (pieces * rows)
        whole = whole.reshape(places, pieces, rows, D // 2)
        for piece in range(pieces):
            at = (piece // 2, slice(None), slice(piece % 2 * (D // 2), (piece % 2 + 1) * (D // 2)))
            part = whole[:, piece].reshape(places * rows, D // 2)
            if len(refs) == 3:
                refs[1][at] = part.astype(jnp.bfloat16)
            else:
                part = part + refs[1][at].astype(jnp.float32)
                refs[4][at], refs[5][at] = split_rows(part, places, half_ref[2])


def feed_grads(half, second, hidden_grad, active, feed_grad, wide, got=None):
    seq, hidden = active.shape
    chunk = lambda i: jnp.maximum(i - 2, 0)
    turned = lambda i, half: jnp.minimum(i, 1) ^ (1 - half[1])
    low = lambda *s: jax.ShapeDtypeStruct(s, jnp.bfloat16)
    expand_tile = pl.BlockSpec((1, D, D), lambda i, half: (turned(i, half), 0, 0))
    rows_of = lambda rows: pl.BlockSpec((2, rows, D), lambda i, half: (0, chunk(i), 0))
    if got is None:
        more = ()
        outs = [(expand_tile, low(2, D, D)), (rows_of(D // 4), low(2, D, D))]
    else:
        more = tuple(got)
        outs = [(whole_block((1, D, D)), low(1, D, D))] * 2
        outs += [(rows_of(D // 8), low(2, D // 2, D))] * 2
    outs.append((whole_block((8, 128)), MARK))
    return pl.pallas_call(
        partial(feed_grads_kernel, wide),
        grid_spec=pltpu.PrefetchScalarGridSpec(
            num_scalar_prefetch=1,
            grid=(6,),
            in_specs=[
                whole_block((seq, D)),
                pl.BlockSpec((seq, D), lambda i, half: (0, half[0] * 2 + turned(i, half))),
                pl.BlockSpec((seq, D), lambda i, half: (0, chunk(i))),
                pl.BlockSpec((seq, D // 2), lambda i, half: (0, half[0])),
            ]
            + [expand_tile, rows_of(D // 4)][: len(more)],
            out_specs=[o[0] for o in outs],
        ),
        out_shape=[o[1] for o in outs],
        compiler_params=pltpu.CompilerParams(vmem_limit_bytes=VMEM),
        cost_estimate=OTHER if got is None else OWN,
        name="feed_grads",
    )(half, second, hidden_grad, active, feed_grad, *more)


def last_grads_kernel(half_ref, first_ref, mixed_ref, a_ref, b_ref, c_ref, branch_ref, out_ref, mark_ref):
    kind = half_ref[0] * 2 + pl.program_id(0)
    mark_ref[...] = jnp.zeros_like(mark_ref)

    def put(whole):
        for i in range(6):
            out_ref[i] = whole[:, i * 128 : (i + 1) * 128].astype(jnp.bfloat16)

    @pl.when(kind < 3)
    def _():
        put(tn(first_ref[...], jnp.concatenate([a_ref[0], b_ref[0], c_ref[0]], axis=1)))

    @pl.when(kind == 3)
    def _():
        put(tn(mixed_ref[...], branch_ref[...]))


def last_grads(half, first_in, mixed, parts, branch_grad):
    seq = mixed.shape[0]
    part = lambda a: pl.BlockSpec(
        (1,) + a.shape[1:], lambda i, half: (jnp.minimum(half[0] * 2 + i, 2), 0, 0)
    )
    return pl.pallas_call(
        last_grads_kernel,
        grid_spec=pltpu.PrefetchScalarGridSpec(
            num_scalar_prefetch=1,
            grid=(2,),
            in_specs=[whole_block((seq, D)), whole_block((seq, D))]
            + [part(a) for a in parts]
            + [whole_block((seq, D))],
            out_specs=[pl.BlockSpec((6, D, 128), lambda i, half: (i, 0, 0)), whole_block((8, 128))],
        ),
        out_shape=[jax.ShapeDtypeStruct((12, D, 128), jnp.bfloat16), MARK],
        compiler_params=pltpu.CompilerParams(vmem_limit_bytes=VMEM),
        cost_estimate=OTHER,
        name="last_grads",
    )(half, first_in, mixed, *parts, branch_grad)


def tokens_back_kernel(
    tokens_ref, a_ref, b_ref, c_ref, middle_ref, gain_ref, weight_ref, out_ref, packed_ref, sums_ref
):
    @pl.when(pl.program_id(0) == 0)
    def _():
        sums_ref[...] = jnp.zeros_like(sums_ref)

    def add_sum(row, value):
        sums_ref[row : row + 1, :] += jnp.sum(value, axis=0, keepdims=True)

    query, keys, value = [
        jnp.concatenate([a_ref[i], b_ref[i], c_ref[i]], axis=1) for i in range(3)
    ]
    grad = nt(query, weight_ref[:, :D])
    grad = grad + nt(keys, weight_ref[:, D : 2 * D])
    grad = grad + nt(value, weight_ref[:, 2 * D :])
    normed, inverse = normalize(tokens_ref[...].astype(jnp.float32))
    add_sum(0, grad * normed)
    add_sum(1, grad)
    add_sum(2, query.astype(jnp.float32))
    add_sum(3, value.astype(jnp.float32))
    out_ref[...] = middle_ref[...] + normalize_back(grad * line(gain_ref), normed, inverse)

    @pl.when(pl.program_id(0) == pl.num_programs(0) - 1)
    def _():
        wide = packed_ref.shape[0]
        part = D // wide
        for w in range(wide):
            packed_ref[w : w + 1, :part] = sums_ref[0:1, w * part : (w + 1) * part]
            packed_ref[w : w + 1, part : 2 * part] = sums_ref[1:2, w * part : (w + 1) * part]
            bias_row = 2 + w * 2 // wide
            at = w % (wide // 2) * 2 * part
            packed_ref[w : w + 1, 2 * part :] = sums_ref[bias_row : bias_row + 1, at : at + 2 * part]


def tokens_back(tokens, parts, middle_grad, gain, weight, wide):
    seq = tokens.shape[0]
    return pl.pallas_call(
        tokens_back_kernel,
        grid=(seq // ROWS,),
        in_specs=[by_block(D)]
        + [pl.BlockSpec((3, ROWS, a.shape[2]), lambda i: (0, i, 0)) for a in parts]
        + [by_block(D)] + [whole_block(gain.shape), whole_block(weight.shape)],
        out_specs=[by_block(D), whole_block((wide, 4 * D // wide))],
        out_shape=[
            jax.ShapeDtypeStruct((seq, D), jnp.float32),
            jax.ShapeDtypeStruct((wide, 4 * D // wide), jnp.float32),
        ],
        scratch_shapes=[pltpu.VMEM((8, D), jnp.float32)],
        compiler_params=pltpu.CompilerParams(vmem_limit_bytes=VMEM),
        cost_estimate=OTHER,
        name="tokens_back",
    )(tokens, *parts, middle_grad, gain, weight)


def pack_kernel(feed_ref, hidden_ref, input_ref, final_ref, token_ref, *refs):
    out_ref = refs[-1]
    out_ref[...] = jnp.zeros_like(out_ref)
    wide, rows, cols = out_ref.shape
    part = D // wide
    block = input_ref.shape[1] // wide
    for w in range(wide):
        out_ref[w, :TOKEN_DIM, :block] = input_ref[:, w * block : (w + 1) * block]
        out_ref[w, :TOKEN_DIM, block : 2 * block] = final_ref[:, w * block : (w + 1) * block]
        out_ref[w, TOKEN_DIM : TOKEN_DIM + 1, :] = hidden_ref[:, w * cols : (w + 1) * cols]
        out_ref[w, TOKEN_DIM + 2 : TOKEN_DIM + 3, :] = token_ref[w : w + 1, :]
        for i in range(4):
            out_ref[w, TOKEN_DIM + 1 : TOKEN_DIM + 2, i * part : (i + 1) * part] = feed_ref[
                i : i + 1, w * part : (w + 1) * part
            ]


def pack(feed_sums, hidden_sum, input_grad, final_grad, token_packed, marks):
    operands = (feed_sums, hidden_sum, input_grad, final_grad, token_packed)
    wide = token_packed.shape[0]
    shape = (wide, TOKEN_DIM + 8, hidden_sum.shape[1] // wide)
    return pl.pallas_call(
        pack_kernel,
        grid=(1,),
        in_specs=[whole_block(a.shape) for a in operands] + [pl.BlockSpec(memory_space=pl.ANY)] * len(marks),
        out_specs=whole_block(shape),
        out_shape=jax.ShapeDtypeStruct(shape, jnp.float32),
        cost_estimate=OTHER,
        name="pack",
    )(*operands, *marks)


def add_up(terms):
    total = terms[0].astype(jnp.float32)
    for term in terms[1:]:
        total = total + term.astype(jnp.float32)
    return total


def swap(array, axis, mask):
    count = lax.axis_size(axis)
    return lax.ppermute(array, axis, [(i, i ^ mask) for i in range(count)])


def bit(axis, mask):
    return lax.axis_index(axis) // mask % 2


def pick(array, index, axis):
    return lax.dynamic_index_in_dim(array, index, axis, keepdims=False)


class Order:
    def __init__(self):
        self.mark = ()
        self.marks = ()

    def __call__(self, *values):
        out = lax.optimization_barrier(values + self.mark)[: len(values)]
        return out if len(values) > 1 else out[0]

    def at(self, *values):
        self.mark = values


def bits():
    return jnp.stack([bit("narrow", 1), bit("narrow", 2), bit("wide", 1)]).astype(jnp.int32)


class Flow:
    AXES = {"x": ("narrow", 2), "y": ("wide", 1)}

    def __init__(self, order, lanes, sends=None):
        self.order = order
        self.wide = lax.axis_size("wide").bit_length() - 1
        self.lanes = [[list(terms), tuple(left)] for terms, left in lanes]
        self.steps = self.run(sends)

    def step(self):
        next(self.steps)

    def take(self):
        got = self.order(*self.got)
        return got if isinstance(got, (tuple, list)) else (got,)

    def send(self, *sends):
        self.got = tuple(swap(*s) for s in sends)
        self.order.at(*[s[0] for s in sends])

    def shaped(self, array, left):
        dims = (2,) * (self.wide - ("y" not in left))
        if "x" in left:
            return array.reshape((2, array.shape[0] // 2) + dims + (-1, array.shape[2]))
        return array.reshape((array.shape[0],) + dims + (-1, array.shape[2]))

    def exchange(self, lane, goal):
        terms, left = lane
        dim = 0 if goal == "x" else self.wide + ("x" in left)
        mine = bit(*self.AXES[goal])
        sent = add_up([pick(t, 1 - mine, dim) for t in terms]).astype(jnp.bfloat16)
        lane[0] = [pick(t, mine, dim) for t in terms]
        lane[1] = tuple(n for n in left if n != goal)
        return (sent,) + self.AXES[goal]

    def run(self, sends):
        if sends is not None:
            shapes = [lane[0][0].shape for lane in self.lanes]
            self.send(*sends)
            yield
            got = self.take()
            for lane, g, shape in zip(self.lanes, got, shapes):
                lane[0].append(g.reshape(shape))
        while any(lane[1] for lane in self.lanes):
            self.send(*[self.exchange(lane, lane[1][0]) for lane in self.lanes])
            yield
            for lane, got in zip(self.lanes, self.take()):
                lane[0].append(got)
        parts = [lane[0] for lane in self.lanes]
        both = []
        for b in reversed(range(1, self.wide)):
            mask = 1 << b
            mine = bit("wide", mask)
            sent = [add_up([pick(t, 1 - mine, 1) for t in terms]) for terms in parts]
            sent = [jnp.concatenate(sent, axis=0)] + [pick(t, 1 - mine, 1) for t in both]
            parts = [[pick(t, mine, 1) for t in terms] for terms in parts]
            both = [pick(t, mine, 1) for t in both]
            self.send((add_up(sent).astype(jnp.bfloat16), "wide", mask))
            yield
            both.append(self.take()[0])
        own = jnp.concatenate([add_up(terms) for terms in parts], axis=0)
        share = add_up([own] + both).astype(jnp.bfloat16)
        self.send((share, "narrow", 2))
        yield
        (other,) = self.take()
        self.send((share, "narrow", 1), (other, "narrow", 1))
        yield
        self.result = (share, other) + tuple(self.take())
        yield

    def finish(self):
        for unused in self.steps:
            pass
        return self.result


class Halves:
    def __init__(self, order, sent):
        *sent, mark = sent
        self.order = order
        self.flight = tuple(swap(a, "narrow", 1) for a in sent)
        order.at(mark)
        order.marks += (mark,)

    def got(self):
        got = self.order(*self.flight)
        return tuple(got) if isinstance(got, (tuple, list)) else (got,)


def unpack_kernel(put, bits_ref, *refs):
    shares, outs = refs[:4], refs[4:]
    core, x = bits_ref[0], bits_ref[1]
    for c in range(2):
        for k in range(2):
            same_x, same_core = x == k, core == c
            for t in range(shares[0].shape[0]):
                one, two, three, four = [s[t].astype(jnp.float32) for s in shares]
                near = jnp.where(same_x, one, two)
                far = jnp.where(same_x, three, four)
                put(outs, c, k, t, jnp.where(same_core, near, far))


def unpack(put, shares, shapes):
    return pl.pallas_call(
        partial(unpack_kernel, put),
        grid=(1,),
        in_specs=[smem()] + [whole_block(a.shape) for a in shares],
        out_specs=[whole_block(s) for s in shapes],
        out_shape=[jax.ShapeDtypeStruct(s, jnp.float32) for s in shapes],
        compiler_params=pltpu.CompilerParams(vmem_limit_bytes=VMEM),
        cost_estimate=OTHER,
        name="unpack",
    )(bits(), *shares)


def put_columns(spans, tiles):
    def put(outs, c, x, t, value):
        column = (c * 2 + x) * tiles + t
        for out_ref, (first, stop) in zip(outs, spans):
            if first <= column < stop:
                at = (column - first) * value.shape[1]
                out_ref[:, at : at + value.shape[1]] = value

    return put


def small_steps(order, rows):
    def send(*sends):
        order.at(*[s[0] for s in sends])
        return [swap(*s) for s in sends]

    wide = lax.axis_size("wide")
    low = rows.astype(jnp.bfloat16)
    for mask in (1, 2):
        (got,) = send((low, "narrow", mask))
        yield
        low = add_up([low, order(got)]).astype(jnp.bfloat16)
    low = low.reshape((wide // 2, 2) + low.shape[1:])
    mine = bit("wide", 1)
    (got,) = send((pick(low, 1 - mine, 1), "wide", 1))
    yield
    low = add_up([pick(low, mine, 1), order(got)]).astype(jnp.bfloat16)
    place = lax.axis_index("wide") // 2
    got = send(*[(pick(low, place ^ (m // 2), 0), "wide", m) for m in range(2, wide, 2)])
    yield
    yield add_up([pick(low, place, 0)] + list(order(*got)))


def shards(
    tokens,
    cotangent,
    latents,
    added_noise,
    timesteps,
    bucket,
    masked,
    deal_start,
    first_gain,
    first_shift,
    joint_weight,
    query_value_bias,
    output_weight,
    output_bias,
    second_gain,
    second_shift,
    expand_weight,
    expand_bias,
    reduce_weight,
    reduce_bias,
    input_proj,
    cond_proj,
    time_first,
    time_second,
    block_mod,
    block_expand,
    block_reduce,
    final_mod,
    final_proj,
):
    wide = lax.axis_size("wide")
    narrow = lax.axis_size("narrow")
    place_wide = lax.axis_index("wide")
    place_narrow = lax.axis_index("narrow")
    mine = bits()
    other = mine.at[0].set(1 - mine[0])
    image_index = place_wide * narrow + place_narrow
    at = jnp.stack([image_index, place_wide, place_narrow, jnp.int32(narrow)]).astype(jnp.int32)

    spot, live = places(at, bucket, deal_start, masked, wide)
    slots = spot.shape[1]
    steps = timesteps.astype(jnp.float32)
    half = time_first.shape[0] // 2
    freqs = jnp.exp(-math.log(10000.0) * jnp.arange(half).astype(jnp.float32) / half)
    angles = steps.reshape(-1, 1) * freqs
    sinus = jnp.concatenate([jnp.cos(angles), jnp.sin(angles)], axis=-1).astype(jnp.bfloat16)
    offset = steps * STEP_ANGLE
    keep_sig = jnp.cos(offset + SHIFT_ANGLE) / math.cos(SHIFT_ANGLE)
    drop_sig = jnp.sqrt(jnp.sin(offset) * jnp.sin(offset + 2.0 * SHIFT_ANGLE)) / math.cos(SHIFT_ANGLE)
    input_turned = input_proj.T
    final_turned = final_proj.T

    first_in, joint = joint_pass(
        tokens, first_gain, first_shift, joint_weight, query_value_bias
    )
    mixed, logsum = attend(at, bucket, joint)
    block_output, middle, second_in, active, slope, dealt, spread = feed_pass(
        at,
        bucket,
        mixed,
        tokens,
        latents,
        spot,
        (
            output_weight,
            output_bias,
            second_gain,
            second_shift,
            expand_weight,
            expand_bias,
            reduce_weight,
            reduce_bias,
        ),
    )

    def deal(array):
        shape = array.shape
        return lax.all_to_all(
            array.reshape(wide, -1, shape[1]), "wide", split_axis=0, concat_axis=0, tiled=True
        ).reshape(shape)

    dealt = deal(dealt)
    low_turned, time_slope, timed = time_embedding(sinus, time_first, time_second)
    (
        guess,
        left,
        fin_grad,
        branch_grad,
        upper_grad,
        mod_grad,
        timed_grad,
        embed_grad,
        rows_grad,
        input_grad,
        final_grad,
    ) = head_pass(
        dealt,
        timed,
        keep_sig[:, None, :],
        drop_sig[:, None, :],
        added_noise,
        live,
        (input_turned, cond_proj, block_mod, block_expand, block_reduce, final_mod, final_turned),
    )
    order = Order()
    order.at(rows_grad)
    returned = deal(rows_grad)
    first_grad = time_back(order(timed_grad), time_second, time_slope)
    order.at(first_grad)
    one_args = (fin_grad, branch_grad, upper_grad)
    halves_one = Halves(order, head_grads_one(other, order(left), *one_args))
    two_args = (mod_grad, timed_grad, dealt, embed_grad, sinus, first_grad, wide)
    halves_two = Halves(order, head_grads_two(other, left, order(low_turned), *two_args))
    returned = order(returned)
    order.at(returned, *order.mark)

    def note(mark):
        order.marks += (mark,)
        order.at(mark)

    sent, kept, mark = head_grads_one(mine, order(left), *one_args, *halves_one.got())
    note(mark)
    shape = lambda a: a.reshape((a.shape[0],) + (2,) * (wide.bit_length() - 1) + (-1, a.shape[2]))
    half_shape = lambda a: a.reshape(
        (2, a.shape[0] // 2) + (2,) * (wide.bit_length() - 2) + (-1, a.shape[2])
    )
    one = Flow(order, [([shape(kept)], ("y",))], [(sent, "narrow", 2)])
    one.step()
    order.at(mark)
    sent_a, kept_a, sent_b, kept_b, mark = head_grads_two(
        mine, left, order(low_turned), *two_args, *halves_two.got()
    )
    note(mark)
    two = Flow(
        order,
        [([shape(kept_a)], ("y",)), ([half_shape(kept_b)], ("x",))],
        [(sent_a, "narrow", 2), (sent_b, "wide", 1)],
    )
    two.step()
    order.at(mark)
    feed_grad, hidden_grad, middle_grad, out_grad, mixed_grad, feed_sums, hidden_sum = feed_back(
        at,
        bucket,
        order(cotangent),
        spot,
        middle,
        slope,
        returned,
        (output_weight, second_gain, expand_weight, reduce_weight),
    )
    order.at(mixed_grad)
    feed_args = (hidden_grad, active, feed_grad, wide)
    halves_feed = Halves(order, feed_grads(other, order(second_in), *feed_args))
    one.step()
    parts = []

    def attend_back_part(i):
        grads = attend_back(2 * i, 2, at, bucket, joint, order(mixed_grad), mixed, logsum)
        order.at(grads)
        parts.append(grads)

    attend_back_part(0)
    two.step()
    sent_e, kept_e, sent_r, kept_r, mark = feed_grads(
        mine, order(second_in), *feed_args, halves_feed.got()
    )
    note(mark)
    feed = Flow(
        order,
        [([shape(kept_e)], ("y",)), ([half_shape(kept_r)], ("x",))],
        [(sent_e, "narrow", 2), (sent_r, "wide", 1)],
    )
    feed.step()
    order.at(mark)
    one.step()
    attend_back_part(1)
    feed.step()
    two.step()
    one.step()
    attend_back_part(2)
    feed.step()
    two.step()
    one.step()
    last_args = (mixed, parts, out_grad)
    halves_last = Halves(order, last_grads(other, order(first_in), *last_args))
    one.step()
    own, mark = last_grads(mine, order(first_in), *last_args)
    note(mark)
    terms = [
        a.reshape((2, 6) + (2,) * (wide.bit_length() - 1) + (-1, 128)) for a in (own,) + halves_last.got()
    ]
    last = Flow(
        order, [([a[:, :3] for a in terms], ("x", "y")), ([a[:, 3:] for a in terms], ("y", "x"))]
    )
    last.step()
    two.step()
    tokens_gradient, token_packed = tokens_back(
        order(tokens), parts, middle_grad, first_gain, joint_weight, wide
    )
    order.at(token_packed)
    width = cond_proj.shape[1]
    rows = width // wide
    cut = cond_proj.shape[0] // wide

    def hold(outs):
        order.at(*outs)
        return outs

    last.step()
    feed.step()
    two.step()
    packed = pack(feed_sums, hidden_sum, input_grad, final_grad, order(token_packed), order.marks)
    order.at(packed)
    small = small_steps(order, packed)
    next(small)
    one = one.finish()
    final_mod_out, block_reduce_out, block_expand_out = hold(
        unpack(
            put_columns(((0, 4), (4, 6), (6, 8)), 2),
            (order(one[0]),) + one[1:],
            ((rows, 2 * width), (rows, width), (rows, width)),
        )
    )
    last.step()
    next(small)
    feed.step()
    two = two.finish()

    def put_two(outs, c, x, t, value):
        column = (c * 2 + x) * 5 + t
        if column < 16:
            put_columns(((0, 12), (12, 16)), 5)(outs, c, x, t, value)
        else:
            cols = slice((column - 16) * 256, (column - 15) * 256)
            outs[2][:, cols] = value[:cut]
            outs[3][:, cols] = value[cut:]

    block_mod_out, time_second_out, cond_out, time_first_out = hold(
        unpack(
            put_two,
            (order(two[0]),) + two[1:],
            ((rows, 3 * width), (rows, width), (cut, width), (rows - cut, width)),
        )
    )
    last.step()
    next(small)
    feed.step()
    feed = feed.finish()

    def put_feed(outs, c, x, t, value):
        if t == 0:
            at = (c * 2 + x) * D
            outs[0][:, at : at + D] = value
        else:
            for i in range(2):
                piece = x * 2 + i
                outs[1][piece * cut : (piece + 1) * cut, c * (D // 2) : (c + 1) * (D // 2)] = value[
                    :, i * (D // 2) : (i + 1) * (D // 2)
                ]

    last.step()
    next(small)
    expand_out, reduce_out = hold(
        unpack(put_feed, (order(feed[0]),) + feed[1:], ((cut, 4 * D), (4 * cut, D)))
    )
    last.step()
    small = next(small)
    last = last.finish()
    joint_out, output_out = unpack(
        put_columns(((0, 18), (18, 24)), 6), last, ((cut, 3 * D), (cut, D))
    )
    part = D // wide
    block = input_grad.shape[1] // wide
    vectors = [small[TOKEN_DIM + 1, i * part : (i + 1) * part] for i in range(4)]
    input_out = small[:TOKEN_DIM, :block].T
    final_out = small[:TOKEN_DIM, block : 2 * block].T
    late = small[TOKEN_DIM + 2]
    outs = [
        late[:part],
        late[part : 2 * part],
        late[2 * part :],
        vectors[3],
        vectors[1],
        vectors[2],
        small[TOKEN_DIM],
        vectors[0],
        input_out,
        final_out,
    ]
    return (
        block_output,
        guess,
        spread[:2, 0].reshape(1, 2),
        tokens_gradient,
        outs[0],
        outs[1],
        joint_out,
        outs[2],
        output_out,
        outs[3],
        outs[4],
        outs[5],
        expand_out,
        outs[6],
        reduce_out,
        outs[7],
        outs[8],
        cond_out,
        time_first_out,
        time_second_out,
        block_mod_out,
        block_expand_out,
        block_reduce_out,
        final_mod_out,
        outs[9],
    )


def solution(mesh):
    in_specs = (
        P(("wide", "narrow"), None),
        P(("wide", "narrow"), None),
        P(("wide", "narrow"), None),
        P(None, None, ("wide", "narrow")),
        P(None, ("wide", "narrow")),
        P(),
        P(("wide", "narrow"), None),
        P(),
        P(),
        P(),
        P(),
        P(),
        P(),
        P(),
        P(),
        P(),
        P(),
        P(),
        P(),
        P(),
        P(),
        P(),
        P(),
        P(),
        P(),
        P(),
        P(),
        P(),
        P(),
    )
    out_specs = (
        P(("wide", "narrow"), None),
        P(None, None, ("wide", "narrow")),
        P(("wide", "narrow"), None),
        P(("wide", "narrow"), None),
        P("wide"),
        P("wide"),
        P("wide", None),
        P("wide"),
        P("wide", None),
        P("wide"),
        P("wide"),
        P("wide"),
        P("wide", None),
        P("wide"),
        P("wide", None),
        P("wide"),
        P("wide", None),
        P("wide", None),
        P("wide", None),
        P("wide", None),
        P("wide", None),
        P("wide", None),
        P("wide", None),
        P("wide", None),
        P("wide", None),
    )
    return jax.shard_map(shards, mesh=mesh, in_specs=in_specs, out_specs=out_specs, check_vma=False)
```

profile of v0, /device:TPU:0, one launch (start us, length us, event | category | flops | bytes accessed | tf_op | source)
XLA Modules:
  0.0 485.1 jit_solution(14263018713188371922)
XLA Ops:
  2.9 8.8 %joint_pass.1 = (bf16[1088,768]{1,0:T(8,128)(2,1)}, bf16[1088,2304]{1,0:T(8,128)(2,1)}) custom-call(bf16[1088,768]{1,0:T(8,128)(2,1)} %tokens_ref.4, f32[768]{0:T(1024)} %gain_ref.7, f32[768]{0:T(1024)} %shift_ref.2, bf16[768,2304]{1,0:T(8,128)(2,1)} %weight_ref.5, f32[1536]{0:T(1024)} %bias_ref.1), custom_call_target="tpu_custom_call" | custom-call | bytes 1048576 | tf_op jit(solution)/shard_map/joint_pass/pallas_call | solution.py:631
  11.7 26.1 %attend.1 = (bf16[1088,768]{1,0:T(8,128)(2,1)}, f32[1088,768]{1,0:T(8,128)}) custom-call(s32[4]{0:T(128)} %pad_add_fusion.at_ref, s32[32]{0:T(128)} %bucket_ref.13, bf16[1088,2304]{1,0:T(8,128)(2,1)} %get-tuple-element.172.q_ref.k_ref.v_ref, bf16[1088,2304]{1,0:T(8,128)(2,1)} %get-tuple-element.172.q_ref.k_ref.v_ref, ...), custom_call_target="tpu_custom_call" | custom-call | bytes 1048576 | tf_op jit(solution)/shard_map/attend/pallas_call | solution.py:498
  40.4 30.2 %feed_pass.1 = (bf16[1088,768]{1,0:T(8,128)(2,1)}, f32[1088,768]{1,0:T(8,128)}, bf16[1088,768]{1,0:T(8,128)(2,1)}, bf16[1088,3072]{1,0:T(8,128)(2,1)}, bf16[1088...) custom-call(s32[4]{0:T(128)} %pad_add_fusion.at_ref, s32[32]{0:T(128)} %bucket_ref.13, ...), custom_call_target="tpu_custom_call" | custom-call | bytes 1048576 | tf_op jit(solution)/shard_map/feed_pass/pallas_call | solution.py:735
  70.6 7.5 %all-to-all-start = ((bf16[8,32,896]{2,1,0:T(8,128)(2,1)}), bf16[8,32,896]{2,1,0:T(8,128)(2,1)S(1)}, u32[]{:S(2)}, u32[]{:S(2)}) async-start(bf16[8,32,896]{2,1,0:T(8,128)(2,1)} %bitcast.301), calls=%async_computation | async-start | bytes 917504 | tf_op jit(solution)/shard_map/all_to_all | solution.py:1314
  82.7 7.4 %time_embedding.1 = (bf16[1024,1024]{1,0:T(8,128)(2,1)}, bf16[1024,1024]{1,0:T(8,128)(2,1)}, f32[1024,1024]{1,0:T(8,128)}) custom-call(bf16[1024,256]{1,0:T(8,128)(2,1)} %pad_maximum_fusion.2.sinus_ref, bf16[256,1024]{1,0:T(8,128)(2,1)} %first_ref.1, bf16[1024,1024]{1,0:T(8,128)(2,1)} %weight_ref.4), custom_call_target="tpu_custom_call" | custom-call | bytes 1048576 | tf_op jit(solution)/shard_map/time_embedding/pallas_call | solution.py:75
  92.0 50.9 %head_pass.1 = (f32[4,16,256]{2,1,0:T(8,128)}, bf16[3,1024,1024]{2,1,0:T(8,128)(2,1)}, bf16[1024,2048]{1,0:T(8,128)(2,1)}, bf16[1024,1024]{1,0:T(8,128)(2,1)}, b...) custom-call(bf16[256,896]{1,0:T(8,128)(2,1)} %bitcast.278, ...), custom_call_target="tpu_custom_call" | custom-call | bytes 1048576 | tf_op jit(solution)/shard_map/head_pass/pallas_call | solution.py:215
  143.0 16.1 %time_back.1.first_ref = bf16[1024,1024]{1,0:T(8,128)(2,1)} custom-call(bf16[1024,1024]{1,0:T(8,128)(2,1)} %get-tuple-element.185.grad_ref.timed_ref, bf16[1024,1024]{1,0:T(8,128)(2,1)} %weight_ref.4, bf16[1024,1024]{1,0:T(8,128)(2,1)} %get-tuple-element.186.slope_ref), custom_call_target="tpu_custom_call" | custom-call | bytes 1048576 | tf_op jit(solution)/shard_map/time_back/pallas_call | solution.py:353
  159.0 10.9 %head_grads_one.2 = (bf16[4,1024,512]{2,1,0:T(8,128)(2,1)}, f32[8,128]{1,0:T(8,128)}) custom-call(s32[3]{0:T(128)} %copy-done.26, bf16[3,1024,1024]{2,1,0:T(8,128)(2,1)} %get-tuple-element.197.left_ref.acted_ref, bf16[1024,2048]{1,0:T(8,128)(2,1)} %get-tuple-element.188.fin_ref, bf16[1024,1024]{1,0:T(8,128)(2,1)} %get-tuple-element.189.branch_ref, ...), custom_call_target="tpu_custom_call" | custom-call | bytes 1048576 | tf_op jit(solution)/shard_map/head_grads_one/pallas_call | solution.py:324
  170.0 4.9 %all-to-all-start.1 = ((bf16[8,32,768]{2,1,0:T(8,128)(2,1)}), bf16[8,32,768]{2,1,0:T(8,128)(2,1)S(1)}, u32[]{:S(2)}, u32[]{:S(2)}) async-start(bf16[8,32,768]{2,1,0:T(8,128)(2,1)} %bitcast.11), calls=%async_computation.1 | async-start | bytes 786432 | tf_op jit(solution)/shard_map/all_to_all | solution.py:1314
  174.9 13.7 %head_grads_two.2 = (bf16[10,1024,256]{2,1,0:T(8,128)(2,1)}, f32[8,128]{1,0:T(8,128)}) custom-call(s32[3]{0:T(128)} %copy-done.26, bf16[3,1024,1024]{2,1,0:T(8,128)(2,1)} %get-tuple-element.197.left_ref.acted_ref, bf16[1024,1024]{1,0:T(8,128)(2,1)} %get-tuple-element.201.low_ref, bf16[1024,3072]{1,0:T(8,128)(2,1)} %get-tuple-element.193.mod_ref, ...), custom_call_target="tpu_custom_call" | custom-call | bytes 1048576 | tf_op jit(solution)/shard_map/head_grads_two/pallas_call | solution.py:448
  189.2 11.1 %head_grads_one.3 = (bf16[2,1024,512]{2,1,0:T(8,128)(2,1)}, bf16[2,1024,512]{2,1,0:T(8,128)(2,1)}, f32[8,128]{1,0:T(8,128)}) custom-call(s32[3]{0:T(128)} %copy-done.24, bf16[3,1024,1024]{2,1,0:T(8,128)(2,1)} %get-tuple-element.197.left_ref.acted_ref, bf16[1024,2048]{1,0:T(8,128)(2,1)} %get-tuple-element.188.fin_ref, ...), custom_call_target="tpu_custom_call" | custom-call | flops 1099511627776 | bytes 1048576 | tf_op jit(solution)/shard_map/head_grads_one/pallas_call | solution.py:324
  200.9 15.9 %head_grads_two.3 = (bf16[2,1024,256]{2,1,0:T(8,128)(2,1)}, bf16[2,1024,256]{2,1,0:T(8,128)(2,1)}, bf16[6,512,256]{2,1,0:T(8,128)(2,1)}, bf16[6,512,256]{2,1,0:T(8,128)(2,1)}, f32[8,128]{1,0:T(8,128)}) custom-call(s32[3]{0:T(128)} %copy-done.24, bf16[3,1024,1024]{2,1,0:T(8,128)(2,1)} %get-tuple-element.197.left_ref.acted_ref, ...), custom_call_target="tpu_custom_call" | custom-call | flops 1099511627776 | bytes 1048576 | tf_op jit(solution)/shard_map/head_grads_two/pallas_call | solution.py:448
  220.1 21.6 %feed_back.1 = (bf16[1088,768]{1,0:T(8,128)(2,1)}, bf16[1088,3072]{1,0:T(8,128)(2,1)}, f32[1088,768]{1,0:T(8,128)}, bf16[1088,768]{1,0:T(8,128)(2,1)}, bf16[1088...) custom-call(s32[4]{0:T(128)} %pad_add_fusion.at_ref, s32[32]{0:T(128)} %bucket_ref.13, ...), custom_call_target="tpu_custom_call" | custom-call | bytes 1048576 | tf_op jit(solution)/shard_map/feed_back/pallas_call | solution.py:823
  241.7 14.2 %feed_grads.2 = (bf16[2,768,768]{2,1,0:T(8,128)(2,1)}, bf16[2,768,768]{2,1,0:T(8,128)(2,1)}, f32[8,128]{1,0:T(8,128)}) custom-call(s32[3]{0:T(128)} %copy-done.26, bf16[1088,768]{1,0:T(8,128)(2,1)} %get-tuple-element.226.second_ref, bf16[1088,3072]{1,0:T(8,128)(2,1)} %get-tuple-element.216.hidden_ref, bf16[1088,3072]{1,0:T(8,128)(2,1)} %get-tuple-element.217.active_ref, ...), custom_call_target="tpu_custom_call" | custom-call | bytes 1048576 | tf_op jit(solution)/shard_map/feed_grads/pallas_call | solution.py:904
  259.3 15.7 %attend_back.3.a_ref = bf16[3,1088,256]{2,1,0:T(8,128)(2,1)} custom-call(s32[4]{0:T(128)} %pad_add_fusion.at_ref, s32[32]{0:T(128)} %bucket_ref.13, bf16[1088,2304]{1,0:T(8,128)(2,1)} %get-tuple-element.172.q_ref.k_ref.v_ref, bf16[1088,2304]{1,0:T(8,128)(2,1)} %get-tuple-element.172.q_ref.k_ref.v_ref, ...), custom_call_target="tpu_custom_call" | custom-call | flops 1099511627776 | bytes 1048576 | tf_op jit(solution)/shard_map/attend_back/pallas_call | solution.py:539
  281.5 15.8 %feed_grads.3 = (bf16[1,768,768]{2,1,0:T(8,128)(2,1)}, bf16[1,768,768]{2,1,0:T(8,128)(2,1)}, bf16[2,384,768]{2,1,0:T(8,128)(2,1)}, bf16[2,384,768]{2,1,0:T(8,128)(2,1)}, f32[8,128]{1,0:T(8,128)}) custom-call(s32[3]{0:T(128)} %copy-done.24, bf16[1088,768]{1,0:T(8,128)(2,1)} %get-tuple-element.226.second_ref, ...), custom_call_target="tpu_custom_call" | custom-call | flops 1099511627776 | bytes 1048576 | tf_op jit(solution)/shard_map/feed_grads/pallas_call | solution.py:904
  304.2 15.7 %attend_back.4.b_ref = bf16[3,1088,256]{2,1,0:T(8,128)(2,1)} custom-call(s32[4]{0:T(128)} %pad_add_fusion.at_ref, s32[32]{0:T(128)} %bucket_ref.13, bf16[1088,2304]{1,0:T(8,128)(2,1)} %get-tuple-element.172.q_ref.k_ref.v_ref, bf16[1088,2304]{1,0:T(8,128)(2,1)} %get-tuple-element.172.q_ref.k_ref.v_ref, ...), custom_call_target="tpu_custom_call" | custom-call | flops 1099511627776 | bytes 1048576 | tf_op jit(solution)/shard_map/attend_back/pallas_call | solution.py:539
  319.8 9.4 %collective-permute-done.9 = bf16[1,768,768]{2,1,0:T(8,128)(2,1)} collective-permute-done((bf16[1,768,768]{2,1,0:T(8,128)(2,1)}, bf16[1,768,768]{2,1,0:T(8,128)(2,1)}, u32[]{:S(2)}, u32[]{:S(2)}) %collective-permute-start.9) | collective-permute-done | bytes 1179680 | tf_op jit(solution)/shard_map/ppermute | solution.py:1060
  343.2 15.8 %attend_back.5.c_ref = bf16[3,1088,256]{2,1,0:T(8,128)(2,1)} custom-call(s32[4]{0:T(128)} %pad_add_fusion.at_ref, s32[32]{0:T(128)} %bucket_ref.13, bf16[1088,2304]{1,0:T(8,128)(2,1)} %get-tuple-element.172.q_ref.k_ref.v_ref, bf16[1088,2304]{1,0:T(8,128)(2,1)} %get-tuple-element.172.q_ref.k_ref.v_ref, ...), custom_call_target="tpu_custom_call" | custom-call | flops 1099511627776 | bytes 1048576 | tf_op jit(solution)/shard_map/attend_back/pallas_call | solution.py:539
  372.2 8.2 %last_grads.2 = (bf16[12,768,128]{2,1,0:T(8,128)(2,1)}, f32[8,128]{1,0:T(8,128)}) custom-call(s32[3]{0:T(128)} %copy-done.26, bf16[1088,768]{1,0:T(8,128)(2,1)} %get-tuple-element.253.first_ref, bf16[1088,768]{1,0:T(8,128)(2,1)} %get-tuple-element.173.mixed_ref.o_ref, bf16[3,1088,256]{2,1,0:T(8,128)(2,1)} %attend_back.3.a_ref, ...), custom_call_target="tpu_custom_call" | custom-call | bytes 1048576 | tf_op jit(solution)/shard_map/last_grads/pallas_call | solution.py:947
  384.6 4.8 collective-permute-done.18.refs_1_
  389.4 8.6 %last_grads.3 = (bf16[12,768,128]{2,1,0:T(8,128)(2,1)}, f32[8,128]{1,0:T(8,128)}) custom-call(s32[3]{0:T(128)} %copy-done.24, bf16[1088,768]{1,0:T(8,128)(2,1)} %get-tuple-element.253.first_ref, bf16[1088,768]{1,0:T(8,128)(2,1)} %get-tuple-element.173.mixed_ref.o_ref, bf16[3,1088,256]{2,1,0:T(8,128)(2,1)} %attend_back.3.a_ref, ...), custom_call_target="tpu_custom_call" | custom-call | bytes 1048576 | tf_op jit(solution)/shard_map/last_grads/pallas_call | solution.py:947
  411.9 10.3 %tokens_back.1 = (f32[1088,768]{1,0:T(8,128)}, f32[8,384]{1,0:T(8,128)}) custom-call(bf16[1088,768]{1,0:T(8,128)(2,1)} %tokens_ref.4, bf16[3,1088,256]{2,1,0:T(8,128)(2,1)} %attend_back.3.a_ref, bf16[3,1088,256]{2,1,0:T(8,128)(2,1)} %attend_back.4.b_ref, bf16[3,1088,256]{2,1,0:T(8,128)(2,1)} %attend_back.5.c_ref, f32[1088,768]{1,0:T(8,128)} %get-tuple-element.260.middle_ref, ...), custom_call_target="tpu_custom_call" | custom-call | bytes 1048576 | tf_op jit(solution)/shard_map/tokens_back/pallas_call | solution.py:1001
  457.0 3.9 collective-permute-done.30
  (215 shorter events, 136.2 us)
Async XLA Ops:
  70.6 20.6 %all-to-all-start = ((bf16[8,32,896]{2,1,0:T(8,128)(2,1)}), bf16[8,32,896]{2,1,0:T(8,128)(2,1)S(1)}, u32[]{:S(2)}, u32[]{:S(2)}) async-start(bf16[8,32,896]{2,1,0:T(8,128)(2,1)} %bitcast.301), calls=%async_computation | async-start | bytes 917504 | tf_op jit(solution)/shard_map/all_to_all | solution.py:1314
  170.0 19.2 %collective-permute-start = (bf16[4,1024,512]{2,1,0:T(8,128)(2,1)}, bf16[4,1024,512]{2,1,0:T(8,128)(2,1)}, u32[]{:S(2)}, u32[]{:S(2)}) collective-permute-start(bf16[4,1024,512]{2,1,0:T(8,128)(2,1)} %get-tuple-element.198), channel_id=1, source_target_pairs={{0,1},{1,0},{2,3},{3,2},{4,5},{5,4},{6,7},{7,6},{8,9},{9,8},{10,11... | collective-permute-start | bytes 12582920 | tf_op jit(solution)/shard_map/ppermute | solution.py:1060
  200.3 56.2 %collective-permute-start.4 = (bf16[2,1024,512]{2,1,0:T(8,128)(2,1)}, bf16[2,1024,512]{2,1,0:T(8,128)(2,1)}, u32[]{:S(2)}, u32[]{:S(2)}) collective-permute-start(bf16[2,1024,512]{2,1,0:T(8,128)(2,1)} %get-tuple-element.213), channel_id=1, source_target_pairs={{0,2},{1,3},{2,0},{3,1},{4,6},{5,7},{6,4},{7,5},{8,10},{9,11},{10,... | collective-permute-start | bytes 6291464 | tf_op jit(solution)/shard_map/ppermute | solution.py:1060
  216.8 58.1 %collective-permute-start.2 = (bf16[2,1024,256]{2,1,0:T(8,128)(2,1)}, bf16[2,1024,256]{2,1,0:T(8,128)(2,1)}, u32[]{:S(2)}, u32[]{:S(2)}) collective-permute-start(bf16[2,1024,256]{2,1,0:T(8,128)(2,1)} %get-tuple-element.205), channel_id=1, source_target_pairs={{0,2},{1,3},{2,0},{3,1},{4,6},{5,7},{6,4},{7,5},{8,10},{9,11},{10,... | collective-permute-start | bytes 3145736 | tf_op jit(solution)/shard_map/ppermute | solution.py:1060
  218.4 56.6 %collective-permute-start.3 = (bf16[6,512,256]{2,1,0:T(8,128)(2,1)}, bf16[6,512,256]{2,1,0:T(8,128)(2,1)}, u32[]{:S(2)}, u32[]{:S(2)}) collective-permute-start(bf16[6,512,256]{2,1,0:T(8,128)(2,1)} %get-tuple-element.206), channel_id=1, source_target_pairs={{0,4},{4,0},{8,12},{12,8},{16,20},{20,16},{24,28},{28,24},{1,5},{5... | collective-permute-start | bytes 4718600 | tf_op jit(solution)/shard_map/ppermute | solution.py:1060
  255.9 25.6 %collective-permute-start.7 = (bf16[2,768,768]{2,1,0:T(8,128)(2,1)}, bf16[2,768,768]{2,1,0:T(8,128)(2,1)}, u32[]{:S(2)}, u32[]{:S(2)}) collective-permute-start(bf16[2,768,768]{2,1,0:T(8,128)(2,1)} %get-tuple-element.227), channel_id=1, source_target_pairs={{0,1},{1,0},{2,3},{3,2},{4,5},{5,4},{6,7},{7,6},{8,9},{9,8},{10,11... | collective-permute-start | bytes 7077896 | tf_op jit(solution)/shard_map/ppermute | solution.py:1060
  256.0 25.6 %collective-permute-start.8 = (bf16[2,768,768]{2,1,0:T(8,128)(2,1)}, bf16[2,768,768]{2,1,0:T(8,128)(2,1)}, u32[]{:S(2)}, u32[]{:S(2)}) collective-permute-start(bf16[2,768,768]{2,1,0:T(8,128)(2,1)} %get-tuple-element.228), channel_id=1, source_target_pairs={{0,1},{1,0},{2,3},{3,2},{4,5},{5,4},{6,7},{7,6},{8,9},{9,8},{10,11... | collective-permute-start | bytes 7077896 | tf_op jit(solution)/shard_map/ppermute | solution.py:1060
  259.0 38.4 %collective-permute-start.11 = (bf16[2,2,2,128,512]{4,3,0,2,1:T(8,128)(2,1)}, bf16[2,2,2,128,512]{4,3,0,2,1:T(8,128)(2,1)}, u32[]{:S(2)}, u32[]{:S(2)}) collective-permute-start(bf16[2,2,2,128,512]{4,3,0,2,1:T(8,128)(2,1)} %fusion), channel_id=1, source_target_pairs={{0,4},{4,0},{8,12},{12,8},{16,20},{20,16},{24,28},{28,24},{1,5},{5... | collective-permute-start | bytes 3145736 | tf_op jit(solution)/shard_map/ppermute | solution.py:1060
  277.1 58.5 %collective-permute-start.5 = (bf16[2,2,2,128,256]{4,3,0,2,1:T(8,128)(2,1)}, bf16[2,2,2,128,256]{4,3,0,2,1:T(8,128)(2,1)}, u32[]{:S(2)}, u32[]{:S(2)}) collective-permute-start(bf16[2,2,2,128,256]{4,3,0,2,1:T(8,128)(2,1)} %fusion.20), channel_id=1, source_target_pairs={{0,4},{4,0},{8,12},{12,8},{16,20},{20,16},{24,28},{28,24},{1,5},{5... | collective-permute-start | bytes 1572872 | tf_op jit(solution)/shard_map/ppermute | solution.py:1060
  281.0 54.6 %collective-permute-start.6 = (bf16[3,2,2,128,256]{4,3,0,2,1:T(8,128)(2,1)}, bf16[3,2,2,128,256]{4,3,0,2,1:T(8,128)(2,1)}, u32[]{:S(2)}, u32[]{:S(2)}) collective-permute-start(bf16[3,2,2,128,256]{4,3,0,2,1:T(8,128)(2,1)} %fusion.2), channel_id=1, source_target_pairs={{0,2},{1,3},{2,0},{3,1},{4,6},{5,7},{6,4},{7,5},{8,10},{9,11},{10,... | collective-permute-start | bytes 2359304 | tf_op jit(solution)/shard_map/ppermute | solution.py:1060
  299.7 39.7 %collective-permute-start.15 = (bf16[2,2,128,512]{3,2,0,1:T(8,128)(2,1)}, bf16[2,2,128,512]{3,2,0,1:T(8,128)(2,1)}, u32[]{:S(2)}, u32[]{:S(2)}) collective-permute-start(bf16[2,2,128,512]{3,2,0,1:T(8,128)(2,1)} %fusion.1), channel_id=1, source_target_pairs={{0,16},{4,20},{8,24},{12,28},{16,0},{20,4},{24,8},{28,12},{1,17},{... | collective-permute-start | bytes 1572872 | tf_op jit(solution)/shard_map/ppermute | solution.py:1060
  302.1 27.2 %collective-permute-start.9 = (bf16[1,768,768]{2,1,0:T(8,128)(2,1)}, bf16[1,768,768]{2,1,0:T(8,128)(2,1)}, u32[]{:S(2)}, u32[]{:S(2)}) collective-permute-start(bf16[1,768,768]{2,1,0:T(8,128)(2,1)} %get-tuple-element.232), channel_id=1, source_target_pairs={{0,2},{1,3},{2,0},{3,1},{4,6},{5,7},{6,4},{7,5},{8,10},{9,11},{10,... | collective-permute-start | bytes 3538952 | tf_op jit(solution)/shard_map/ppermute | solution.py:1060
  303.6 26.9 %collective-permute-start.10 = (bf16[2,384,768]{2,1,0:T(8,128)(2,1)}, bf16[2,384,768]{2,1,0:T(8,128)(2,1)}, u32[]{:S(2)}, u32[]{:S(2)}) collective-permute-start(bf16[2,384,768]{2,1,0:T(8,128)(2,1)} %get-tuple-element.233), channel_id=1, source_target_pairs={{0,4},{4,0},{8,12},{12,8},{16,20},{20,16},{24,28},{28,24},{1,5},{5... | collective-permute-start | bytes 3538952 | tf_op jit(solution)/shard_map/ppermute | solution.py:1060
  332.5 30.7 %collective-permute-start.13 = (bf16[1,2,2,96,768]{4,3,2,1,0:T(8,128)(2,1)}, bf16[1,2,2,96,768]{4,3,2,1,0:T(8,128)(2,1)}, u32[]{:S(2)}, u32[]{:S(2)}) collective-permute-start(bf16[1,2,2,96,768]{4,3,2,1,0:T(8,128)(2,1)} %fusion.7), channel_id=1, source_target_pairs={{0,4},{4,0},{8,12},{12,8},{16,20},{20,16},{24,28},{28,24},{1,5},{5... | collective-permute-start | bytes 1769480 | tf_op jit(solution)/shard_map/ppermute | solution.py:1060
  335.1 28.1 %collective-permute-start.14 = (bf16[1,2,2,96,768]{4,3,2,1,0:T(8,128)(2,1)}, bf16[1,2,2,96,768]{4,3,2,1,0:T(8,128)(2,1)}, u32[]{:S(2)}, u32[]{:S(2)}) collective-permute-start(bf16[1,2,2,96,768]{4,3,2,1,0:T(8,128)(2,1)} %fusion.8), channel_id=1, source_target_pairs={{0,2},{1,3},{2,0},{3,1},{4,6},{5,7},{6,4},{7,5},{8,10},{9,11},{10,... | collective-permute-start | bytes 1769480 | tf_op jit(solution)/shard_map/ppermute | solution.py:1060
  339.1 29.1 %collective-permute-start.12 = (bf16[5,2,128,256]{3,2,0,1:T(8,128)(2,1)}, bf16[5,2,128,256]{3,2,0,1:T(8,128)(2,1)}, u32[]{:S(2)}, u32[]{:S(2)}) collective-permute-start(bf16[5,2,128,256]{3,2,0,1:T(8,128)(2,1)} %pad_maximum_fusion), channel_id=1, source_target_pairs={{0,16},{4,20},{8,24},{12,28},{16,0},{20,4},{24,8},{28,12},{1,17},{... | collective-permute-start | bytes 1966088 | tf_op jit(solution)/shard_map/ppermute | solution.py:1060
  341.4 28.6 %collective-permute-start.17 = (bf16[2,128,512]{2,1,0:T(8,128)(2,1)}, bf16[2,128,512]{2,1,0:T(8,128)(2,1)}, u32[]{:S(2)}, u32[]{:S(2)}) collective-permute-start(bf16[2,128,512]{2,1,0:T(8,128)(2,1)} %fusion.23), channel_id=1, source_target_pairs={{0,8},{4,12},{8,0},{12,4},{16,24},{20,28},{24,16},{28,20},{1,9},{5... | collective-permute-start | bytes 786440 | tf_op jit(solution)/shard_map/ppermute | solution.py:1060
  380.4 19.5 %collective-permute-start.19 = (bf16[12,768,128]{2,1,0:T(8,128)(2,1)}, bf16[12,768,128]{2,1,0:T(8,128)(2,1)}, u32[]{:S(2)}, u32[]{:S(2)}) collective-permute-start(bf16[12,768,128]{2,1,0:T(8,128)(2,1)} %get-tuple-element.255), channel_id=1, source_target_pairs={{0,1},{1,0},{2,3},{3,2},{4,5},{5,4},{6,7},{7,6},{8,9},{9,8},{10,11... | collective-permute-start | bytes 7077896 | tf_op jit(solution)/shard_map/ppermute | solution.py:1060
  382.8 45.3 %collective-permute-start.21 = (bf16[2,2,96,768]{3,2,0,1:T(8,128)(2,1)}, bf16[2,2,96,768]{3,2,0,1:T(8,128)(2,1)}, u32[]{:S(2)}, u32[]{:S(2)}) collective-permute-start(bf16[2,2,96,768]{3,2,0,1:T(8,128)(2,1)} %copy.90), channel_id=1, source_target_pairs={{0,16},{4,20},{8,24},{12,28},{16,0},{20,4},{24,8},{28,12},{1,17},{... | collective-permute-start | bytes 1769480 | tf_op jit(solution)/shard_map/ppermute | solution.py:1060
  382.8 26.7 %collective-permute-start.16 = (bf16[5,128,256]{2,1,0:T(8,128)(2,1)}, bf16[5,128,256]{2,1,0:T(8,128)(2,1)}, u32[]{:S(2)}, u32[]{:S(2)}) collective-permute-start(bf16[5,128,256]{2,1,0:T(8,128)(2,1)} %fusion.6), channel_id=1, source_target_pairs={{0,8},{4,12},{8,0},{12,4},{16,24},{20,28},{24,16},{28,20},{1,9},{5... | collective-permute-start | bytes 983048 | tf_op jit(solution)/shard_map/ppermute | solution.py:1060
  402.9 20.3 %collective-permute-start.22 = (bf16[3,2,2,2,96,128]{5,4,0,3,2,1:T(8,128)(2,1)}, bf16[3,2,2,2,96,128]{5,4,0,3,2,1:T(8,128)(2,1)}, u32[]{:S(2)}, u32[]{:S(2)}) collective-permute-start(bf16[3,2,2,2,96,128]{5,4,0,3,2,1:T(8,128)(2,1)} %fusion.9), channel_id=1, source_target_pairs={{0,2},{1,3},{2,0},{3,1},{4,6},{5,7},{6,4},{7,5},{8,10},{9,11},{10,... | collective-permute-start | bytes 1769480 | tf_op jit(solution)/shard_map/ppermute | solution.py:1060
  409.4 28.1 %collective-permute-start.27 = (bf16[2,128,512]{2,1,0:T(8,128)(2,1)}, bf16[2,128,512]{2,1,0:T(8,128)(2,1)}, u32[]{:S(2)}, u32[]{:S(2)}) collective-permute-start(bf16[2,128,512]{2,1,0:T(8,128)(2,1)} %fusion.22.refs_0_), channel_id=1, source_target_pairs={{0,1},{1,0},{2,3},{3,2},{4,5},{5,4},{6,7},{7,6},{8,9},{9,8},{10,11... | collective-permute-start | bytes 786440 | tf_op jit(solution)/shard_map/ppermute | solution.py:1060
  409.4 28.6 %collective-permute-start.28 = (bf16[2,128,512]{2,1,0:T(8,128)(2,1)}, bf16[2,128,512]{2,1,0:T(8,128)(2,1)}, u32[]{:S(2)}, u32[]{:S(2)}) collective-permute-start(bf16[2,128,512]{2,1,0:T(8,128)(2,1)} %collective-permute-done.18.refs_1_), channel_id=1, source_target_pairs={{0,1},{1,0},{2,3},{3,2},{4,5},{5,4},{6,7},{7,6},{8,9},{9,8},{10,11... | collective-permute-start | bytes 786440 | tf_op jit(solution)/shard_map/ppermute | solution.py:1060
  434.2 19.8 %collective-permute-start.32 = (bf16[5,128,256]{2,1,0:T(8,128)(2,1)}, bf16[5,128,256]{2,1,0:T(8,128)(2,1)}, u32[]{:S(2)}, u32[]{:S(2)}) collective-permute-start(bf16[5,128,256]{2,1,0:T(8,128)(2,1)} %fusion.5.refs_0_), channel_id=1, source_target_pairs={{0,1},{1,0},{2,3},{3,2},{4,5},{5,4},{6,7},{7,6},{8,9},{9,8},{10,11... | collective-permute-start | bytes 983048 | tf_op jit(solution)/shard_map/ppermute | solution.py:1060
  (50 other events, 504.8 us)
where the time goes:
time: 491 us; the launch traced here: 485 us
  Pallas kernels  333 us (68%)
  other arithmetic  58.7 us (12%)
  starting transfers between devices  48.1 us (10%)
  waiting for transfers between devices  26.7 us (5%)
  local copies, waits for them, and re-layouts  17.7 us (4%)
    pallas_call x1, Pallas kernels, head_pass(): pl.pallas_call(head_kernel, grid=(REPEATS,), in_specs=[whole_block(dealt....  50.9 us
    pallas_call x3, Pallas kernels, attend_back(): pl.pallas_call(partial(attend_back_kernel, KB), grid=(count,), in_specs=[...  47.1 us
    ppermute x45, starting transfers between devices, swap(): return lax.ppermute(array, axis, [(i, i ^ mask) for i in range(count)])  35.7 us
    pallas_call x1, Pallas kernels, feed_pass(): pl.pallas_call(feed_kernel, grid=(seq // ROWS,), in_specs=[smem(), smem()...  30.2 us
    pallas_call x2, Pallas kernels, feed_grads(): pl.pallas_call(partial(feed_grads_kernel, wide), grid_spec=pltpu.Prefetch...  30 us
    pallas_call x2, Pallas kernels, head_grads_two(): pl.pallas_call(partial(head_grads_two_kernel, wide), grid_spec=pltpu.Pref...  29.6 us
    pallas_call x1, Pallas kernels, attend(): pl.pallas_call(partial(attend_kernel, QB), grid=(PAIRS,), in_specs=[smem(...  26.1 us
    ppermute x45, waiting for transfers between devices, swap(): return lax.ppermute(array, axis, [(i, i ^ mask) for i in range(count)])  25.6 us
  transfers between devices with their start and end apart: 47, of which 8 were waited for; matrix products, arithmetic and copies ran while one was open for 14% of the time, Pallas kernels for 36%

commit v1 on v0

--- a/solution.py
+++ b/solution.py
@@ -922,13 +922,29 @@
     )(half, second, hidden_grad, active, feed_grad, *more)
 
 
-def last_grads_kernel(half_ref, first_ref, mixed_ref, a_ref, b_ref, c_ref, branch_ref, out_ref, mark_ref):
-    kind = half_ref[0] * 2 + pl.program_id(0)
+def last_kind(turn, half):
+    return (turn // 2 ^ (1 - half[0])) * 2 + turn % 2
+
+
+def last_grads_kernel(
+    half_ref, first_ref, mixed_ref, a_ref, b_ref, c_ref, branch_ref, sent_ref, kept_ref, mark_ref
+):
+    turn = pl.program_id(0)
+    kind = last_kind(turn, half_ref)
     mark_ref[...] = jnp.zeros_like(mark_ref)
 
     def put(whole):
-        for i in range(6):
-            out_ref[i] = whole[:, i * 128 : (i + 1) * 128].astype(jnp.bfloat16)
+        whole = whole.astype(jnp.bfloat16)
+
+        @pl.when(turn < 2)
+        def _():
+            for i in range(6):
+                sent_ref[i] = whole[:, i * 128 : (i + 1) * 128]
+
+        @pl.when(turn >= 2)
+        def _():
+            for i in range(6):
+                kept_ref[i] = whole[:, i * 128 : (i + 1) * 128]
 
     @pl.when(kind < 3)
     def _():
@@ -942,19 +958,24 @@
 def last_grads(half, first_in, mixed, parts, branch_grad):
     seq = mixed.shape[0]
     part = lambda a: pl.BlockSpec(
-        (1,) + a.shape[1:], lambda i, half: (jnp.minimum(half[0] * 2 + i, 2), 0, 0)
-    )
+        (1,) + a.shape[1:], lambda i, half: (jnp.minimum(last_kind(i, half), 2), 0, 0)
+    )
+    tiles = jax.ShapeDtypeStruct((12, D, 128), jnp.bfloat16)
     return pl.pallas_call(
         last_grads_kernel,
         grid_spec=pltpu.PrefetchScalarGridSpec(
             num_scalar_prefetch=1,
-            grid=(2,),
+            grid=(4,),
             in_specs=[whole_block((seq, D)), whole_block((seq, D))]
             + [part(a) for a in parts]
             + [whole_block((seq, D))],
-            out_specs=[pl.BlockSpec((6, D, 128), lambda i, half: (i, 0, 0)), whole_block((8, 128))],
+            out_specs=[
+                pl.BlockSpec((6, D, 128), lambda i, half: (jnp.minimum(i, 1), 0, 0)),
+                pl.BlockSpec((6, D, 128), lambda i, half: (jnp.maximum(i - 2, 0), 0, 0)),
+                whole_block((8, 128)),
+            ],
         ),
-        out_shape=[jax.ShapeDtypeStruct((12, D, 128), jnp.bfloat16), MARK],
+        out_shape=[tiles, tiles, MARK],
         compiler_params=pltpu.CompilerParams(vmem_limit_bytes=VMEM),
         cost_estimate=OTHER,
         name="last_grads",
@@ -1017,7 +1038,7 @@
 
 
 def pack_kernel(feed_ref, hidden_ref, input_ref, final_ref, token_ref, *refs):
-    out_ref = refs[-1]
+    low_ref, out_ref = refs[-2:]
     out_ref[...] = jnp.zeros_like(out_ref)
     wide, rows, cols = out_ref.shape
     part = D // wide
@@ -1031,18 +1052,20 @@
             out_ref[w, TOKEN_DIM + 1 : TOKEN_DIM + 2, i * part : (i + 1) * part] = feed_ref[
                 i : i + 1, w * part : (w + 1) * part
             ]
+    low_ref[...] = out_ref[...].astype(jnp.bfloat16)
 
 
 def pack(feed_sums, hidden_sum, input_grad, final_grad, token_packed, marks):
     operands = (feed_sums, hidden_sum, input_grad, final_grad, token_packed)
     wide = token_packed.shape[0]
-    shape = (wide, TOKEN_DIM + 8, hidden_sum.shape[1] // wide)
+    shape = (wide, TOKEN_DIM + 16, hidden_sum.shape[1] // wide)
     return pl.pallas_call(
         pack_kernel,
         grid=(1,),
         in_specs=[whole_block(a.shape) for a in operands] + [pl.BlockSpec(memory_space=pl.ANY)] * len(marks),
         out_specs=whole_block(shape),
-        out_shape=jax.ShapeDtypeStruct(shape, jnp.float32),
+        out_shape=jax.ShapeDtypeStruct(shape, jnp.bfloat16),
+        scratch_shapes=[pltpu.VMEM(shape, jnp.float32)],
         cost_estimate=OTHER,
         name="pack",
     )(*operands, *marks)
@@ -1150,6 +1173,7 @@
         self.send((share, "narrow", 2))
         yield
         (other,) = self.take()
+        share = self.order(share)
         self.send((share, "narrow", 1), (other, "narrow", 1))
         yield
         self.result = (share, other) + tuple(self.take())
@@ -1410,18 +1434,15 @@
     order.at(mark)
     one.step()
     attend_back_part(1)
-    feed.step()
     two.step()
     one.step()
+    feed.step()
     attend_back_part(2)
     feed.step()
     two.step()
     one.step()
-    last_args = (mixed, parts, out_grad)
-    halves_last = Halves(order, last_grads(other, order(first_in), *last_args))
-    one.step()
-    own, mark = last_grads(mine, order(first_in), *last_args)
-    note(mark)
+    sent, own, mark = last_grads(mine, order(first_in), mixed, parts, out_grad)
+    halves_last = Halves(order, (sent, mark))
     terms = [
         a.reshape((2, 6) + (2,) * (wide.bit_length() - 1) + (-1, 128)) for a in (own,) + halves_last.got()
     ]
@@ -1429,7 +1450,6 @@
         order, [([a[:, :3] for a in terms], ("x", "y")), ([a[:, 3:] for a in terms], ("y", "x"))]
     )
     last.step()
-    two.step()
     tokens_gradient, token_packed = tokens_back(
         order(tokens), parts, middle_grad, first_gain, joint_weight, wide
     )
@@ -1443,11 +1463,14 @@
         return outs
 
     last.step()
+    two.step()
     feed.step()
-    two.step()
+    one.step()
     packed = pack(feed_sums, hidden_sum, input_grad, final_grad, order(token_packed), order.marks)
     order.at(packed)
     small = small_steps(order, packed)
+    next(small)
+    last.step()
     next(small)
     one = one.finish()
     final_mod_out, block_reduce_out, block_expand_out = hold(
@@ -1457,8 +1480,7 @@
             ((rows, 2 * width), (rows, width), (rows, width)),
         )
     )
-    last.step()
-    next(small)
+    two.step()
     feed.step()
     two = two.finish()
 

time: 491 us -> 486 us (0.990)
  starting transfers between devices: 48.1 us -> 63.4 us
  waiting for transfers between devices: 26.7 us -> 14.7 us
    ppermute x45, starting transfers between devices: 35.7 us -> 51 us  [swap(): return lax.ppermute(array, axis, [(i, i ^ mask) for i in range(count)])]
    ppermute x45, waiting for transfers between devices: 25.6 us -> 13.6 us  [swap(): return lax.ppermute(array, axis, [(i, i ^ mask) for i in range(count)])]
    pallas_call x2 -> x1, Pallas kernels: 16.9 us -> 12.9 us  [last_grads(): pl.pallas_call(last_grads_kernel, grid_spec=pltpu.PrefetchScalarGridSpec(...]
  transfers between devices with their start and end apart: 47 -> 47, of which waited for: 8 -> 7; matrix products, arithmetic and copies ran while one was open for 14% -> 13% of each run, Pallas kernels for 36% -> 35%
where the time goes in v1:
time: 486 us; the launch traced here: 479 us
  Pallas kernels  329 us (68%)
  starting transfers between devices  63.4 us (13%)
  other arithmetic  56.1 us (12%)
  local copies, waits for them, and re-layouts  15 us (3%)
  waiting for transfers between devices  14.7 us (3%)
    ppermute x45, starting transfers between devices, swap(): return lax.ppermute(array, axis, [(i, i ^ mask) for i in range(count)])  51 us
    pallas_call x1, Pallas kernels, head_pass(): pl.pallas_call(head_kernel, grid=(REPEATS,), in_specs=[whole_block(dealt....  50.9 us
    pallas_call x3, Pallas kernels, attend_back(): pl.pallas_call(partial(attend_back_kernel, KB), grid=(count,), in_specs=[...  47.2 us
    pallas_call x1, Pallas kernels, feed_pass(): pl.pallas_call(feed_kernel, grid=(seq // ROWS,), in_specs=[smem(), smem()...  30.2 us
    pallas_call x2, Pallas kernels, feed_grads(): pl.pallas_call(partial(feed_grads_kernel, wide), grid_spec=pltpu.Prefetch...  30 us
    pallas_call x2, Pallas kernels, head_grads_two(): pl.pallas_call(partial(head_grads_two_kernel, wide), grid_spec=pltpu.Pref...  29.6 us
    pallas_call x1, Pallas kernels, attend(): pl.pallas_call(partial(attend_kernel, QB), grid=(PAIRS,), in_specs=[smem(...  26.1 us
    pallas_call x2, Pallas kernels, head_grads_one(): pl.pallas_call(head_grads_one_kernel, grid_spec=pltpu.PrefetchScalarGridS...  22 us
  transfers between devices with their start and end apart: 47, of which 7 were waited for; matrix products, arithmetic and copies ran while one was open for 13% of the time, Pallas kernels for 35%

profile of v1, /device:TPU:0, one launch (start us, length us, event | category | flops | bytes accessed | tf_op | source)
XLA Modules:
  0.0 479.4 jit_solution(6238644665260507151)
XLA Ops:
  2.9 8.8 %joint_pass.1 = (bf16[1088,768]{1,0:T(8,128)(2,1)}, bf16[1088,2304]{1,0:T(8,128)(2,1)}) custom-call(bf16[1088,768]{1,0:T(8,128)(2,1)} %tokens_ref.4, f32[768]{0:T(1024)} %gain_ref.7, f32[768]{0:T(1024)} %shift_ref.2, bf16[768,2304]{1,0:T(8,128)(2,1)} %weight_ref.5, f32[1536]{0:T(1024)} %bias_ref.1), custom_call_target="tpu_custom_call" | custom-call | bytes 1048576 | tf_op jit(solution)/shard_map/joint_pass/pallas_call | solution.py:631
  11.7 26.1 %attend.1 = (bf16[1088,768]{1,0:T(8,128)(2,1)}, f32[1088,768]{1,0:T(8,128)}) custom-call(s32[4]{0:T(128)} %pad_add_fusion.at_ref, s32[32]{0:T(128)} %bucket_ref.13, bf16[1088,2304]{1,0:T(8,128)(2,1)} %get-tuple-element.174.q_ref.k_ref.v_ref, bf16[1088,2304]{1,0:T(8,128)(2,1)} %get-tuple-element.174.q_ref.k_ref.v_ref, ...), custom_call_target="tpu_custom_call" | custom-call | bytes 1048576 | tf_op jit(solution)/shard_map/attend/pallas_call | solution.py:498
  40.4 30.2 %feed_pass.1 = (bf16[1088,768]{1,0:T(8,128)(2,1)}, f32[1088,768]{1,0:T(8,128)}, bf16[1088,768]{1,0:T(8,128)(2,1)}, bf16[1088,3072]{1,0:T(8,128)(2,1)}, bf16[1088...) custom-call(s32[4]{0:T(128)} %pad_add_fusion.at_ref, s32[32]{0:T(128)} %bucket_ref.13, ...), custom_call_target="tpu_custom_call" | custom-call | bytes 1048576 | tf_op jit(solution)/shard_map/feed_pass/pallas_call | solution.py:735
  70.6 7.5 %all-to-all-start = ((bf16[8,32,896]{2,1,0:T(8,128)(2,1)}), bf16[8,32,896]{2,1,0:T(8,128)(2,1)S(1)}, u32[]{:S(2)}, u32[]{:S(2)}) async-start(bf16[8,32,896]{2,1,0:T(8,128)(2,1)} %bitcast.302), calls=%async_computation | async-start | bytes 917504 | tf_op jit(solution)/shard_map/all_to_all | solution.py:1338
  82.7 7.4 %time_embedding.1 = (bf16[1024,1024]{1,0:T(8,128)(2,1)}, bf16[1024,1024]{1,0:T(8,128)(2,1)}, f32[1024,1024]{1,0:T(8,128)}) custom-call(bf16[1024,256]{1,0:T(8,128)(2,1)} %pad_maximum_fusion.2.sinus_ref, bf16[256,1024]{1,0:T(8,128)(2,1)} %first_ref.1, bf16[1024,1024]{1,0:T(8,128)(2,1)} %weight_ref.4), custom_call_target="tpu_custom_call" | custom-call | bytes 1048576 | tf_op jit(solution)/shard_map/time_embedding/pallas_call | solution.py:75
  92.0 50.9 %head_pass.1 = (f32[4,16,256]{2,1,0:T(8,128)}, bf16[3,1024,1024]{2,1,0:T(8,128)(2,1)}, bf16[1024,2048]{1,0:T(8,128)(2,1)}, bf16[1024,1024]{1,0:T(8,128)(2,1)}, b...) custom-call(bf16[256,896]{1,0:T(8,128)(2,1)} %bitcast.278, ...), custom_call_target="tpu_custom_call" | custom-call | bytes 1048576 | tf_op jit(solution)/shard_map/head_pass/pallas_call | solution.py:215
  143.0 16.1 %time_back.1.first_ref = bf16[1024,1024]{1,0:T(8,128)(2,1)} custom-call(bf16[1024,1024]{1,0:T(8,128)(2,1)} %get-tuple-element.188.grad_ref.timed_ref, bf16[1024,1024]{1,0:T(8,128)(2,1)} %weight_ref.4, bf16[1024,1024]{1,0:T(8,128)(2,1)} %get-tuple-element.189.slope_ref), custom_call_target="tpu_custom_call" | custom-call | bytes 1048576 | tf_op jit(solution)/shard_map/time_back/pallas_call | solution.py:353
  159.0 10.9 %head_grads_one.2 = (bf16[4,1024,512]{2,1,0:T(8,128)(2,1)}, f32[8,128]{1,0:T(8,128)}) custom-call(s32[3]{0:T(128)} %copy-done.32, bf16[3,1024,1024]{2,1,0:T(8,128)(2,1)} %get-tuple-element.200.left_ref.acted_ref, bf16[1024,2048]{1,0:T(8,128)(2,1)} %get-tuple-element.191.fin_ref, bf16[1024,1024]{1,0:T(8,128)(2,1)} %get-tuple-element.192.branch_ref, ...), custom_call_target="tpu_custom_call" | custom-call | bytes 1048576 | tf_op jit(solution)/shard_map/head_grads_one/pallas_call | solution.py:324
  170.0 4.9 %all-to-all-start.1 = ((bf16[8,32,768]{2,1,0:T(8,128)(2,1)}), bf16[8,32,768]{2,1,0:T(8,128)(2,1)S(1)}, u32[]{:S(2)}, u32[]{:S(2)}) async-start(bf16[8,32,768]{2,1,0:T(8,128)(2,1)} %bitcast.11), calls=%async_computation.1 | async-start | bytes 786432 | tf_op jit(solution)/shard_map/all_to_all | solution.py:1338
  174.9 13.7 %head_grads_two.2 = (bf16[10,1024,256]{2,1,0:T(8,128)(2,1)}, f32[8,128]{1,0:T(8,128)}) custom-call(s32[3]{0:T(128)} %copy-done.32, bf16[3,1024,1024]{2,1,0:T(8,128)(2,1)} %get-tuple-element.200.left_ref.acted_ref, bf16[1024,1024]{1,0:T(8,128)(2,1)} %get-tuple-element.207.low_ref, bf16[1024,3072]{1,0:T(8,128)(2,1)} %get-tuple-element.196.mod_ref, ...), custom_call_target="tpu_custom_call" | custom-call | bytes 1048576 | tf_op jit(solution)/shard_map/head_grads_two/pallas_call | solution.py:448
  189.2 11.1 %head_grads_one.3 = (bf16[2,1024,512]{2,1,0:T(8,128)(2,1)}, bf16[2,1024,512]{2,1,0:T(8,128)(2,1)}, f32[8,128]{1,0:T(8,128)}) custom-call(s32[3]{0:T(128)} %copy-done.30, bf16[3,1024,1024]{2,1,0:T(8,128)(2,1)} %get-tuple-element.200.left_ref.acted_ref, bf16[1024,2048]{1,0:T(8,128)(2,1)} %get-tuple-element.191.fin_ref, ...), custom_call_target="tpu_custom_call" | custom-call | flops 1099511627776 | bytes 1048576 | tf_op jit(solution)/shard_map/head_grads_one/pallas_call | solution.py:324
  200.9 15.9 %head_grads_two.3 = (bf16[2,1024,256]{2,1,0:T(8,128)(2,1)}, bf16[2,1024,256]{2,1,0:T(8,128)(2,1)}, bf16[6,512,256]{2,1,0:T(8,128)(2,1)}, bf16[6,512,256]{2,1,0:T(8,128)(2,1)}, f32[8,128]{1,0:T(8,128)}) custom-call(s32[3]{0:T(128)} %copy-done.30, bf16[3,1024,1024]{2,1,0:T(8,128)(2,1)} %get-tuple-element.200.left_ref.acted_ref, ...), custom_call_target="tpu_custom_call" | custom-call | flops 1099511627776 | bytes 1048576 | tf_op jit(solution)/shard_map/head_grads_two/pallas_call | solution.py:448
  216.8 21.6 %feed_back.1 = (bf16[1088,768]{1,0:T(8,128)(2,1)}, bf16[1088,3072]{1,0:T(8,128)(2,1)}, f32[1088,768]{1,0:T(8,128)}, bf16[1088,768]{1,0:T(8,128)(2,1)}, bf16[1088...) custom-call(s32[4]{0:T(128)} %pad_add_fusion.at_ref, s32[32]{0:T(128)} %bucket_ref.13, ...), custom_call_target="tpu_custom_call" | custom-call | bytes 1048576 | tf_op jit(solution)/shard_map/feed_back/pallas_call | solution.py:823
  241.7 14.1 %feed_grads.2 = (bf16[2,768,768]{2,1,0:T(8,128)(2,1)}, bf16[2,768,768]{2,1,0:T(8,128)(2,1)}, f32[8,128]{1,0:T(8,128)}) custom-call(s32[3]{0:T(128)} %copy-done.32, bf16[1088,768]{1,0:T(8,128)(2,1)} %get-tuple-element.229.second_ref, bf16[1088,3072]{1,0:T(8,128)(2,1)} %get-tuple-element.216.hidden_ref, bf16[1088,3072]{1,0:T(8,128)(2,1)} %get-tuple-element.217.active_ref, ...), custom_call_target="tpu_custom_call" | custom-call | bytes 1048576 | tf_op jit(solution)/shard_map/feed_grads/pallas_call | solution.py:904
  259.3 15.7 %attend_back.3.a_ref = bf16[3,1088,256]{2,1,0:T(8,128)(2,1)} custom-call(s32[4]{0:T(128)} %pad_add_fusion.at_ref, s32[32]{0:T(128)} %bucket_ref.13, bf16[1088,2304]{1,0:T(8,128)(2,1)} %get-tuple-element.174.q_ref.k_ref.v_ref, bf16[1088,2304]{1,0:T(8,128)(2,1)} %get-tuple-element.174.q_ref.k_ref.v_ref, ...), custom_call_target="tpu_custom_call" | custom-call | flops 1099511627776 | bytes 1048576 | tf_op jit(solution)/shard_map/attend_back/pallas_call | solution.py:539
  284.1 15.8 %feed_grads.3 = (bf16[1,768,768]{2,1,0:T(8,128)(2,1)}, bf16[1,768,768]{2,1,0:T(8,128)(2,1)}, bf16[2,384,768]{2,1,0:T(8,128)(2,1)}, bf16[2,384,768]{2,1,0:T(8,128)(2,1)}, f32[8,128]{1,0:T(8,128)}) custom-call(s32[3]{0:T(128)} %copy-done.30, bf16[1088,768]{1,0:T(8,128)(2,1)} %get-tuple-element.229.second_ref, ...), custom_call_target="tpu_custom_call" | custom-call | flops 1099511627776 | bytes 1048576 | tf_op jit(solution)/shard_map/feed_grads/pallas_call | solution.py:904
  307.1 15.7 %attend_back.4.b_ref = bf16[3,1088,256]{2,1,0:T(8,128)(2,1)} custom-call(s32[4]{0:T(128)} %pad_add_fusion.at_ref, s32[32]{0:T(128)} %bucket_ref.13, bf16[1088,2304]{1,0:T(8,128)(2,1)} %get-tuple-element.174.q_ref.k_ref.v_ref, bf16[1088,2304]{1,0:T(8,128)(2,1)} %get-tuple-element.174.q_ref.k_ref.v_ref, ...), custom_call_target="tpu_custom_call" | custom-call | flops 1099511627776 | bytes 1048576 | tf_op jit(solution)/shard_map/attend_back/pallas_call | solution.py:539
  333.1 10.4 %collective-permute-start.11 = (bf16[2,128,512]{2,1,0:T(8,128)(2,1)}, bf16[2,128,512]{2,1,0:T(8,128)(2,1)}, u32[]{:S(2)}, u32[]{:S(2)}) collective-permute-start(bf16[2,128,512]{2,1,0:T(8,128)(2,1)} %fusion.21), channel_id=1, source_target_pairs={{0,8},{4,12},{8,0},{12,4},{16,24},{20,28},{24,16},{28,20},{1,9},{5... | collective-permute-start | bytes 786440 | tf_op jit(solution)/shard_map/ppermute | solution.py:1083
  349.6 15.8 %attend_back.5.c_ref = bf16[3,1088,256]{2,1,0:T(8,128)(2,1)} custom-call(s32[4]{0:T(128)} %pad_add_fusion.at_ref, s32[32]{0:T(128)} %bucket_ref.13, bf16[1088,2304]{1,0:T(8,128)(2,1)} %get-tuple-element.174.q_ref.k_ref.v_ref, bf16[1088,2304]{1,0:T(8,128)(2,1)} %get-tuple-element.174.q_ref.k_ref.v_ref, ...), custom_call_target="tpu_custom_call" | custom-call | flops 1099511627776 | bytes 1048576 | tf_op jit(solution)/shard_map/attend_back/pallas_call | solution.py:539
  371.9 12.9 %last_grads.1 = (bf16[12,768,128]{2,1,0:T(8,128)(2,1)}, bf16[12,768,128]{2,1,0:T(8,128)(2,1)}, f32[8,128]{1,0:T(8,128)}) custom-call(s32[3]{0:T(128)} %copy-done.30, bf16[1088,768]{1,0:T(8,128)(2,1)} %get-tuple-element.251.first_ref, bf16[1088,768]{1,0:T(8,128)(2,1)} %get-tuple-element.175.mixed_ref.o_ref, bf16[3,1088,256]{2,1,0:T(8,128)(2,1)} %attend_back.3.a_ref, ...), custom_call_target="tpu_custom_call" | custom-call | bytes 1048576 | tf_op jit(solution)/shard_map/last_grads/pallas_call | solution.py:964
  402.5 10.5 %tokens_back.1 = (f32[1088,768]{1,0:T(8,128)}, f32[8,384]{1,0:T(8,128)}) custom-call(bf16[1088,768]{1,0:T(8,128)(2,1)} %tokens_ref.4, bf16[3,1088,256]{2,1,0:T(8,128)(2,1)} %attend_back.3.a_ref, bf16[3,1088,256]{2,1,0:T(8,128)(2,1)} %attend_back.4.b_ref, bf16[3,1088,256]{2,1,0:T(8,128)(2,1)} %attend_back.5.c_ref, f32[1088,768]{1,0:T(8,128)} %get-tuple-element.258.middle_ref, ...), custom_call_target="tpu_custom_call" | custom-call | bytes 1048576 | tf_op jit(solution)/shard_map/tokens_back/pallas_call | solution.py:1022
  421.5 4.6 collective-permute-done.18
  436.5 3.4 collective-permute-start.27
  469.4 3.1 unpack.6
  (218 shorter events, 130.8 us)
Async XLA Ops:
  70.6 20.6 %all-to-all-start = ((bf16[8,32,896]{2,1,0:T(8,128)(2,1)}), bf16[8,32,896]{2,1,0:T(8,128)(2,1)S(1)}, u32[]{:S(2)}, u32[]{:S(2)}) async-start(bf16[8,32,896]{2,1,0:T(8,128)(2,1)} %bitcast.302), calls=%async_computation | async-start | bytes 917504 | tf_op jit(solution)/shard_map/all_to_all | solution.py:1338
  170.0 19.2 %collective-permute-start = (bf16[4,1024,512]{2,1,0:T(8,128)(2,1)}, bf16[4,1024,512]{2,1,0:T(8,128)(2,1)}, u32[]{:S(2)}, u32[]{:S(2)}) collective-permute-start(bf16[4,1024,512]{2,1,0:T(8,128)(2,1)} %get-tuple-element.201), channel_id=1, source_target_pairs={{0,1},{1,0},{2,3},{3,2},{4,5},{5,4},{6,7},{7,6},{8,9},{9,8},{10,11... | collective-permute-start | bytes 12582920 | tf_op jit(solution)/shard_map/ppermute | solution.py:1083
  170.0 19.2 %all-to-all-start.1 = ((bf16[8,32,768]{2,1,0:T(8,128)(2,1)}), bf16[8,32,768]{2,1,0:T(8,128)(2,1)S(1)}, u32[]{:S(2)}, u32[]{:S(2)}) async-start(bf16[8,32,768]{2,1,0:T(8,128)(2,1)} %bitcast.11), calls=%async_computation.1 | async-start | bytes 786432 | tf_op jit(solution)/shard_map/all_to_all | solution.py:1338
  200.3 56.2 %collective-permute-start.1 = (bf16[2,1024,512]{2,1,0:T(8,128)(2,1)}, bf16[2,1024,512]{2,1,0:T(8,128)(2,1)}, u32[]{:S(2)}, u32[]{:S(2)}) collective-permute-start(bf16[2,1024,512]{2,1,0:T(8,128)(2,1)} %get-tuple-element.204), channel_id=1, source_target_pairs={{0,2},{1,3},{2,0},{3,1},{4,6},{5,7},{6,4},{7,5},{8,10},{9,11},{10,... | collective-permute-start | bytes 6291464 | tf_op jit(solution)/shard_map/ppermute | solution.py:1083
  238.5 36.5 %collective-permute-start.4 = (bf16[2,1024,256]{2,1,0:T(8,128)(2,1)}, bf16[2,1024,256]{2,1,0:T(8,128)(2,1)}, u32[]{:S(2)}, u32[]{:S(2)}) collective-permute-start(bf16[2,1024,256]{2,1,0:T(8,128)(2,1)} %get-tuple-element.222), channel_id=1, source_target_pairs={{0,2},{1,3},{2,0},{3,1},{4,6},{5,7},{6,4},{7,5},{8,10},{9,11},{10,... | collective-permute-start | bytes 3145736 | tf_op jit(solution)/shard_map/ppermute | solution.py:1083
  240.0 37.6 %collective-permute-start.5 = (bf16[6,512,256]{2,1,0:T(8,128)(2,1)}, bf16[6,512,256]{2,1,0:T(8,128)(2,1)}, u32[]{:S(2)}, u32[]{:S(2)}) collective-permute-start(bf16[6,512,256]{2,1,0:T(8,128)(2,1)} %get-tuple-element.223), channel_id=1, source_target_pairs={{0,4},{4,0},{8,12},{12,8},{16,20},{20,16},{24,28},{28,24},{1,5},{5... | collective-permute-start | bytes 4718600 | tf_op jit(solution)/shard_map/ppermute | solution.py:1083
  255.9 28.2 %collective-permute-start.6 = (bf16[2,768,768]{2,1,0:T(8,128)(2,1)}, bf16[2,768,768]{2,1,0:T(8,128)(2,1)}, u32[]{:S(2)}, u32[]{:S(2)}) collective-permute-start(bf16[2,768,768]{2,1,0:T(8,128)(2,1)} %get-tuple-element.230), channel_id=1, source_target_pairs={{0,1},{1,0},{2,3},{3,2},{4,5},{5,4},{6,7},{7,6},{8,9},{9,8},{10,11... | collective-permute-start | bytes 7077896 | tf_op jit(solution)/shard_map/ppermute | solution.py:1083
  256.0 28.1 %collective-permute-start.7 = (bf16[2,768,768]{2,1,0:T(8,128)(2,1)}, bf16[2,768,768]{2,1,0:T(8,128)(2,1)}, u32[]{:S(2)}, u32[]{:S(2)}) collective-permute-start(bf16[2,768,768]{2,1,0:T(8,128)(2,1)} %get-tuple-element.231), channel_id=1, source_target_pairs={{0,1},{1,0},{2,3},{3,2},{4,5},{5,4},{6,7},{7,6},{8,9},{9,8},{10,11... | collective-permute-start | bytes 7077896 | tf_op jit(solution)/shard_map/ppermute | solution.py:1083
  259.0 41.1 %collective-permute-start.3 = (bf16[2,2,2,128,512]{4,3,0,2,1:T(8,128)(2,1)}, bf16[2,2,2,128,512]{4,3,0,2,1:T(8,128)(2,1)}, u32[]{:S(2)}, u32[]{:S(2)}) collective-permute-start(bf16[2,2,2,128,512]{4,3,0,2,1:T(8,128)(2,1)} %fusion), channel_id=1, source_target_pairs={{0,4},{4,0},{8,12},{12,8},{16,20},{20,16},{24,28},{28,24},{1,5},{5... | collective-permute-start | bytes 3145736 | tf_op jit(solution)/shard_map/ppermute | solution.py:1083
  279.6 43.2 %collective-permute-start.9 = (bf16[2,2,2,128,256]{4,3,0,2,1:T(8,128)(2,1)}, bf16[2,2,2,128,256]{4,3,0,2,1:T(8,128)(2,1)}, u32[]{:S(2)}, u32[]{:S(2)}) collective-permute-start(bf16[2,2,2,128,256]{4,3,0,2,1:T(8,128)(2,1)} %fusion.20), channel_id=1, source_target_pairs={{0,4},{4,0},{8,12},{12,8},{16,20},{20,16},{24,28},{28,24},{1,5},{5... | collective-permute-start | bytes 1572872 | tf_op jit(solution)/shard_map/ppermute | solution.py:1083
  283.5 39.3 %collective-permute-start.10 = (bf16[3,2,2,128,256]{4,3,0,2,1:T(8,128)(2,1)}, bf16[3,2,2,128,256]{4,3,0,2,1:T(8,128)(2,1)}, u32[]{:S(2)}, u32[]{:S(2)}) collective-permute-start(bf16[3,2,2,128,256]{4,3,0,2,1:T(8,128)(2,1)} %fusion.2), channel_id=1, source_target_pairs={{0,2},{1,3},{2,0},{3,1},{4,6},{5,7},{6,4},{7,5},{8,10},{9,11},{10,... | collective-permute-start | bytes 2359304 | tf_op jit(solution)/shard_map/ppermute | solution.py:1083
  302.4 28.6 %collective-permute-start.8 = (bf16[2,2,128,512]{3,2,0,1:T(8,128)(2,1)}, bf16[2,2,128,512]{3,2,0,1:T(8,128)(2,1)}, u32[]{:S(2)}, u32[]{:S(2)}) collective-permute-start(bf16[2,2,128,512]{3,2,0,1:T(8,128)(2,1)} %fusion.1), channel_id=1, source_target_pairs={{0,16},{4,20},{8,24},{12,28},{16,0},{20,4},{24,8},{28,12},{1,17},{... | collective-permute-start | bytes 1572872 | tf_op jit(solution)/shard_map/ppermute | solution.py:1083
  305.1 38.4 %collective-permute-start.13 = (bf16[1,768,768]{2,1,0:T(8,128)(2,1)}, bf16[1,768,768]{2,1,0:T(8,128)(2,1)}, u32[]{:S(2)}, u32[]{:S(2)}) collective-permute-start(bf16[1,768,768]{2,1,0:T(8,128)(2,1)} %get-tuple-element.241), channel_id=1, source_target_pairs={{0,2},{1,3},{2,0},{3,1},{4,6},{5,7},{6,4},{7,5},{8,10},{9,11},{10,... | collective-permute-start | bytes 3538952 | tf_op jit(solution)/shard_map/ppermute | solution.py:1083
  306.1 37.4 %collective-permute-start.14 = (bf16[2,384,768]{2,1,0:T(8,128)(2,1)}, bf16[2,384,768]{2,1,0:T(8,128)(2,1)}, u32[]{:S(2)}, u32[]{:S(2)}) collective-permute-start(bf16[2,384,768]{2,1,0:T(8,128)(2,1)} %get-tuple-element.242), channel_id=1, source_target_pairs={{0,4},{4,0},{8,12},{12,8},{16,20},{20,16},{24,28},{28,24},{1,5},{5... | collective-permute-start | bytes 3538952 | tf_op jit(solution)/shard_map/ppermute | solution.py:1083
  326.2 41.9 %collective-permute-start.12 = (bf16[5,2,128,256]{3,2,0,1:T(8,128)(2,1)}, bf16[5,2,128,256]{3,2,0,1:T(8,128)(2,1)}, u32[]{:S(2)}, u32[]{:S(2)}) collective-permute-start(bf16[5,2,128,256]{3,2,0,1:T(8,128)(2,1)} %pad_maximum_fusion), channel_id=1, source_target_pairs={{0,16},{4,20},{8,24},{12,28},{16,0},{20,4},{24,8},{28,12},{1,17},{... | collective-permute-start | bytes 1966088 | tf_op jit(solution)/shard_map/ppermute | solution.py:1083
  333.1 36.7 %collective-permute-start.11 = (bf16[2,128,512]{2,1,0:T(8,128)(2,1)}, bf16[2,128,512]{2,1,0:T(8,128)(2,1)}, u32[]{:S(2)}, u32[]{:S(2)}) collective-permute-start(bf16[2,128,512]{2,1,0:T(8,128)(2,1)} %fusion.21), channel_id=1, source_target_pairs={{0,8},{4,12},{8,0},{12,4},{16,24},{20,28},{24,16},{28,20},{1,9},{5... | collective-permute-start | bytes 786440 | tf_op jit(solution)/shard_map/ppermute | solution.py:1083
  345.5 19.9 %collective-permute-start.15 = (bf16[1,2,2,96,768]{4,3,2,1,0:T(8,128)(2,1)}, bf16[1,2,2,96,768]{4,3,2,1,0:T(8,128)(2,1)}, u32[]{:S(2)}, u32[]{:S(2)}) collective-permute-start(bf16[1,2,2,96,768]{4,3,2,1,0:T(8,128)(2,1)} %fusion.7), channel_id=1, source_target_pairs={{0,4},{4,0},{8,12},{12,8},{16,20},{20,16},{24,28},{28,24},{1,5},{5... | collective-permute-start | bytes 1769480 | tf_op jit(solution)/shard_map/ppermute | solution.py:1083
  391.0 22.0 %collective-permute-start.20 = (bf16[3,2,2,2,96,128]{5,4,0,3,2,1:T(8,128)(2,1)}, bf16[3,2,2,2,96,128]{5,4,0,3,2,1:T(8,128)(2,1)}, u32[]{:S(2)}, u32[]{:S(2)}) collective-permute-start(bf16[3,2,2,2,96,128]{5,4,0,3,2,1:T(8,128)(2,1)} %fusion.9), channel_id=1, source_target_pairs={{0,2},{1,3},{2,0},{3,1},{4,6},{5,7},{6,4},{7,5},{8,10},{9,11},{10,... | collective-permute-start | bytes 1769480 | tf_op jit(solution)/shard_map/ppermute | solution.py:1083
  393.4 19.6 %collective-permute-start.21 = (bf16[2,3,2,2,96,128]{5,4,1,3,2,0:T(8,128)(2,1)}, bf16[2,3,2,2,96,128]{5,4,1,3,2,0:T(8,128)(2,1)}, u32[]{:S(2)}, u32[]{:S(2)}) collective-permute-start(bf16[2,3,2,2,96,128]{5,4,1,3,2,0:T(8,128)(2,1)} %fusion.10), channel_id=1, source_target_pairs={{0,4},{4,0},{8,12},{12,8},{16,20},{20,16},{24,28},{28,24},{1,5},{5... | collective-permute-start | bytes 1769480 | tf_op jit(solution)/shard_map/ppermute | solution.py:1083
  395.9 23.7 %collective-permute-start.19 = (bf16[5,128,256]{2,1,0:T(8,128)(2,1)}, bf16[5,128,256]{2,1,0:T(8,128)(2,1)}, u32[]{:S(2)}, u32[]{:S(2)}) collective-permute-start(bf16[5,128,256]{2,1,0:T(8,128)(2,1)} %fusion.4), channel_id=1, source_target_pairs={{0,8},{4,12},{8,0},{12,4},{16,24},{20,28},{24,16},{28,20},{1,9},{5... | collective-permute-start | bytes 983048 | tf_op jit(solution)/shard_map/ppermute | solution.py:1083
  397.4 30.4 %collective-permute-start.22 = (bf16[2,128,512]{2,1,0:T(8,128)(2,1)}, bf16[2,128,512]{2,1,0:T(8,128)(2,1)}, u32[]{:S(2)}, u32[]{:S(2)}) collective-permute-start(bf16[2,128,512]{2,1,0:T(8,128)(2,1)} %fusion.23.refs_0_), channel_id=1, source_target_pairs={{0,2},{1,3},{2,0},{3,1},{4,6},{5,7},{6,4},{7,5},{8,10},{9,11},{10,... | collective-permute-start | bytes 786440 | tf_op jit(solution)/shard_map/ppermute | solution.py:1083
  397.4 28.7 %collective-permute-start.18 = (bf16[2,2,96,768]{3,2,0,1:T(8,128)(2,1)}, bf16[2,2,96,768]{3,2,0,1:T(8,128)(2,1)}, u32[]{:S(2)}, u32[]{:S(2)}) collective-permute-start(bf16[2,2,96,768]{3,2,0,1:T(8,128)(2,1)} %copy.86), channel_id=1, source_target_pairs={{0,16},{4,20},{8,24},{12,28},{16,0},{20,4},{24,8},{28,12},{1,17},{... | collective-permute-start | bytes 1769480 | tf_op jit(solution)/shard_map/ppermute | solution.py:1083
  428.4 17.6 %collective-permute-start.30 = (bf16[2,96,768]{2,1,0:T(8,128)(2,1)}, bf16[2,96,768]{2,1,0:T(8,128)(2,1)}, u32[]{:S(2)}, u32[]{:S(2)}) collective-permute-start(bf16[2,96,768]{2,1,0:T(8,128)(2,1)} %fusion.11), channel_id=1, source_target_pairs={{0,8},{4,12},{8,0},{12,4},{16,24},{20,28},{24,16},{28,20},{1,9},{5... | collective-permute-start | bytes 884744 | tf_op jit(solution)/shard_map/ppermute | solution.py:1083
  435.8 19.1 %collective-permute-start.26 = (bf16[8,32,384]{2,1,0:T(8,128)(2,1)}, bf16[8,32,384]{2,1,0:T(8,128)(2,1)}, u32[]{:S(2)}, u32[]{:S(2)}) collective-permute-start(bf16[8,32,384]{2,1,0:T(8,128)(2,1)} %add_convert_fusion.8), channel_id=1, source_target_pairs={{0,2},{1,3},{2,0},{3,1},{4,6},{5,7},{6,4},{7,5},{8,10},{9,11},{10,... | collective-permute-start | bytes 589832 | tf_op jit(solution)/shard_map/ppermute | solution.py:1083
  (56 other events, 500.2 us)

commit v2 on v1

--- a/solution.py
+++ b/solution.py
@@ -555,7 +555,7 @@
     return pl.BlockSpec(memory_space=pltpu.SMEM)
 
 
-def place_kernel(wide, at_ref, bucket_ref, start_ref, chosen_ref, spot_ref, live_ref):
+def place_kernel(wide, at_ref, bucket_ref, start_ref, chosen_ref, latent_ref, spot_ref, live_ref, dealt_ref):
     image, place_wide, place_narrow, narrow = at_ref[0], at_ref[1], at_ref[2], at_ref[3]
     seq = chosen_ref.shape[1]
     slots = live_ref.shape[1]
@@ -574,7 +574,9 @@
     target = ((start_ref[image] + order) & (wide - 1)) * deep + (order >> shift)
     target = jnp.where(is_chosen, target, -1)
     slot = lax.broadcasted_iota(jnp.int32, (seq, slots), 1)
-    spot_ref[...] = (slot == target).astype(jnp.float32).astype(jnp.bfloat16)
+    spot = (slot == target).astype(jnp.float32).astype(jnp.bfloat16)
+    spot_ref[...] = spot
+    dealt_ref[...] = nn(latent_ref[...], spot).T.astype(jnp.bfloat16)
     lane = lax.broadcasted_iota(jnp.int32, (1, slots), 1)
     live = jnp.zeros((1, slots), jnp.float32)
     for source in range(wide):
@@ -587,21 +589,26 @@
     live_ref[...] = live
 
 
-def places(at, bucket, deal_start, masked, wide):
+def places(at, bucket, deal_start, masked, latents, wide):
     seq = masked.shape[1]
     return pl.pallas_call(
         partial(place_kernel, wide),
-        in_specs=[smem(), smem(), smem(), whole_block((1, seq))],
-        out_specs=[whole_block((seq, MASK_MAX)), whole_block((1, MASK_MAX))],
+        in_specs=[smem(), smem(), smem(), whole_block((1, seq)), whole_block((TOKEN_DIM, seq))],
+        out_specs=[
+            whole_block((seq, MASK_MAX)),
+            whole_block((1, MASK_MAX)),
+            whole_block((MASK_MAX, TOKEN_DIM)),
+        ],
         grid=(1,),
         out_shape=[
             jax.ShapeDtypeStruct((seq, MASK_MAX), jnp.bfloat16),
             jax.ShapeDtypeStruct((1, MASK_MAX), jnp.float32),
+            jax.ShapeDtypeStruct((MASK_MAX, TOKEN_DIM), jnp.bfloat16),
         ],
         compiler_params=pltpu.CompilerParams(vmem_limit_bytes=VMEM),
         cost_estimate=OTHER,
         name="places",
-    )(at, bucket, deal_start, masked)
+    )(at, bucket, deal_start, masked, latents)
 
 
 def joint_kernel(tokens_ref, gain_ref, shift_ref, weight_ref, bias_ref, first_ref, joint_ref):
@@ -716,10 +723,10 @@
     spread_scratch[1:2, :] += jnp.sum(keep * feed * feed, axis=0, keepdims=True)
     spot = spot_ref[...]
     dealt_scratch[:, :D] += tn(spot, output)
-    dealt_scratch[:, D : D + TOKEN_DIM] += tn(spot, latent_ref[...])
 
     @pl.when(step == pl.num_programs(0) - 1)
     def _():
+        dealt_scratch[:, D : D + TOKEN_DIM] = latent_ref[...].astype(jnp.float32)
         dealt_ref[...] = dealt_scratch[...].astype(jnp.bfloat16)
         count = (BUFFER + bucket_ref[at_ref[0]]).astype(jnp.float32) * D
         total = jnp.sum(spread_scratch[...], axis=1, keepdims=True)
@@ -735,7 +742,7 @@
     return pl.pallas_call(
         feed_kernel,
         grid=(seq // ROWS,),
-        in_specs=[smem(), smem(), by_block(D), by_block(D), by_block(TOKEN_DIM), by_block(slots)]
+        in_specs=[smem(), smem(), by_block(D), by_block(D), whole_block((slots, TOKEN_DIM)), by_block(slots)]
         + [whole_block(a.shape) for a in weights],
         out_specs=[
             by_block(D),
@@ -1297,7 +1304,7 @@
     image_index = place_wide * narrow + place_narrow
     at = jnp.stack([image_index, place_wide, place_narrow, jnp.int32(narrow)]).astype(jnp.int32)
 
-    spot, live = places(at, bucket, deal_start, masked, wide)
+    spot, live, dealt_latents = places(at, bucket, deal_start, masked, latents.T, wide)
     slots = spot.shape[1]
     steps = timesteps.astype(jnp.float32)
     half = time_first.shape[0] // 2
@@ -1319,7 +1326,7 @@
         bucket,
         mixed,
         tokens,
-        latents,
+        dealt_latents,
         spot,
         (
             output_weight,

time: 486 us -> 484 us (level)
  no operation moved by 1% of the time
where the time goes in v2:
time: 484 us; the launch traced here: 477 us
  Pallas kernels  329 us (68%)
  starting transfers between devices  63.1 us (13%)
  other arithmetic  56.1 us (12%)
  waiting for transfers between devices  14.7 us (3%)
  local copies, waits for them, and re-layouts  13.3 us (3%)
    pallas_call x1, Pallas kernels, head_pass(): pl.pallas_call(head_kernel, grid=(REPEATS,), in_specs=[whole_block(dealt....  50.9 us
    ppermute x45, starting transfers between devices, swap(): return lax.ppermute(array, axis, [(i, i ^ mask) for i in range(count)])  50.9 us
    pallas_call x3, Pallas kernels, attend_back(): pl.pallas_call(partial(attend_back_kernel, KB), grid=(count,), in_specs=[...  47.2 us
    pallas_call x2, Pallas kernels, feed_grads(): pl.pallas_call(partial(feed_grads_kernel, wide), grid_spec=pltpu.Prefetch...  30 us
    pallas_call x1, Pallas kernels, feed_pass(): pl.pallas_call(feed_kernel, grid=(seq // ROWS,), in_specs=[smem(), smem()...  29.9 us
    pallas_call x2, Pallas kernels, head_grads_two(): pl.pallas_call(partial(head_grads_two_kernel, wide), grid_spec=pltpu.Pref...  29.6 us
    pallas_call x1, Pallas kernels, attend(): pl.pallas_call(partial(attend_kernel, QB), grid=(PAIRS,), in_specs=[smem(...  26.1 us
    pallas_call x2, Pallas kernels, head_grads_one(): pl.pallas_call(head_grads_one_kernel, grid_spec=pltpu.PrefetchScalarGridS...  22 us
  transfers between devices with their start and end apart: 47, of which 7 were waited for; matrix products, arithmetic and copies ran while one was open for 13% of the time, Pallas kernels for 35%

profile of v2, /device:TPU:0, one launch (start us, length us, event | category | flops | bytes accessed | tf_op | source)
XLA Modules:
  0.0 477.5 jit_solution(16440380062115953611)
XLA Ops:
  1.3 8.8 %joint_pass.1 = (bf16[1088,768]{1,0:T(8,128)(2,1)}, bf16[1088,2304]{1,0:T(8,128)(2,1)}) custom-call(bf16[1088,768]{1,0:T(8,128)(2,1)} %tokens_ref.4, f32[768]{0:T(1024)} %gain_ref.7, f32[768]{0:T(1024)} %shift_ref.2, bf16[768,2304]{1,0:T(8,128)(2,1)} %weight_ref.5, f32[1536]{0:T(1024)} %bias_ref.1), custom_call_target="tpu_custom_call" | custom-call | bytes 1048576 | tf_op jit(solution)/shard_map/joint_pass/pallas_call | solution.py:638
  10.1 26.1 %attend.1 = (bf16[1088,768]{1,0:T(8,128)(2,1)}, f32[1088,768]{1,0:T(8,128)}) custom-call(s32[4]{0:T(128)} %pad_add_fusion.at_ref, s32[32]{0:T(128)} %bucket_ref.13, bf16[1088,2304]{1,0:T(8,128)(2,1)} %get-tuple-element.175.q_ref.k_ref.v_ref, bf16[1088,2304]{1,0:T(8,128)(2,1)} %get-tuple-element.175.q_ref.k_ref.v_ref, ...), custom_call_target="tpu_custom_call" | custom-call | bytes 1048576 | tf_op jit(solution)/shard_map/attend/pallas_call | solution.py:498
  39.1 29.9 %feed_pass.1 = (bf16[1088,768]{1,0:T(8,128)(2,1)}, f32[1088,768]{1,0:T(8,128)}, bf16[1088,768]{1,0:T(8,128)(2,1)}, bf16[1088,3072]{1,0:T(8,128)(2,1)}, bf16[1088...) custom-call(s32[4]{0:T(128)} %pad_add_fusion.at_ref, s32[32]{0:T(128)} %bucket_ref.13, ...), custom_call_target="tpu_custom_call" | custom-call | bytes 1048576 | tf_op jit(solution)/shard_map/feed_pass/pallas_call | solution.py:742
  69.0 7.3 %all-to-all-start = ((bf16[8,32,896]{2,1,0:T(8,128)(2,1)}), bf16[8,32,896]{2,1,0:T(8,128)(2,1)S(1)}, u32[]{:S(2)}, u32[]{:S(2)}) async-start(bf16[8,32,896]{2,1,0:T(8,128)(2,1)} %bitcast.303), calls=%async_computation | async-start | bytes 917504 | tf_op jit(solution)/shard_map/all_to_all | solution.py:1345
  80.8 7.4 %time_embedding.1 = (bf16[1024,1024]{1,0:T(8,128)(2,1)}, bf16[1024,1024]{1,0:T(8,128)(2,1)}, f32[1024,1024]{1,0:T(8,128)}) custom-call(bf16[1024,256]{1,0:T(8,128)(2,1)} %pad_maximum_fusion.2.sinus_ref, bf16[256,1024]{1,0:T(8,128)(2,1)} %first_ref.1, bf16[1024,1024]{1,0:T(8,128)(2,1)} %weight_ref.4), custom_call_target="tpu_custom_call" | custom-call | bytes 1048576 | tf_op jit(solution)/shard_map/time_embedding/pallas_call | solution.py:75
  90.1 50.9 %head_pass.1 = (f32[4,16,256]{2,1,0:T(8,128)}, bf16[3,1024,1024]{2,1,0:T(8,128)(2,1)}, bf16[1024,2048]{1,0:T(8,128)(2,1)}, bf16[1024,1024]{1,0:T(8,128)(2,1)}, b...) custom-call(bf16[256,896]{1,0:T(8,128)(2,1)} %bitcast.279, ...), custom_call_target="tpu_custom_call" | custom-call | bytes 1048576 | tf_op jit(solution)/shard_map/head_pass/pallas_call | solution.py:215
  141.0 16.1 %time_back.1.first_ref = bf16[1024,1024]{1,0:T(8,128)(2,1)} custom-call(bf16[1024,1024]{1,0:T(8,128)(2,1)} %get-tuple-element.190.grad_ref.timed_ref, bf16[1024,1024]{1,0:T(8,128)(2,1)} %weight_ref.4, bf16[1024,1024]{1,0:T(8,128)(2,1)} %get-tuple-element.191.slope_ref), custom_call_target="tpu_custom_call" | custom-call | bytes 1048576 | tf_op jit(solution)/shard_map/time_back/pallas_call | solution.py:353
  157.1 10.9 %head_grads_one.2 = (bf16[4,1024,512]{2,1,0:T(8,128)(2,1)}, f32[8,128]{1,0:T(8,128)}) custom-call(s32[3]{0:T(128)} %copy-done.32, bf16[3,1024,1024]{2,1,0:T(8,128)(2,1)} %get-tuple-element.202.left_ref.acted_ref, bf16[1024,2048]{1,0:T(8,128)(2,1)} %get-tuple-element.193.fin_ref, bf16[1024,1024]{1,0:T(8,128)(2,1)} %get-tuple-element.194.branch_ref, ...), custom_call_target="tpu_custom_call" | custom-call | bytes 1048576 | tf_op jit(solution)/shard_map/head_grads_one/pallas_call | solution.py:324
  168.0 4.9 %all-to-all-start.1 = ((bf16[8,32,768]{2,1,0:T(8,128)(2,1)}), bf16[8,32,768]{2,1,0:T(8,128)(2,1)S(1)}, u32[]{:S(2)}, u32[]{:S(2)}) async-start(bf16[8,32,768]{2,1,0:T(8,128)(2,1)} %bitcast.12), calls=%async_computation.1 | async-start | bytes 786432 | tf_op jit(solution)/shard_map/all_to_all | solution.py:1345
  173.0 13.7 %head_grads_two.2 = (bf16[10,1024,256]{2,1,0:T(8,128)(2,1)}, f32[8,128]{1,0:T(8,128)}) custom-call(s32[3]{0:T(128)} %copy-done.32, bf16[3,1024,1024]{2,1,0:T(8,128)(2,1)} %get-tuple-element.202.left_ref.acted_ref, bf16[1024,1024]{1,0:T(8,128)(2,1)} %get-tuple-element.209.low_ref, bf16[1024,3072]{1,0:T(8,128)(2,1)} %get-tuple-element.198.mod_ref, ...), custom_call_target="tpu_custom_call" | custom-call | bytes 1048576 | tf_op jit(solution)/shard_map/head_grads_two/pallas_call | solution.py:448
  187.3 11.1 %head_grads_one.3 = (bf16[2,1024,512]{2,1,0:T(8,128)(2,1)}, bf16[2,1024,512]{2,1,0:T(8,128)(2,1)}, f32[8,128]{1,0:T(8,128)}) custom-call(s32[3]{0:T(128)} %copy-done.30, bf16[3,1024,1024]{2,1,0:T(8,128)(2,1)} %get-tuple-element.202.left_ref.acted_ref, bf16[1024,2048]{1,0:T(8,128)(2,1)} %get-tuple-element.193.fin_ref, ...), custom_call_target="tpu_custom_call" | custom-call | flops 1099511627776 | bytes 1048576 | tf_op jit(solution)/shard_map/head_grads_one/pallas_call | solution.py:324
  199.0 15.9 %head_grads_two.3 = (bf16[2,1024,256]{2,1,0:T(8,128)(2,1)}, bf16[2,1024,256]{2,1,0:T(8,128)(2,1)}, bf16[6,512,256]{2,1,0:T(8,128)(2,1)}, bf16[6,512,256]{2,1,0:T(8,128)(2,1)}, f32[8,128]{1,0:T(8,128)}) custom-call(s32[3]{0:T(128)} %copy-done.30, bf16[3,1024,1024]{2,1,0:T(8,128)(2,1)} %get-tuple-element.202.left_ref.acted_ref, ...), custom_call_target="tpu_custom_call" | custom-call | flops 1099511627776 | bytes 1048576 | tf_op jit(solution)/shard_map/head_grads_two/pallas_call | solution.py:448
  214.9 21.6 %feed_back.1 = (bf16[1088,768]{1,0:T(8,128)(2,1)}, bf16[1088,3072]{1,0:T(8,128)(2,1)}, f32[1088,768]{1,0:T(8,128)}, bf16[1088,768]{1,0:T(8,128)(2,1)}, bf16[1088...) custom-call(s32[4]{0:T(128)} %pad_add_fusion.at_ref, s32[32]{0:T(128)} %bucket_ref.13, ...), custom_call_target="tpu_custom_call" | custom-call | bytes 1048576 | tf_op jit(solution)/shard_map/feed_back/pallas_call | solution.py:830
  239.8 14.1 %feed_grads.2 = (bf16[2,768,768]{2,1,0:T(8,128)(2,1)}, bf16[2,768,768]{2,1,0:T(8,128)(2,1)}, f32[8,128]{1,0:T(8,128)}) custom-call(s32[3]{0:T(128)} %copy-done.32, bf16[1088,768]{1,0:T(8,128)(2,1)} %get-tuple-element.231.second_ref, bf16[1088,3072]{1,0:T(8,128)(2,1)} %get-tuple-element.218.hidden_ref, bf16[1088,3072]{1,0:T(8,128)(2,1)} %get-tuple-element.219.active_ref, ...), custom_call_target="tpu_custom_call" | custom-call | bytes 1048576 | tf_op jit(solution)/shard_map/feed_grads/pallas_call | solution.py:911
  257.4 15.7 %attend_back.3.a_ref = bf16[3,1088,256]{2,1,0:T(8,128)(2,1)} custom-call(s32[4]{0:T(128)} %pad_add_fusion.at_ref, s32[32]{0:T(128)} %bucket_ref.13, bf16[1088,2304]{1,0:T(8,128)(2,1)} %get-tuple-element.175.q_ref.k_ref.v_ref, bf16[1088,2304]{1,0:T(8,128)(2,1)} %get-tuple-element.175.q_ref.k_ref.v_ref, ...), custom_call_target="tpu_custom_call" | custom-call | flops 1099511627776 | bytes 1048576 | tf_op jit(solution)/shard_map/attend_back/pallas_call | solution.py:539
  282.1 15.8 %feed_grads.3 = (bf16[1,768,768]{2,1,0:T(8,128)(2,1)}, bf16[1,768,768]{2,1,0:T(8,128)(2,1)}, bf16[2,384,768]{2,1,0:T(8,128)(2,1)}, bf16[2,384,768]{2,1,0:T(8,128)(2,1)}, f32[8,128]{1,0:T(8,128)}) custom-call(s32[3]{0:T(128)} %copy-done.30, bf16[1088,768]{1,0:T(8,128)(2,1)} %get-tuple-element.231.second_ref, ...), custom_call_target="tpu_custom_call" | custom-call | flops 1099511627776 | bytes 1048576 | tf_op jit(solution)/shard_map/feed_grads/pallas_call | solution.py:911
  305.1 15.7 %attend_back.4.b_ref = bf16[3,1088,256]{2,1,0:T(8,128)(2,1)} custom-call(s32[4]{0:T(128)} %pad_add_fusion.at_ref, s32[32]{0:T(128)} %bucket_ref.13, bf16[1088,2304]{1,0:T(8,128)(2,1)} %get-tuple-element.175.q_ref.k_ref.v_ref, bf16[1088,2304]{1,0:T(8,128)(2,1)} %get-tuple-element.175.q_ref.k_ref.v_ref, ...), custom_call_target="tpu_custom_call" | custom-call | flops 1099511627776 | bytes 1048576 | tf_op jit(solution)/shard_map/attend_back/pallas_call | solution.py:539
  331.2 10.4 %collective-permute-start.11 = (bf16[2,128,512]{2,1,0:T(8,128)(2,1)}, bf16[2,128,512]{2,1,0:T(8,128)(2,1)}, u32[]{:S(2)}, u32[]{:S(2)}) collective-permute-start(bf16[2,128,512]{2,1,0:T(8,128)(2,1)} %fusion.21), channel_id=1, source_target_pairs={{0,8},{4,12},{8,0},{12,4},{16,24},{20,28},{24,16},{28,20},{1,9},{5... | collective-permute-start | bytes 786440 | tf_op jit(solution)/shard_map/ppermute | solution.py:1090
  347.7 15.8 %attend_back.5.c_ref = bf16[3,1088,256]{2,1,0:T(8,128)(2,1)} custom-call(s32[4]{0:T(128)} %pad_add_fusion.at_ref, s32[32]{0:T(128)} %bucket_ref.13, bf16[1088,2304]{1,0:T(8,128)(2,1)} %get-tuple-element.175.q_ref.k_ref.v_ref, bf16[1088,2304]{1,0:T(8,128)(2,1)} %get-tuple-element.175.q_ref.k_ref.v_ref, ...), custom_call_target="tpu_custom_call" | custom-call | flops 1099511627776 | bytes 1048576 | tf_op jit(solution)/shard_map/attend_back/pallas_call | solution.py:539
  370.0 12.9 %last_grads.1 = (bf16[12,768,128]{2,1,0:T(8,128)(2,1)}, bf16[12,768,128]{2,1,0:T(8,128)(2,1)}, f32[8,128]{1,0:T(8,128)}) custom-call(s32[3]{0:T(128)} %copy-done.30, bf16[1088,768]{1,0:T(8,128)(2,1)} %get-tuple-element.253.first_ref, bf16[1088,768]{1,0:T(8,128)(2,1)} %get-tuple-element.176.mixed_ref.o_ref, bf16[3,1088,256]{2,1,0:T(8,128)(2,1)} %attend_back.3.a_ref, ...), custom_call_target="tpu_custom_call" | custom-call | bytes 1048576 | tf_op jit(solution)/shard_map/last_grads/pallas_call | solution.py:971
  400.6 10.5 %tokens_back.1 = (f32[1088,768]{1,0:T(8,128)}, f32[8,384]{1,0:T(8,128)}) custom-call(bf16[1088,768]{1,0:T(8,128)(2,1)} %tokens_ref.4, bf16[3,1088,256]{2,1,0:T(8,128)(2,1)} %attend_back.3.a_ref, bf16[3,1088,256]{2,1,0:T(8,128)(2,1)} %attend_back.4.b_ref, bf16[3,1088,256]{2,1,0:T(8,128)(2,1)} %attend_back.5.c_ref, f32[1088,768]{1,0:T(8,128)} %get-tuple-element.260.middle_ref, ...), custom_call_target="tpu_custom_call" | custom-call | bytes 1048576 | tf_op jit(solution)/shard_map/tokens_back/pallas_call | solution.py:1029
  419.6 4.6 collective-permute-done.18
  434.6 3.4 collective-permute-start.27
  467.5 3.1 unpack.6
  (217 shorter events, 129.5 us)
Async XLA Ops:
  69.0 20.4 %all-to-all-start = ((bf16[8,32,896]{2,1,0:T(8,128)(2,1)}), bf16[8,32,896]{2,1,0:T(8,128)(2,1)S(1)}, u32[]{:S(2)}, u32[]{:S(2)}) async-start(bf16[8,32,896]{2,1,0:T(8,128)(2,1)} %bitcast.303), calls=%async_computation | async-start | bytes 917504 | tf_op jit(solution)/shard_map/all_to_all | solution.py:1345
  168.0 19.3 %collective-permute-start = (bf16[4,1024,512]{2,1,0:T(8,128)(2,1)}, bf16[4,1024,512]{2,1,0:T(8,128)(2,1)}, u32[]{:S(2)}, u32[]{:S(2)}) collective-permute-start(bf16[4,1024,512]{2,1,0:T(8,128)(2,1)} %get-tuple-element.203), channel_id=1, source_target_pairs={{0,1},{1,0},{2,3},{3,2},{4,5},{5,4},{6,7},{7,6},{8,9},{9,8},{10,11... | collective-permute-start | bytes 12582920 | tf_op jit(solution)/shard_map/ppermute | solution.py:1090
  168.0 19.2 %all-to-all-start.1 = ((bf16[8,32,768]{2,1,0:T(8,128)(2,1)}), bf16[8,32,768]{2,1,0:T(8,128)(2,1)S(1)}, u32[]{:S(2)}, u32[]{:S(2)}) async-start(bf16[8,32,768]{2,1,0:T(8,128)(2,1)} %bitcast.12), calls=%async_computation.1 | async-start | bytes 786432 | tf_op jit(solution)/shard_map/all_to_all | solution.py:1345
  198.4 56.2 %collective-permute-start.1 = (bf16[2,1024,512]{2,1,0:T(8,128)(2,1)}, bf16[2,1024,512]{2,1,0:T(8,128)(2,1)}, u32[]{:S(2)}, u32[]{:S(2)}) collective-permute-start(bf16[2,1024,512]{2,1,0:T(8,128)(2,1)} %get-tuple-element.206), channel_id=1, source_target_pairs={{0,2},{1,3},{2,0},{3,1},{4,6},{5,7},{6,4},{7,5},{8,10},{9,11},{10,... | collective-permute-start | bytes 6291464 | tf_op jit(solution)/shard_map/ppermute | solution.py:1090
  236.5 36.5 %collective-permute-start.4 = (bf16[2,1024,256]{2,1,0:T(8,128)(2,1)}, bf16[2,1024,256]{2,1,0:T(8,128)(2,1)}, u32[]{:S(2)}, u32[]{:S(2)}) collective-permute-start(bf16[2,1024,256]{2,1,0:T(8,128)(2,1)} %get-tuple-element.224), channel_id=1, source_target_pairs={{0,2},{1,3},{2,0},{3,1},{4,6},{5,7},{6,4},{7,5},{8,10},{9,11},{10,... | collective-permute-start | bytes 3145736 | tf_op jit(solution)/shard_map/ppermute | solution.py:1090
  238.1 37.6 %collective-permute-start.5 = (bf16[6,512,256]{2,1,0:T(8,128)(2,1)}, bf16[6,512,256]{2,1,0:T(8,128)(2,1)}, u32[]{:S(2)}, u32[]{:S(2)}) collective-permute-start(bf16[6,512,256]{2,1,0:T(8,128)(2,1)} %get-tuple-element.225), channel_id=1, source_target_pairs={{0,4},{4,0},{8,12},{12,8},{16,20},{20,16},{24,28},{28,24},{1,5},{5... | collective-permute-start | bytes 4718600 | tf_op jit(solution)/shard_map/ppermute | solution.py:1090
  254.0 28.2 %collective-permute-start.6 = (bf16[2,768,768]{2,1,0:T(8,128)(2,1)}, bf16[2,768,768]{2,1,0:T(8,128)(2,1)}, u32[]{:S(2)}, u32[]{:S(2)}) collective-permute-start(bf16[2,768,768]{2,1,0:T(8,128)(2,1)} %get-tuple-element.232), channel_id=1, source_target_pairs={{0,1},{1,0},{2,3},{3,2},{4,5},{5,4},{6,7},{7,6},{8,9},{9,8},{10,11... | collective-permute-start | bytes 7077896 | tf_op jit(solution)/shard_map/ppermute | solution.py:1090
  254.0 28.1 %collective-permute-start.7 = (bf16[2,768,768]{2,1,0:T(8,128)(2,1)}, bf16[2,768,768]{2,1,0:T(8,128)(2,1)}, u32[]{:S(2)}, u32[]{:S(2)}) collective-permute-start(bf16[2,768,768]{2,1,0:T(8,128)(2,1)} %get-tuple-element.233), channel_id=1, source_target_pairs={{0,1},{1,0},{2,3},{3,2},{4,5},{5,4},{6,7},{7,6},{8,9},{9,8},{10,11... | collective-permute-start | bytes 7077896 | tf_op jit(solution)/shard_map/ppermute | solution.py:1090
  257.1 41.1 %collective-permute-start.3 = (bf16[2,2,2,128,512]{4,3,0,2,1:T(8,128)(2,1)}, bf16[2,2,2,128,512]{4,3,0,2,1:T(8,128)(2,1)}, u32[]{:S(2)}, u32[]{:S(2)}) collective-permute-start(bf16[2,2,2,128,512]{4,3,0,2,1:T(8,128)(2,1)} %fusion), channel_id=1, source_target_pairs={{0,4},{4,0},{8,12},{12,8},{16,20},{20,16},{24,28},{28,24},{1,5},{5... | collective-permute-start | bytes 3145736 | tf_op jit(solution)/shard_map/ppermute | solution.py:1090
  277.6 43.2 %collective-permute-start.9 = (bf16[2,2,2,128,256]{4,3,0,2,1:T(8,128)(2,1)}, bf16[2,2,2,128,256]{4,3,0,2,1:T(8,128)(2,1)}, u32[]{:S(2)}, u32[]{:S(2)}) collective-permute-start(bf16[2,2,2,128,256]{4,3,0,2,1:T(8,128)(2,1)} %fusion.20), channel_id=1, source_target_pairs={{0,4},{4,0},{8,12},{12,8},{16,20},{20,16},{24,28},{28,24},{1,5},{5... | collective-permute-start | bytes 1572872 | tf_op jit(solution)/shard_map/ppermute | solution.py:1090
  281.6 39.2 %collective-permute-start.10 = (bf16[3,2,2,128,256]{4,3,0,2,1:T(8,128)(2,1)}, bf16[3,2,2,128,256]{4,3,0,2,1:T(8,128)(2,1)}, u32[]{:S(2)}, u32[]{:S(2)}) collective-permute-start(bf16[3,2,2,128,256]{4,3,0,2,1:T(8,128)(2,1)} %fusion.2), channel_id=1, source_target_pairs={{0,2},{1,3},{2,0},{3,1},{4,6},{5,7},{6,4},{7,5},{8,10},{9,11},{10,... | collective-permute-start | bytes 2359304 | tf_op jit(solution)/shard_map/ppermute | solution.py:1090
  300.5 28.6 %collective-permute-start.8 = (bf16[2,2,128,512]{3,2,0,1:T(8,128)(2,1)}, bf16[2,2,128,512]{3,2,0,1:T(8,128)(2,1)}, u32[]{:S(2)}, u32[]{:S(2)}) collective-permute-start(bf16[2,2,128,512]{3,2,0,1:T(8,128)(2,1)} %fusion.1), channel_id=1, source_target_pairs={{0,16},{4,20},{8,24},{12,28},{16,0},{20,4},{24,8},{28,12},{1,17},{... | collective-permute-start | bytes 1572872 | tf_op jit(solution)/shard_map/ppermute | solution.py:1090
  303.1 38.4 %collective-permute-start.13 = (bf16[1,768,768]{2,1,0:T(8,128)(2,1)}, bf16[1,768,768]{2,1,0:T(8,128)(2,1)}, u32[]{:S(2)}, u32[]{:S(2)}) collective-permute-start(bf16[1,768,768]{2,1,0:T(8,128)(2,1)} %get-tuple-element.243), channel_id=1, source_target_pairs={{0,2},{1,3},{2,0},{3,1},{4,6},{5,7},{6,4},{7,5},{8,10},{9,11},{10,... | collective-permute-start | bytes 3538952 | tf_op jit(solution)/shard_map/ppermute | solution.py:1090
  304.2 37.4 %collective-permute-start.14 = (bf16[2,384,768]{2,1,0:T(8,128)(2,1)}, bf16[2,384,768]{2,1,0:T(8,128)(2,1)}, u32[]{:S(2)}, u32[]{:S(2)}) collective-permute-start(bf16[2,384,768]{2,1,0:T(8,128)(2,1)} %get-tuple-element.244), channel_id=1, source_target_pairs={{0,4},{4,0},{8,12},{12,8},{16,20},{20,16},{24,28},{28,24},{1,5},{5... | collective-permute-start | bytes 3538952 | tf_op jit(solution)/shard_map/ppermute | solution.py:1090
  324.2 41.9 %collective-permute-start.12 = (bf16[5,2,128,256]{3,2,0,1:T(8,128)(2,1)}, bf16[5,2,128,256]{3,2,0,1:T(8,128)(2,1)}, u32[]{:S(2)}, u32[]{:S(2)}) collective-permute-start(bf16[5,2,128,256]{3,2,0,1:T(8,128)(2,1)} %pad_maximum_fusion), channel_id=1, source_target_pairs={{0,16},{4,20},{8,24},{12,28},{16,0},{20,4},{24,8},{28,12},{1,17},{... | collective-permute-start | bytes 1966088 | tf_op jit(solution)/shard_map/ppermute | solution.py:1090
  331.2 36.7 %collective-permute-start.11 = (bf16[2,128,512]{2,1,0:T(8,128)(2,1)}, bf16[2,128,512]{2,1,0:T(8,128)(2,1)}, u32[]{:S(2)}, u32[]{:S(2)}) collective-permute-start(bf16[2,128,512]{2,1,0:T(8,128)(2,1)} %fusion.21), channel_id=1, source_target_pairs={{0,8},{4,12},{8,0},{12,4},{16,24},{20,28},{24,16},{28,20},{1,9},{5... | collective-permute-start | bytes 786440 | tf_op jit(solution)/shard_map/ppermute | solution.py:1090
  343.6 19.9 %collective-permute-start.15 = (bf16[1,2,2,96,768]{4,3,2,1,0:T(8,128)(2,1)}, bf16[1,2,2,96,768]{4,3,2,1,0:T(8,128)(2,1)}, u32[]{:S(2)}, u32[]{:S(2)}) collective-permute-start(bf16[1,2,2,96,768]{4,3,2,1,0:T(8,128)(2,1)} %fusion.7), channel_id=1, source_target_pairs={{0,4},{4,0},{8,12},{12,8},{16,20},{20,16},{24,28},{28,24},{1,5},{5... | collective-permute-start | bytes 1769480 | tf_op jit(solution)/shard_map/ppermute | solution.py:1090
  389.1 22.0 %collective-permute-start.20 = (bf16[3,2,2,2,96,128]{5,4,0,3,2,1:T(8,128)(2,1)}, bf16[3,2,2,2,96,128]{5,4,0,3,2,1:T(8,128)(2,1)}, u32[]{:S(2)}, u32[]{:S(2)}) collective-permute-start(bf16[3,2,2,2,96,128]{5,4,0,3,2,1:T(8,128)(2,1)} %fusion.9), channel_id=1, source_target_pairs={{0,2},{1,3},{2,0},{3,1},{4,6},{5,7},{6,4},{7,5},{8,10},{9,11},{10,... | collective-permute-start | bytes 1769480 | tf_op jit(solution)/shard_map/ppermute | solution.py:1090
  391.5 19.6 %collective-permute-start.21 = (bf16[2,3,2,2,96,128]{5,4,1,3,2,0:T(8,128)(2,1)}, bf16[2,3,2,2,96,128]{5,4,1,3,2,0:T(8,128)(2,1)}, u32[]{:S(2)}, u32[]{:S(2)}) collective-permute-start(bf16[2,3,2,2,96,128]{5,4,1,3,2,0:T(8,128)(2,1)} %fusion.10), channel_id=1, source_target_pairs={{0,4},{4,0},{8,12},{12,8},{16,20},{20,16},{24,28},{28,24},{1,5},{5... | collective-permute-start | bytes 1769480 | tf_op jit(solution)/shard_map/ppermute | solution.py:1090
  394.0 23.7 %collective-permute-start.19 = (bf16[5,128,256]{2,1,0:T(8,128)(2,1)}, bf16[5,128,256]{2,1,0:T(8,128)(2,1)}, u32[]{:S(2)}, u32[]{:S(2)}) collective-permute-start(bf16[5,128,256]{2,1,0:T(8,128)(2,1)} %fusion.4), channel_id=1, source_target_pairs={{0,8},{4,12},{8,0},{12,4},{16,24},{20,28},{24,16},{28,20},{1,9},{5... | collective-permute-start | bytes 983048 | tf_op jit(solution)/shard_map/ppermute | solution.py:1090
  395.5 30.4 %collective-permute-start.22 = (bf16[2,128,512]{2,1,0:T(8,128)(2,1)}, bf16[2,128,512]{2,1,0:T(8,128)(2,1)}, u32[]{:S(2)}, u32[]{:S(2)}) collective-permute-start(bf16[2,128,512]{2,1,0:T(8,128)(2,1)} %fusion.23.refs_0_), channel_id=1, source_target_pairs={{0,2},{1,3},{2,0},{3,1},{4,6},{5,7},{6,4},{7,5},{8,10},{9,11},{10,... | collective-permute-start | bytes 786440 | tf_op jit(solution)/shard_map/ppermute | solution.py:1090
  395.5 28.7 %collective-permute-start.18 = (bf16[2,2,96,768]{3,2,0,1:T(8,128)(2,1)}, bf16[2,2,96,768]{3,2,0,1:T(8,128)(2,1)}, u32[]{:S(2)}, u32[]{:S(2)}) collective-permute-start(bf16[2,2,96,768]{3,2,0,1:T(8,128)(2,1)} %copy.84), channel_id=1, source_target_pairs={{0,16},{4,20},{8,24},{12,28},{16,0},{20,4},{24,8},{28,12},{1,17},{... | collective-permute-start | bytes 1769480 | tf_op jit(solution)/shard_map/ppermute | solution.py:1090
  426.4 17.7 %collective-permute-start.30 = (bf16[2,96,768]{2,1,0:T(8,128)(2,1)}, bf16[2,96,768]{2,1,0:T(8,128)(2,1)}, u32[]{:S(2)}, u32[]{:S(2)}) collective-permute-start(bf16[2,96,768]{2,1,0:T(8,128)(2,1)} %fusion.11), channel_id=1, source_target_pairs={{0,8},{4,12},{8,0},{12,4},{16,24},{20,28},{24,16},{28,20},{1,9},{5... | collective-permute-start | bytes 884744 | tf_op jit(solution)/shard_map/ppermute | solution.py:1090
  433.9 19.1 %collective-permute-start.26 = (bf16[8,32,384]{2,1,0:T(8,128)(2,1)}, bf16[8,32,384]{2,1,0:T(8,128)(2,1)}, u32[]{:S(2)}, u32[]{:S(2)}) collective-permute-start(bf16[8,32,384]{2,1,0:T(8,128)(2,1)} %add_convert_fusion.8), channel_id=1, source_target_pairs={{0,2},{1,3},{2,0},{3,1},{4,6},{5,7},{6,4},{7,5},{8,10},{9,11},{10,... | collective-permute-start | bytes 589832 | tf_op jit(solution)/shard_map/ppermute | solution.py:1090
  (56 other events, 499.5 us)

commit v3 on v2

--- a/solution.py
+++ b/solution.py
@@ -135,7 +135,7 @@
     left_ref[0] = acted.T
     start = dealt_ref[:, D:].astype(jnp.float32).T[:TOKEN_DIM]
     noise = noise_ref[0]
-    noisy = (keep_ref[0] * start + drop_ref[0] * noise).astype(jnp.bfloat16)
+    noisy = (keep_ref[pl.ds(turn, 1), :] * start + drop_ref[pl.ds(turn, 1), :] * noise).astype(jnp.bfloat16)
     entry = tn(noisy, input_ref[...])
     inner_normed, inner_inverse = normalize(entry)
     shift_a = nn(acted, mod_ref[:, :width])
@@ -218,8 +218,8 @@
         in_specs=[
             whole_block(dealt.shape),
             by_rows(width),
-            by_turn((1, slots)),
-            by_turn((1, slots)),
+            whole_block(keep_sig.shape),
+            whole_block(drop_sig.shape),
             by_turn((TOKEN_DIM, slots)),
         ]
         + [whole_block(a.shape) for a in operands[5:]],
@@ -1363,8 +1363,8 @@
     ) = head_pass(
         dealt,
         timed,
-        keep_sig[:, None, :],
-        drop_sig[:, None, :],
+        keep_sig,
+        drop_sig,
         added_noise,
         live,
         (input_turned, cond_proj, block_mod, block_expand, block_reduce, final_mod, final_turned),

time: 484 us -> 483 us (level)
  no operation moved by 1% of the time
where the time goes in v3:
time: 483 us; the launch traced here: 477 us
  Pallas kernels  329 us (68%)
  starting transfers between devices  62.6 us (13%)
  other arithmetic  56.7 us (12%)
  waiting for transfers between devices  15.3 us (3%)
  local copies, waits for them, and re-layouts  12.1 us (3%)
    ppermute x45, starting transfers between devices, swap(): return lax.ppermute(array, axis, [(i, i ^ mask) for i in range(count)])  50.9 us
    pallas_call x1, Pallas kernels, head_pass(): pl.pallas_call(head_kernel, grid=(REPEATS,), in_specs=[whole_block(dealt....  50.9 us
    pallas_call x3, Pallas kernels, attend_back(): pl.pallas_call(partial(attend_back_kernel, KB), grid=(count,), in_specs=[...  47.2 us
    pallas_call x2, Pallas kernels, feed_grads(): pl.pallas_call(partial(feed_grads_kernel, wide), grid_spec=pltpu.Prefetch...  30 us
    pallas_call x1, Pallas kernels, feed_pass(): pl.pallas_call(feed_kernel, grid=(seq // ROWS,), in_specs=[smem(), smem()...  29.9 us
    pallas_call x2, Pallas kernels, head_grads_two(): pl.pallas_call(partial(head_grads_two_kernel, wide), grid_spec=pltpu.Pref...  29.6 us
    pallas_call x1, Pallas kernels, attend(): pl.pallas_call(partial(attend_kernel, QB), grid=(PAIRS,), in_specs=[smem(...  26.1 us
    pallas_call x2, Pallas kernels, head_grads_one(): pl.pallas_call(head_grads_one_kernel, grid_spec=pltpu.PrefetchScalarGridS...  22 us
  transfers between devices with their start and end apart: 47, of which 7 were waited for; matrix products, arithmetic and copies ran while one was open for 13% of the time, Pallas kernels for 35%

profile of v3, /device:TPU:0, one launch (start us, length us, event | category | flops | bytes accessed | tf_op | source)
XLA Modules:
  0.0 476.9 jit_solution(859648355704215500)
XLA Ops:
  1.3 8.8 %joint_pass.1 = (bf16[1088,768]{1,0:T(8,128)(2,1)}, bf16[1088,2304]{1,0:T(8,128)(2,1)}) custom-call(bf16[1088,768]{1,0:T(8,128)(2,1)} %tokens_ref.4, f32[768]{0:T(1024)} %gain_ref.7, f32[768]{0:T(1024)} %shift_ref.2, bf16[768,2304]{1,0:T(8,128)(2,1)} %weight_ref.5, f32[1536]{0:T(1024)} %bias_ref.1), custom_call_target="tpu_custom_call" | custom-call | bytes 1048576 | tf_op jit(solution)/shard_map/joint_pass/pallas_call | solution.py:638
  10.1 26.1 %attend.1 = (bf16[1088,768]{1,0:T(8,128)(2,1)}, f32[1088,768]{1,0:T(8,128)}) custom-call(s32[4]{0:T(128)} %pad_add_fusion.at_ref, s32[32]{0:T(128)} %bucket_ref.13, bf16[1088,2304]{1,0:T(8,128)(2,1)} %get-tuple-element.175.q_ref.k_ref.v_ref, bf16[1088,2304]{1,0:T(8,128)(2,1)} %get-tuple-element.175.q_ref.k_ref.v_ref, ...), custom_call_target="tpu_custom_call" | custom-call | bytes 1048576 | tf_op jit(solution)/shard_map/attend/pallas_call | solution.py:498
  39.1 29.9 %feed_pass.1 = (bf16[1088,768]{1,0:T(8,128)(2,1)}, f32[1088,768]{1,0:T(8,128)}, bf16[1088,768]{1,0:T(8,128)(2,1)}, bf16[1088,3072]{1,0:T(8,128)(2,1)}, bf16[1088...) custom-call(s32[4]{0:T(128)} %pad_add_fusion.at_ref, s32[32]{0:T(128)} %bucket_ref.13, ...), custom_call_target="tpu_custom_call" | custom-call | bytes 1048576 | tf_op jit(solution)/shard_map/feed_pass/pallas_call | solution.py:742
  69.0 7.3 %all-to-all-start = ((bf16[8,32,896]{2,1,0:T(8,128)(2,1)}), bf16[8,32,896]{2,1,0:T(8,128)(2,1)S(1)}, u32[]{:S(2)}, u32[]{:S(2)}) async-start(bf16[8,32,896]{2,1,0:T(8,128)(2,1)} %bitcast.301), calls=%async_computation | async-start | bytes 917504 | tf_op jit(solution)/shard_map/all_to_all | solution.py:1345
  79.5 7.4 %time_embedding.1 = (bf16[1024,1024]{1,0:T(8,128)(2,1)}, bf16[1024,1024]{1,0:T(8,128)(2,1)}, f32[1024,1024]{1,0:T(8,128)}) custom-call(bf16[1024,256]{1,0:T(8,128)(2,1)} %pad_maximum_fusion.2.sinus_ref, bf16[256,1024]{1,0:T(8,128)(2,1)} %first_ref.1, bf16[1024,1024]{1,0:T(8,128)(2,1)} %weight_ref.4), custom_call_target="tpu_custom_call" | custom-call | bytes 1048576 | tf_op jit(solution)/shard_map/time_embedding/pallas_call | solution.py:75
  90.1 50.9 %head_pass.1 = (f32[4,16,256]{2,1,0:T(8,128)}, bf16[3,1024,1024]{2,1,0:T(8,128)(2,1)}, bf16[1024,2048]{1,0:T(8,128)(2,1)}, bf16[1024,1024]{1,0:T(8,128)(2,1)}, b...) custom-call(bf16[256,896]{1,0:T(8,128)(2,1)} %bitcast.277, ...), custom_call_target="tpu_custom_call" | custom-call | bytes 1048576 | tf_op jit(solution)/shard_map/head_pass/pallas_call | solution.py:215
  141.0 16.1 %time_back.1.first_ref = bf16[1024,1024]{1,0:T(8,128)(2,1)} custom-call(bf16[1024,1024]{1,0:T(8,128)(2,1)} %get-tuple-element.190.grad_ref.timed_ref, bf16[1024,1024]{1,0:T(8,128)(2,1)} %weight_ref.4, bf16[1024,1024]{1,0:T(8,128)(2,1)} %get-tuple-element.191.slope_ref), custom_call_target="tpu_custom_call" | custom-call | bytes 1048576 | tf_op jit(solution)/shard_map/time_back/pallas_call | solution.py:353
  157.1 10.9 %head_grads_one.2 = (bf16[4,1024,512]{2,1,0:T(8,128)(2,1)}, f32[8,128]{1,0:T(8,128)}) custom-call(s32[3]{0:T(128)} %copy-done.32, bf16[3,1024,1024]{2,1,0:T(8,128)(2,1)} %get-tuple-element.202.left_ref.acted_ref, bf16[1024,2048]{1,0:T(8,128)(2,1)} %get-tuple-element.193.fin_ref, bf16[1024,1024]{1,0:T(8,128)(2,1)} %get-tuple-element.194.branch_ref, ...), custom_call_target="tpu_custom_call" | custom-call | bytes 1048576 | tf_op jit(solution)/shard_map/head_grads_one/pallas_call | solution.py:324
  168.0 4.4 all-to-all-start.1
  172.4 13.7 %head_grads_two.2 = (bf16[10,1024,256]{2,1,0:T(8,128)(2,1)}, f32[8,128]{1,0:T(8,128)}) custom-call(s32[3]{0:T(128)} %copy-done.32, bf16[3,1024,1024]{2,1,0:T(8,128)(2,1)} %get-tuple-element.202.left_ref.acted_ref, bf16[1024,1024]{1,0:T(8,128)(2,1)} %get-tuple-element.209.low_ref, bf16[1024,3072]{1,0:T(8,128)(2,1)} %get-tuple-element.198.mod_ref, ...), custom_call_target="tpu_custom_call" | custom-call | bytes 1048576 | tf_op jit(solution)/shard_map/head_grads_two/pallas_call | solution.py:448
  186.7 11.1 %head_grads_one.3 = (bf16[2,1024,512]{2,1,0:T(8,128)(2,1)}, bf16[2,1024,512]{2,1,0:T(8,128)(2,1)}, f32[8,128]{1,0:T(8,128)}) custom-call(s32[3]{0:T(128)} %copy-done.30, bf16[3,1024,1024]{2,1,0:T(8,128)(2,1)} %get-tuple-element.202.left_ref.acted_ref, bf16[1024,2048]{1,0:T(8,128)(2,1)} %get-tuple-element.193.fin_ref, ...), custom_call_target="tpu_custom_call" | custom-call | flops 1099511627776 | bytes 1048576 | tf_op jit(solution)/shard_map/head_grads_one/pallas_call | solution.py:324
  198.4 15.9 %head_grads_two.3 = (bf16[2,1024,256]{2,1,0:T(8,128)(2,1)}, bf16[2,1024,256]{2,1,0:T(8,128)(2,1)}, bf16[6,512,256]{2,1,0:T(8,128)(2,1)}, bf16[6,512,256]{2,1,0:T(8,128)(2,1)}, f32[8,128]{1,0:T(8,128)}) custom-call(s32[3]{0:T(128)} %copy-done.30, bf16[3,1024,1024]{2,1,0:T(8,128)(2,1)} %get-tuple-element.202.left_ref.acted_ref, ...), custom_call_target="tpu_custom_call" | custom-call | flops 1099511627776 | bytes 1048576 | tf_op jit(solution)/shard_map/head_grads_two/pallas_call | solution.py:448
  214.3 21.6 %feed_back.1 = (bf16[1088,768]{1,0:T(8,128)(2,1)}, bf16[1088,3072]{1,0:T(8,128)(2,1)}, f32[1088,768]{1,0:T(8,128)}, bf16[1088,768]{1,0:T(8,128)(2,1)}, bf16[1088...) custom-call(s32[4]{0:T(128)} %pad_add_fusion.at_ref, s32[32]{0:T(128)} %bucket_ref.13, ...), custom_call_target="tpu_custom_call" | custom-call | bytes 1048576 | tf_op jit(solution)/shard_map/feed_back/pallas_call | solution.py:830
  239.2 14.1 %feed_grads.2 = (bf16[2,768,768]{2,1,0:T(8,128)(2,1)}, bf16[2,768,768]{2,1,0:T(8,128)(2,1)}, f32[8,128]{1,0:T(8,128)}) custom-call(s32[3]{0:T(128)} %copy-done.32, bf16[1088,768]{1,0:T(8,128)(2,1)} %get-tuple-element.231.second_ref, bf16[1088,3072]{1,0:T(8,128)(2,1)} %get-tuple-element.218.hidden_ref, bf16[1088,3072]{1,0:T(8,128)(2,1)} %get-tuple-element.219.active_ref, ...), custom_call_target="tpu_custom_call" | custom-call | bytes 1048576 | tf_op jit(solution)/shard_map/feed_grads/pallas_call | solution.py:911
  256.8 15.7 %attend_back.3.a_ref = bf16[3,1088,256]{2,1,0:T(8,128)(2,1)} custom-call(s32[4]{0:T(128)} %pad_add_fusion.at_ref, s32[32]{0:T(128)} %bucket_ref.13, bf16[1088,2304]{1,0:T(8,128)(2,1)} %get-tuple-element.175.q_ref.k_ref.v_ref, bf16[1088,2304]{1,0:T(8,128)(2,1)} %get-tuple-element.175.q_ref.k_ref.v_ref, ...), custom_call_target="tpu_custom_call" | custom-call | flops 1099511627776 | bytes 1048576 | tf_op jit(solution)/shard_map/attend_back/pallas_call | solution.py:539
  281.5 15.8 %feed_grads.3 = (bf16[1,768,768]{2,1,0:T(8,128)(2,1)}, bf16[1,768,768]{2,1,0:T(8,128)(2,1)}, bf16[2,384,768]{2,1,0:T(8,128)(2,1)}, bf16[2,384,768]{2,1,0:T(8,128)(2,1)}, f32[8,128]{1,0:T(8,128)}) custom-call(s32[3]{0:T(128)} %copy-done.30, bf16[1088,768]{1,0:T(8,128)(2,1)} %get-tuple-element.231.second_ref, ...), custom_call_target="tpu_custom_call" | custom-call | flops 1099511627776 | bytes 1048576 | tf_op jit(solution)/shard_map/feed_grads/pallas_call | solution.py:911
  304.5 15.7 %attend_back.4.b_ref = bf16[3,1088,256]{2,1,0:T(8,128)(2,1)} custom-call(s32[4]{0:T(128)} %pad_add_fusion.at_ref, s32[32]{0:T(128)} %bucket_ref.13, bf16[1088,2304]{1,0:T(8,128)(2,1)} %get-tuple-element.175.q_ref.k_ref.v_ref, bf16[1088,2304]{1,0:T(8,128)(2,1)} %get-tuple-element.175.q_ref.k_ref.v_ref, ...), custom_call_target="tpu_custom_call" | custom-call | flops 1099511627776 | bytes 1048576 | tf_op jit(solution)/shard_map/attend_back/pallas_call | solution.py:539
  330.6 10.4 %collective-permute-start.11 = (bf16[2,128,512]{2,1,0:T(8,128)(2,1)}, bf16[2,128,512]{2,1,0:T(8,128)(2,1)}, u32[]{:S(2)}, u32[]{:S(2)}) collective-permute-start(bf16[2,128,512]{2,1,0:T(8,128)(2,1)} %fusion.21), channel_id=1, source_target_pairs={{0,8},{4,12},{8,0},{12,4},{16,24},{20,28},{24,16},{28,20},{1,9},{5... | collective-permute-start | bytes 786440 | tf_op jit(solution)/shard_map/ppermute | solution.py:1090
  347.1 15.8 %attend_back.5.c_ref = bf16[3,1088,256]{2,1,0:T(8,128)(2,1)} custom-call(s32[4]{0:T(128)} %pad_add_fusion.at_ref, s32[32]{0:T(128)} %bucket_ref.13, bf16[1088,2304]{1,0:T(8,128)(2,1)} %get-tuple-element.175.q_ref.k_ref.v_ref, bf16[1088,2304]{1,0:T(8,128)(2,1)} %get-tuple-element.175.q_ref.k_ref.v_ref, ...), custom_call_target="tpu_custom_call" | custom-call | flops 1099511627776 | bytes 1048576 | tf_op jit(solution)/shard_map/attend_back/pallas_call | solution.py:539
  369.4 12.9 %last_grads.1 = (bf16[12,768,128]{2,1,0:T(8,128)(2,1)}, bf16[12,768,128]{2,1,0:T(8,128)(2,1)}, f32[8,128]{1,0:T(8,128)}) custom-call(s32[3]{0:T(128)} %copy-done.30, bf16[1088,768]{1,0:T(8,128)(2,1)} %get-tuple-element.253.first_ref, bf16[1088,768]{1,0:T(8,128)(2,1)} %get-tuple-element.176.mixed_ref.o_ref, bf16[3,1088,256]{2,1,0:T(8,128)(2,1)} %attend_back.3.a_ref, ...), custom_call_target="tpu_custom_call" | custom-call | bytes 1048576 | tf_op jit(solution)/shard_map/last_grads/pallas_call | solution.py:971
  400.0 10.5 %tokens_back.1 = (f32[1088,768]{1,0:T(8,128)}, f32[8,384]{1,0:T(8,128)}) custom-call(bf16[1088,768]{1,0:T(8,128)(2,1)} %tokens_ref.4, bf16[3,1088,256]{2,1,0:T(8,128)(2,1)} %attend_back.3.a_ref, bf16[3,1088,256]{2,1,0:T(8,128)(2,1)} %attend_back.4.b_ref, bf16[3,1088,256]{2,1,0:T(8,128)(2,1)} %attend_back.5.c_ref, f32[1088,768]{1,0:T(8,128)} %get-tuple-element.260.middle_ref, ...), custom_call_target="tpu_custom_call" | custom-call | bytes 1048576 | tf_op jit(solution)/shard_map/tokens_back/pallas_call | solution.py:1029
  419.0 4.6 collective-permute-done.18
  434.0 3.4 collective-permute-start.27
  466.9 3.1 unpack.6
  (215 shorter events, 129.5 us)
Async XLA Ops:
  69.0 20.4 %all-to-all-start = ((bf16[8,32,896]{2,1,0:T(8,128)(2,1)}), bf16[8,32,896]{2,1,0:T(8,128)(2,1)S(1)}, u32[]{:S(2)}, u32[]{:S(2)}) async-start(bf16[8,32,896]{2,1,0:T(8,128)(2,1)} %bitcast.301), calls=%async_computation | async-start | bytes 917504 | tf_op jit(solution)/shard_map/all_to_all | solution.py:1345
  168.0 18.7 %collective-permute-start = (bf16[4,1024,512]{2,1,0:T(8,128)(2,1)}, bf16[4,1024,512]{2,1,0:T(8,128)(2,1)}, u32[]{:S(2)}, u32[]{:S(2)}) collective-permute-start(bf16[4,1024,512]{2,1,0:T(8,128)(2,1)} %get-tuple-element.203), channel_id=1, source_target_pairs={{0,1},{1,0},{2,3},{3,2},{4,5},{5,4},{6,7},{7,6},{8,9},{9,8},{10,11... | collective-permute-start | bytes 12582920 | tf_op jit(solution)/shard_map/ppermute | solution.py:1090
  168.0 18.7 %all-to-all-start.1 = ((bf16[8,32,768]{2,1,0:T(8,128)(2,1)}), bf16[8,32,768]{2,1,0:T(8,128)(2,1)S(1)}, u32[]{:S(2)}, u32[]{:S(2)}) async-start(bf16[8,32,768]{2,1,0:T(8,128)(2,1)} %bitcast.11), calls=%async_computation.1 | async-start | bytes 786432 | tf_op jit(solution)/shard_map/all_to_all | solution.py:1345
  197.8 56.2 %collective-permute-start.1 = (bf16[2,1024,512]{2,1,0:T(8,128)(2,1)}, bf16[2,1024,512]{2,1,0:T(8,128)(2,1)}, u32[]{:S(2)}, u32[]{:S(2)}) collective-permute-start(bf16[2,1024,512]{2,1,0:T(8,128)(2,1)} %get-tuple-element.206), channel_id=1, source_target_pairs={{0,2},{1,3},{2,0},{3,1},{4,6},{5,7},{6,4},{7,5},{8,10},{9,11},{10,... | collective-permute-start | bytes 6291464 | tf_op jit(solution)/shard_map/ppermute | solution.py:1090
  235.9 36.5 %collective-permute-start.4 = (bf16[2,1024,256]{2,1,0:T(8,128)(2,1)}, bf16[2,1024,256]{2,1,0:T(8,128)(2,1)}, u32[]{:S(2)}, u32[]{:S(2)}) collective-permute-start(bf16[2,1024,256]{2,1,0:T(8,128)(2,1)} %get-tuple-element.224), channel_id=1, source_target_pairs={{0,2},{1,3},{2,0},{3,1},{4,6},{5,7},{6,4},{7,5},{8,10},{9,11},{10,... | collective-permute-start | bytes 3145736 | tf_op jit(solution)/shard_map/ppermute | solution.py:1090
  237.5 37.6 %collective-permute-start.5 = (bf16[6,512,256]{2,1,0:T(8,128)(2,1)}, bf16[6,512,256]{2,1,0:T(8,128)(2,1)}, u32[]{:S(2)}, u32[]{:S(2)}) collective-permute-start(bf16[6,512,256]{2,1,0:T(8,128)(2,1)} %get-tuple-element.225), channel_id=1, source_target_pairs={{0,4},{4,0},{8,12},{12,8},{16,20},{20,16},{24,28},{28,24},{1,5},{5... | collective-permute-start | bytes 4718600 | tf_op jit(solution)/shard_map/ppermute | solution.py:1090
  253.4 28.2 %collective-permute-start.6 = (bf16[2,768,768]{2,1,0:T(8,128)(2,1)}, bf16[2,768,768]{2,1,0:T(8,128)(2,1)}, u32[]{:S(2)}, u32[]{:S(2)}) collective-permute-start(bf16[2,768,768]{2,1,0:T(8,128)(2,1)} %get-tuple-element.232), channel_id=1, source_target_pairs={{0,1},{1,0},{2,3},{3,2},{4,5},{5,4},{6,7},{7,6},{8,9},{9,8},{10,11... | collective-permute-start | bytes 7077896 | tf_op jit(solution)/shard_map/ppermute | solution.py:1090
  253.4 28.1 %collective-permute-start.7 = (bf16[2,768,768]{2,1,0:T(8,128)(2,1)}, bf16[2,768,768]{2,1,0:T(8,128)(2,1)}, u32[]{:S(2)}, u32[]{:S(2)}) collective-permute-start(bf16[2,768,768]{2,1,0:T(8,128)(2,1)} %get-tuple-element.233), channel_id=1, source_target_pairs={{0,1},{1,0},{2,3},{3,2},{4,5},{5,4},{6,7},{7,6},{8,9},{9,8},{10,11... | collective-permute-start | bytes 7077896 | tf_op jit(solution)/shard_map/ppermute | solution.py:1090
  256.5 41.1 %collective-permute-start.3 = (bf16[2,2,2,128,512]{4,3,0,2,1:T(8,128)(2,1)}, bf16[2,2,2,128,512]{4,3,0,2,1:T(8,128)(2,1)}, u32[]{:S(2)}, u32[]{:S(2)}) collective-permute-start(bf16[2,2,2,128,512]{4,3,0,2,1:T(8,128)(2,1)} %fusion), channel_id=1, source_target_pairs={{0,4},{4,0},{8,12},{12,8},{16,20},{20,16},{24,28},{28,24},{1,5},{5... | collective-permute-start | bytes 3145736 | tf_op jit(solution)/shard_map/ppermute | solution.py:1090
  277.1 43.2 %collective-permute-start.9 = (bf16[2,2,2,128,256]{4,3,0,2,1:T(8,128)(2,1)}, bf16[2,2,2,128,256]{4,3,0,2,1:T(8,128)(2,1)}, u32[]{:S(2)}, u32[]{:S(2)}) collective-permute-start(bf16[2,2,2,128,256]{4,3,0,2,1:T(8,128)(2,1)} %fusion.20), channel_id=1, source_target_pairs={{0,4},{4,0},{8,12},{12,8},{16,20},{20,16},{24,28},{28,24},{1,5},{5... | collective-permute-start | bytes 1572872 | tf_op jit(solution)/shard_map/ppermute | solution.py:1090
  281.0 39.2 %collective-permute-start.10 = (bf16[3,2,2,128,256]{4,3,0,2,1:T(8,128)(2,1)}, bf16[3,2,2,128,256]{4,3,0,2,1:T(8,128)(2,1)}, u32[]{:S(2)}, u32[]{:S(2)}) collective-permute-start(bf16[3,2,2,128,256]{4,3,0,2,1:T(8,128)(2,1)} %fusion.2), channel_id=1, source_target_pairs={{0,2},{1,3},{2,0},{3,1},{4,6},{5,7},{6,4},{7,5},{8,10},{9,11},{10,... | collective-permute-start | bytes 2359304 | tf_op jit(solution)/shard_map/ppermute | solution.py:1090
  299.9 28.6 %collective-permute-start.8 = (bf16[2,2,128,512]{3,2,0,1:T(8,128)(2,1)}, bf16[2,2,128,512]{3,2,0,1:T(8,128)(2,1)}, u32[]{:S(2)}, u32[]{:S(2)}) collective-permute-start(bf16[2,2,128,512]{3,2,0,1:T(8,128)(2,1)} %fusion.1), channel_id=1, source_target_pairs={{0,16},{4,20},{8,24},{12,28},{16,0},{20,4},{24,8},{28,12},{1,17},{... | collective-permute-start | bytes 1572872 | tf_op jit(solution)/shard_map/ppermute | solution.py:1090
  302.5 38.4 %collective-permute-start.13 = (bf16[1,768,768]{2,1,0:T(8,128)(2,1)}, bf16[1,768,768]{2,1,0:T(8,128)(2,1)}, u32[]{:S(2)}, u32[]{:S(2)}) collective-permute-start(bf16[1,768,768]{2,1,0:T(8,128)(2,1)} %get-tuple-element.243), channel_id=1, source_target_pairs={{0,2},{1,3},{2,0},{3,1},{4,6},{5,7},{6,4},{7,5},{8,10},{9,11},{10,... | collective-permute-start | bytes 3538952 | tf_op jit(solution)/shard_map/ppermute | solution.py:1090
  303.6 37.4 %collective-permute-start.14 = (bf16[2,384,768]{2,1,0:T(8,128)(2,1)}, bf16[2,384,768]{2,1,0:T(8,128)(2,1)}, u32[]{:S(2)}, u32[]{:S(2)}) collective-permute-start(bf16[2,384,768]{2,1,0:T(8,128)(2,1)} %get-tuple-element.244), channel_id=1, source_target_pairs={{0,4},{4,0},{8,12},{12,8},{16,20},{20,16},{24,28},{28,24},{1,5},{5... | collective-permute-start | bytes 3538952 | tf_op jit(solution)/shard_map/ppermute | solution.py:1090
  323.6 41.9 %collective-permute-start.12 = (bf16[5,2,128,256]{3,2,0,1:T(8,128)(2,1)}, bf16[5,2,128,256]{3,2,0,1:T(8,128)(2,1)}, u32[]{:S(2)}, u32[]{:S(2)}) collective-permute-start(bf16[5,2,128,256]{3,2,0,1:T(8,128)(2,1)} %pad_maximum_fusion), channel_id=1, source_target_pairs={{0,16},{4,20},{8,24},{12,28},{16,0},{20,4},{24,8},{28,12},{1,17},{... | collective-permute-start | bytes 1966088 | tf_op jit(solution)/shard_map/ppermute | solution.py:1090
  330.6 36.7 %collective-permute-start.11 = (bf16[2,128,512]{2,1,0:T(8,128)(2,1)}, bf16[2,128,512]{2,1,0:T(8,128)(2,1)}, u32[]{:S(2)}, u32[]{:S(2)}) collective-permute-start(bf16[2,128,512]{2,1,0:T(8,128)(2,1)} %fusion.21), channel_id=1, source_target_pairs={{0,8},{4,12},{8,0},{12,4},{16,24},{20,28},{24,16},{28,20},{1,9},{5... | collective-permute-start | bytes 786440 | tf_op jit(solution)/shard_map/ppermute | solution.py:1090
  343.0 19.9 %collective-permute-start.15 = (bf16[1,2,2,96,768]{4,3,2,1,0:T(8,128)(2,1)}, bf16[1,2,2,96,768]{4,3,2,1,0:T(8,128)(2,1)}, u32[]{:S(2)}, u32[]{:S(2)}) collective-permute-start(bf16[1,2,2,96,768]{4,3,2,1,0:T(8,128)(2,1)} %fusion.7), channel_id=1, source_target_pairs={{0,4},{4,0},{8,12},{12,8},{16,20},{20,16},{24,28},{28,24},{1,5},{5... | collective-permute-start | bytes 1769480 | tf_op jit(solution)/shard_map/ppermute | solution.py:1090
  388.5 22.0 %collective-permute-start.20 = (bf16[3,2,2,2,96,128]{5,4,0,3,2,1:T(8,128)(2,1)}, bf16[3,2,2,2,96,128]{5,4,0,3,2,1:T(8,128)(2,1)}, u32[]{:S(2)}, u32[]{:S(2)}) collective-permute-start(bf16[3,2,2,2,96,128]{5,4,0,3,2,1:T(8,128)(2,1)} %fusion.9), channel_id=1, source_target_pairs={{0,2},{1,3},{2,0},{3,1},{4,6},{5,7},{6,4},{7,5},{8,10},{9,11},{10,... | collective-permute-start | bytes 1769480 | tf_op jit(solution)/shard_map/ppermute | solution.py:1090
  390.9 19.6 %collective-permute-start.21 = (bf16[2,3,2,2,96,128]{5,4,1,3,2,0:T(8,128)(2,1)}, bf16[2,3,2,2,96,128]{5,4,1,3,2,0:T(8,128)(2,1)}, u32[]{:S(2)}, u32[]{:S(2)}) collective-permute-start(bf16[2,3,2,2,96,128]{5,4,1,3,2,0:T(8,128)(2,1)} %fusion.10), channel_id=1, source_target_pairs={{0,4},{4,0},{8,12},{12,8},{16,20},{20,16},{24,28},{28,24},{1,5},{5... | collective-permute-start | bytes 1769480 | tf_op jit(solution)/shard_map/ppermute | solution.py:1090
  393.4 23.7 %collective-permute-start.19 = (bf16[5,128,256]{2,1,0:T(8,128)(2,1)}, bf16[5,128,256]{2,1,0:T(8,128)(2,1)}, u32[]{:S(2)}, u32[]{:S(2)}) collective-permute-start(bf16[5,128,256]{2,1,0:T(8,128)(2,1)} %fusion.4), channel_id=1, source_target_pairs={{0,8},{4,12},{8,0},{12,4},{16,24},{20,28},{24,16},{28,20},{1,9},{5... | collective-permute-start | bytes 983048 | tf_op jit(solution)/shard_map/ppermute | solution.py:1090
  394.9 30.4 %collective-permute-start.22 = (bf16[2,128,512]{2,1,0:T(8,128)(2,1)}, bf16[2,128,512]{2,1,0:T(8,128)(2,1)}, u32[]{:S(2)}, u32[]{:S(2)}) collective-permute-start(bf16[2,128,512]{2,1,0:T(8,128)(2,1)} %fusion.23.refs_0_), channel_id=1, source_target_pairs={{0,2},{1,3},{2,0},{3,1},{4,6},{5,7},{6,4},{7,5},{8,10},{9,11},{10,... | collective-permute-start | bytes 786440 | tf_op jit(solution)/shard_map/ppermute | solution.py:1090
  394.9 28.7 %collective-permute-start.18 = (bf16[2,2,96,768]{3,2,0,1:T(8,128)(2,1)}, bf16[2,2,96,768]{3,2,0,1:T(8,128)(2,1)}, u32[]{:S(2)}, u32[]{:S(2)}) collective-permute-start(bf16[2,2,96,768]{3,2,0,1:T(8,128)(2,1)} %copy.82), channel_id=1, source_target_pairs={{0,16},{4,20},{8,24},{12,28},{16,0},{20,4},{24,8},{28,12},{1,17},{... | collective-permute-start | bytes 1769480 | tf_op jit(solution)/shard_map/ppermute | solution.py:1090
  425.8 17.7 %collective-permute-start.30 = (bf16[2,96,768]{2,1,0:T(8,128)(2,1)}, bf16[2,96,768]{2,1,0:T(8,128)(2,1)}, u32[]{:S(2)}, u32[]{:S(2)}) collective-permute-start(bf16[2,96,768]{2,1,0:T(8,128)(2,1)} %fusion.11), channel_id=1, source_target_pairs={{0,8},{4,12},{8,0},{12,4},{16,24},{20,28},{24,16},{28,20},{1,9},{5... | collective-permute-start | bytes 884744 | tf_op jit(solution)/shard_map/ppermute | solution.py:1090
  433.3 19.1 %collective-permute-start.26 = (bf16[8,32,384]{2,1,0:T(8,128)(2,1)}, bf16[8,32,384]{2,1,0:T(8,128)(2,1)}, u32[]{:S(2)}, u32[]{:S(2)}) collective-permute-start(bf16[8,32,384]{2,1,0:T(8,128)(2,1)} %add_convert_fusion.8), channel_id=1, source_target_pairs={{0,2},{1,3},{2,0},{3,1},{4,6},{5,7},{6,4},{7,5},{8,10},{9,11},{10,... | collective-permute-start | bytes 589832 | tf_op jit(solution)/shard_map/ppermute | solution.py:1090
  (56 other events, 499.5 us)
